TPU v7x, 32 devices: a whole 2x2x4 slice. The times are simulated.
32 devices in a mesh: dp: 2 (over y), mp: 16 (over z, x, core).
Axes of the slice: x: 2, y: 2, z: 4, core: 2. Of those that a mesh axis runs over, the one named last changes fastest.
Arguments:
- query: bfloat16 [512, 1024], P('dp', 'mp'), may hold values from -0.75 to 0.75
- kv_cache: bfloat16 [1024, 2048], P('dp', 'mp'), may hold values from -4 to 4, as said below
- out_grad: bfloat16 [512, 1024], P('dp', 'mp'), may hold values from -384 to 384
- source_lengths: int32 [2, 8], P('dp'), may hold values from 1 to 128, 512 in all within a row
- target_lengths: int32 [2, 8], P('dp'), may hold values from 1 to 64, 256 in all within a row
- low_rank: bfloat16 [1024, 32], P(('dp', 'mp')), may hold values from -0.125 to 0.125
- adapter_up_matrix: bfloat16 [32, 1024], replicated, may hold values from -0.1875 to 0.1875
Outputs:
- query_grad: bfloat16 [512, 1024], P('dp', 'mp')
- key_gradient: bfloat16 [1024, 1024], P(('dp', 'mp'))
- value_grad: bfloat16 [1024, 1024], P(('dp', 'mp'))
- low_rank_gradient: float32 [1024, 32], P(('dp', 'mp'))
- adapter_up_gradient: float32 [1024, 32], P(('dp', 'mp'))
Inputs may be any that keep to these rules, and one draw needn't show every extreme that they name: `source_lengths`: each row sums to 512; its largest entry is exactly 128. `target_lengths`: each row sums to 256; its largest entry is exactly 64. `kv_cache`: the key columns lie within -0.75 to 0.75.
All inputs are finite; a program needn't handle non-finite values.
Results may differ from a plain program's by a relative error of at most 0.0053.
Values may be sent and summed in bfloat16 or wider, within the bound.
No kernel may reach another device: no remote copies, remote signals or barrier semaphores. Data moves between devices by JAX's collectives and lax.ppermute only.
A program may use at most 64 MiB of HBM per device.

v0:
```python
import functools

import jax
import jax.numpy as jnp
from jax import lax
from jax.experimental import pallas as pl
from jax.experimental.pallas import tpu as pltpu
from jax.sharding import PartitionSpec as P

HS = 64
LANES = 128
CUT = 8

adapter_factor = 2.0

NT = (((1,), (1,)), ((), ()))
TN = (((0,), (0,)), ((), ()))


def dot(left, right, dims):
    return lax.dot_general(left, right, dims, preferred_element_type=jnp.float32)


def group_order(count):
    quarter = count // 4
    bits = quarter.bit_length() - 1
    assert count == 4 << bits
    turned = [sum(((i >> b) & 1) << (bits - 1 - b) for b in range(bits)) for i in range(quarter)]
    order = []
    for near, far in ((2, 3), (1, 0)):
        for i in range(quarter):
            order.append(near * quarter + turned[quarter - 1 - i])
            order.append(far * quarter + turned[(quarter - 1 - i) ^ 1])
    return order


def source_range(source_ref, target_ref, count):
    position = lax.broadcasted_iota(jnp.int32, (1, count), 1)
    first = jnp.zeros((1, count), jnp.int32)
    last = jnp.zeros((1, count), jnp.int32)
    target_start = jnp.int32(0)
    source_start = jnp.int32(0)
    for i in range(source_ref.shape[1]):
        source_end = source_start + source_ref[0, i]
        inside = position >= target_start
        first = jnp.where(inside, source_start, first)
        last = jnp.where(inside, source_end, last)
        target_start = target_start + target_ref[0, i]
        source_start = source_end
    return first, last


def attention_kernel(
    source_any, target_any, query_any, grad_any, kv_any, low_any, query_grad_ref, sent_ref, turned_ref,
    source_ref, target_ref, query_ref, grad_ref, kv_ref, low_ref, sems,
):
    pairs = [
        (kv_any, kv_ref), (query_any, query_ref), (grad_any, grad_ref),
        (source_any, source_ref), (target_any, target_ref), (low_any, low_ref),
    ]
    copies = [
        pltpu.make_async_copy(here, there, sems.at[i]) for i, (here, there) in enumerate(pairs)
    ]
    for copy in copies:
        copy.start()
    for copy in copies:
        copy.wait()
    tgt_count = query_ref.shape[1]
    both = kv_ref[...]
    query_t = query_ref[...]
    grad_t = grad_ref[...]
    blank = jnp.zeros_like(query_t)
    query_wide = jnp.concatenate([query_t, blank], axis=0)
    grad_wide = jnp.concatenate([blank, grad_t], axis=0)
    scores = jnp.dot(both, query_wide, preferred_element_type=jnp.float32)
    dprob = jnp.dot(both, grad_wide, preferred_element_type=jnp.float32)
    first, last = source_range(source_ref, target_ref, tgt_count)
    position = lax.broadcasted_iota(jnp.int32, scores.shape, 0)
    allowed = jnp.logical_and(position >= first, position < last)
    expo = jnp.where(allowed, jnp.exp(scores), 0.0)
    total = jnp.sum(expo, axis=0, keepdims=True)
    delta = jnp.sum(expo * dprob, axis=0, keepdims=True) / total
    prob = expo * (1.0 / total)
    prob_low = prob.astype(jnp.bfloat16)
    dscore = (prob * (dprob - delta)).astype(jnp.bfloat16)
    both_grad = dot(dscore, query_wide, NT) + dot(prob_low, grad_wide, NT)
    both_low = both_grad.astype(jnp.bfloat16)
    low = low_ref[...].astype(jnp.float32)
    rows = low.shape[0]
    blocks = sent_ref.shape[0]
    packed = jnp.concatenate([low[at:at + CUT] for at in range(0, rows, CUT)], axis=1)
    packed = packed.astype(jnp.bfloat16)
    for at, block in enumerate(group_order(blocks)):
        sent_ref[at, :rows, :] = both_low[block * rows:(block + 1) * rows]
        sent_ref[at, rows:, :] = packed

    wide = both_low.astype(jnp.float32)
    parts = []
    for start in range(0, rows, CUT):
        for block in range(blocks):
            parts.append(wide[block * rows + start:block * rows + start + CUT])
    turned_ref[...] = jnp.concatenate(parts, axis=0).T.astype(jnp.bfloat16)

    query_grad = dot(both, dscore, TN)
    query_grad_ref[...] = query_grad[:HS].astype(jnp.bfloat16)


def split_kernel(turned_ref, *out_refs):
    dp = len(out_refs)
    step = HS // dp
    turned = turned_ref[...].astype(jnp.float32)
    pieces = []
    for j in range(dp):
        rows = [turned[j * step:(j + 1) * step], turned[HS + j * step:HS + (j + 1) * step]]
        pieces.append(jnp.concatenate(rows, axis=0))
    e = lax.rem(lax.axis_index("mp"), dp)
    pack = lax.axis_index("dp")
    for s, out_ref in enumerate(out_refs):
        turn = lax.rem(2 * e + s + dp - pack, dp)
        chosen = pieces[0]
        for j in range(1, dp):
            chosen = jnp.where(turn == j, pieces[j], chosen)
        out_ref[...] = chosen.astype(jnp.bfloat16)


def order_kernel(*refs):
    *arrived_refs, out_ref = refs
    dp = len(arrived_refs)
    mine = lax.rem(lax.axis_index("mp"), dp)
    for s, arrived_ref in enumerate(arrived_refs):
        out_ref[lax.rem(mine + dp - s, dp)] = arrived_ref[...]


def share_kernel(rows, both_rank, got_ref, pieces_ref, *out_refs):
    dp, piece_rows, _ = pieces_ref.shape
    blocks = got_ref.shape[0]
    order = group_order(blocks)
    lows = [
        got_ref[order.index(block), rows:, :].astype(jnp.float32) for block in range(blocks)
    ]
    lows = jnp.concatenate(lows, axis=0).astype(jnp.bfloat16)
    columns = jnp.concatenate([pieces_ref[e] for e in range(dp)], axis=0)
    share = None
    for cut in range(rows // CUT):
        tokens = columns[:, cut * blocks * CUT:(cut + 1) * blocks * CUT]
        product = jnp.dot(tokens, lows, preferred_element_type=jnp.float32)
        part = product[:, cut * both_rank:(cut + 1) * both_rank]
        share = part if share is None else share + part
    step = piece_rows // 2
    column = lax.broadcasted_iota(jnp.int32, (step, both_rank), 1)
    shares = []
    for e in range(dp):
        keys = share[e * piece_rows:e * piece_rows + step]
        values = share[e * piece_rows + step:(e + 1) * piece_rows]
        shares.append(adapter_factor * jnp.where(column < both_rank // 2, keys, values))
    mine = lax.axis_index("dp")
    for s, out_ref in enumerate(out_refs):
        turn = lax.rem(mine + s, dp)
        chosen = shares[0]
        for e in range(1, dp):
            chosen = jnp.where(turn == e, shares[e], chosen)
        out_ref[...] = chosen


def owner_kernel(got_ref, up_ref, key_ref, value_ref, low_grad_ref):
    rows = key_ref.shape[0]
    rank = up_ref.shape[0] // 2
    order = group_order(got_ref.shape[0])
    for pair in range(len(order) // 2):
        first = got_ref[order.index(2 * pair), :rows, :]
        second = got_ref[order.index(2 * pair + 1), :rows, :]
        columns = slice(2 * pair * HS, (2 * pair + 2) * HS)
        key_ref[:, columns] = jnp.concatenate([first[:, :HS], second[:, :HS]], axis=1)
        value_ref[:, columns] = jnp.concatenate([first[:, HS:], second[:, HS:]], axis=1)
    up = up_ref[...]
    from_key = dot(key_ref[...], up, NT)
    from_value = dot(value_ref[...], up, NT)
    column = lax.broadcasted_iota(jnp.int32, from_key.shape, 1)
    low_grad_ref[...] = adapter_factor * jnp.where(column < rank, from_key, from_value)


def local(dp, mp, query, kv_cache, out_grad, source_lengths, target_lengths, low_rank, adapter_up_matrix):
    tgt_count = query.shape[0]
    src_count = kv_cache.shape[0]
    rows, both_rank = low_rank.shape
    width = adapter_up_matrix.shape[1]
    step = HS // dp
    assert rows // CUT * both_rank == LANES
    vmem = pl.BlockSpec(memory_space=pltpu.VMEM)
    hbm = pl.BlockSpec(memory_space=pl.ANY)
    params = pltpu.CompilerParams(vmem_limit_bytes=48 * 1024 * 1024)
    whole_vmem = pltpu.CompilerParams(vmem_limit_bytes=60 * 1024 * 1024)

    query_t = query.T
    grad_t = out_grad.T
    query_grad_t, sent, turned = pl.pallas_call(
        attention_kernel,
        out_shape=[
            jax.ShapeDtypeStruct((HS, tgt_count), jnp.bfloat16),
            jax.ShapeDtypeStruct((mp, rows + CUT, LANES), jnp.bfloat16),
            jax.ShapeDtypeStruct((2 * HS, src_count), jnp.bfloat16),
        ],
        in_specs=[hbm] * 6,
        out_specs=[vmem] * 3,
        scratch_shapes=[
            pltpu.SMEM(source_lengths.shape, jnp.int32),
            pltpu.SMEM(target_lengths.shape, jnp.int32),
            pltpu.VMEM(query_t.shape, jnp.bfloat16),
            pltpu.VMEM(grad_t.shape, jnp.bfloat16),
            pltpu.VMEM(kv_cache.shape, jnp.bfloat16),
            pltpu.VMEM(low_rank.shape, jnp.bfloat16),
            pltpu.SemaphoreType.DMA((6,)),
        ],
        compiler_params=whole_vmem,
        name="attention_backward",
    )(source_lengths, target_lengths, query_t, grad_t, kv_cache, low_rank)

    route = [(h, h * dp % mp + h * dp // mp) for h in range(mp)]
    pieces = pl.pallas_call(
        split_kernel,
        out_shape=[jax.ShapeDtypeStruct((2 * step, src_count), jnp.bfloat16)] * dp,
        in_specs=[vmem],
        out_specs=[vmem] * dp,
        compiler_params=params,
        cost_estimate=pl.CostEstimate(flops=2 ** 36, bytes_accessed=2 ** 28, transcendentals=0),
        name="split_columns",
    )(lax.ppermute(turned, "mp", route))
    arrived = [pieces[0]]
    for s in range(1, dp):
        route = [(m, m - m % dp + (m + s) % dp) for m in range(mp)]
        arrived.append(lax.ppermute(pieces[s], "mp", route))
    ordered = pl.pallas_call(
        order_kernel,
        out_shape=jax.ShapeDtypeStruct((dp, 2 * step, src_count), jnp.bfloat16),
        in_specs=[vmem] * dp,
        out_specs=vmem,
        compiler_params=params,
        name="order_pieces",
    )(*arrived)

    got = lax.all_to_all(sent, "mp", 0, 0, axis_index_groups=[group_order(mp)], tiled=True)

    shares = pl.pallas_call(
        functools.partial(share_kernel, rows, both_rank),
        out_shape=[jax.ShapeDtypeStruct((step, both_rank), jnp.float32)] * dp,
        in_specs=[vmem] * 2,
        out_specs=[vmem] * dp,
        compiler_params=params,
        name="adapter_shares",
    )(got, ordered)
    up_grad = shares[0]
    for s in range(1, dp):
        route = [
            (d * mp + m, (d + s) % dp * mp + m - m % dp + (m + s) % dp)
            for d in range(dp) for m in range(mp)
        ]
        up_grad = up_grad + lax.ppermute(shares[s], ("dp", "mp"), route)

    key_gradient, value_grad, low_grad = pl.pallas_call(
        owner_kernel,
        out_shape=[
            jax.ShapeDtypeStruct((rows, width), jnp.bfloat16),
            jax.ShapeDtypeStruct((rows, width), jnp.bfloat16),
            jax.ShapeDtypeStruct((rows, both_rank), jnp.float32),
        ],
        in_specs=[vmem] * 2,
        out_specs=[vmem] * 3,
        compiler_params=params,
        name="owner_outputs",
    )(got, adapter_up_matrix)
    return query_grad_t.T, key_gradient, value_grad, low_grad, up_grad


def solution(mesh):
    in_specs = (
        P("dp", "mp"),
        P("dp", "mp"),
        P("dp", "mp"),
        P("dp", None),
        P("dp", None),
        P(("dp", "mp"), None),
        P(),
    )
    out_specs = (
        P("dp", "mp"),
        P(("dp", "mp"), None),
        P(("dp", "mp"), None),
        P(("dp", "mp"), None),
        P(("dp", "mp"), None),
    )
    body = functools.partial(local, mesh.shape["dp"], mesh.shape["mp"])
    return jax.shard_map(body, mesh=mesh, in_specs=in_specs, out_specs=out_specs, check_vma=False)
```

profile of v0, /device:TPU:0, one launch (start us, length us, event | category | flops | bytes accessed | tf_op | source)
XLA Modules:
  0.0 23.2 jit_solution(12775119000399556983)
XLA Ops:
  0.6 2.5 %attention_backward.1 = (bf16[64,256]{1,0:T(8,128)(2,1)}, bf16[16,40,128]{2,1,0:T(8,128)(2,1)}, bf16[128,512]{1,0:T(8,128)(2,1)}) custom-call(s32[1,8]{1,0:T(1,128)} %source_any.1, s32[1,8]{1,0:T(1,128)} %target_any.1, bf16[64,256]{1,0:T(8,128)(2,1)} %bitcast.3, bf16[64,256]{1,0:T(8,128)(2,1)} %bitcast.4, bf16[512,128]{1,0:T(8,128)(2,1)} %kv_any.1, ...), custom_call_target="tpu_custom_call" | custom-call | tf_op jit(solution)/shard_map/attention_backward/pallas_call | solution.py:196
  3.1 1.6 %collective-permute-start = (bf16[128,512]{1,0:T(8,128)(2,1)}, bf16[128,512]{1,0:T(8,128)(2,1)S(1)}, u32[]{:S(2)}, u32[]{:S(2)}) collective-permute-start(bf16[128,512]{1,0:T(8,128)(2,1)} %get-tuple-element.20), channel_id=1, source_target_pairs={{0,0},{1,2},{2,4},{3,6},{4,8},{5,10},{6,12},{7,14},{8,1},{9,3},{10... | collective-permute-start | bytes 393224 | tf_op jit(solution)/shard_map/ppermute | solution.py:227
  4.7 9.4 %all-to-all-start = ((bf16[16,40,128]{2,1,0:T(8,128)(2,1)}), bf16[16,40,128]{2,1,0:T(8,128)(2,1)S(1)}, u32[]{:S(2)}, u32[]{:S(2)}) async-start(bf16[16,40,128]{2,1,0:T(8,128)(2,1)} %get-tuple-element.16), calls=%async_computation | async-start | bytes 327680 | tf_op jit(solution)/shard_map/all_to_all | solution.py:241
  14.1 0.0 collective-permute-done.turned_ref
  14.1 0.1 collective-permute-start.1
  14.3 1.2 %collective-permute-done.1.refs_1_ = bf16[64,512]{1,0:T(8,128)(2,1)S(1)} collective-permute-done((bf16[64,512]{1,0:T(8,128)(2,1)S(1)}, bf16[64,512]{1,0:T(8,128)(2,1)S(1)}, u32[]{:S(2)}, u32[]{:S(2)}) %collective-permute-start.1) | collective-permute-done | bytes 65568 | tf_op jit(solution)/shard_map/ppermute | solution.py:231
  15.5 0.0 copy-start
  15.5 3.6 %all-to-all-done.got_ref = bf16[16,40,128]{2,1,0:T(8,128)(2,1)S(1)} async-done(((bf16[16,40,128]{2,1,0:T(8,128)(2,1)}), bf16[16,40,128]{2,1,0:T(8,128)(2,1)S(1)}, u32[]{:S(2)}, u32[]{:S(2)}) %all-to-all-start) | async-done | bytes 163872 | tf_op jit(solution)/shard_map/all_to_all | solution.py:241
  19.1 0.3 %adapter_shares.1 = (f32[32,32]{1,0:T(8,128)S(1)}, f32[32,32]{1,0:T(8,128)S(1)}) custom-call(bf16[16,40,128]{2,1,0:T(8,128)(2,1)S(1)} %all-to-all-done.got_ref, bf16[2,64,512]{2,1,0:T(8,128)(2,1)S(1)} %order_pieces.1.pieces_ref), custom_call_target="tpu_custom_call" | custom-call | tf_op jit(solution)/shard_map/adapter_shares/pallas_call | solution.py:243
  19.3 1.2 %collective-permute-start.2 = (f32[32,32]{1,0:T(8,128)S(1)}, f32[32,32]{1,0:T(8,128)S(1)}, u32[]{:S(2)}, u32[]{:S(2)}) collective-permute-start(f32[32,32]{1,0:T(8,128)S(1)} %get-tuple-element.24), channel_id=1, source_target_pairs={{0,17},{1,16},{2,19},{3,18},{4,21},{5,20},{6,23},{7,22},{8,25},{9,... | collective-permute-start | bytes 12296 | tf_op jit(solution)/shard_map/ppermute | solution.py:257
  20.6 0.0 copy-done
  20.6 0.9 %owner_outputs.1 = (bf16[32,1024]{1,0:T(8,128)(2,1)}, bf16[32,1024]{1,0:T(8,128)(2,1)}, f32[32,32]{1,0:T(8,128)}) custom-call(bf16[16,40,128]{2,1,0:T(8,128)(2,1)S(1)} %all-to-all-done.got_ref, bf16[32,1024]{1,0:T(8,128)(2,1)S(1)} %copy-done), custom_call_target="tpu_custom_call" | custom-call | tf_op jit(solution)/shard_map/owner_outputs/pallas_call | solution.py:259
  21.4 1.1 %collective-permute-done.2 = f32[32,32]{1,0:T(8,128)S(1)} collective-permute-done((f32[32,32]{1,0:T(8,128)S(1)}, f32[32,32]{1,0:T(8,128)S(1)}, u32[]{:S(2)}, u32[]{:S(2)}) %collective-permute-start.2) | collective-permute-done | bytes 4128 | tf_op jit(solution)/shard_map/ppermute | solution.py:257
  22.5 0.6 %add.3 = f32[32,32]{1,0:T(8,128)} add(f32[32,32]{1,0:T(8,128)S(1)} %get-tuple-element.23, f32[32,32]{1,0:T(8,128)S(1)} %collective-permute-done.2) | non-fusion elementwise | flops 1024 | bytes 12288 | tf_op jit(solution)/shard_map/add | solution.py:257
  (2 shorter events, 0.1 us)
Async XLA Ops:
  3.1 11.0 %collective-permute-start = (bf16[128,512]{1,0:T(8,128)(2,1)}, bf16[128,512]{1,0:T(8,128)(2,1)S(1)}, u32[]{:S(2)}, u32[]{:S(2)}) collective-permute-start(bf16[128,512]{1,0:T(8,128)(2,1)} %get-tuple-element.20), channel_id=1, source_target_pairs={{0,0},{1,2},{2,4},{3,6},{4,8},{5,10},{6,12},{7,14},{8,1},{9,3},{10... | collective-permute-start | bytes 393224 | tf_op jit(solution)/shard_map/ppermute | solution.py:227
  4.7 14.4 %all-to-all-start = ((bf16[16,40,128]{2,1,0:T(8,128)(2,1)}), bf16[16,40,128]{2,1,0:T(8,128)(2,1)S(1)}, u32[]{:S(2)}, u32[]{:S(2)}) async-start(bf16[16,40,128]{2,1,0:T(8,128)(2,1)} %get-tuple-element.16), calls=%async_computation | async-start | bytes 327680 | tf_op jit(solution)/shard_map/all_to_all | solution.py:241
  14.1 1.3 %collective-permute-start.1 = (bf16[64,512]{1,0:T(8,128)(2,1)S(1)}, bf16[64,512]{1,0:T(8,128)(2,1)S(1)}, u32[]{:S(2)}, u32[]{:S(2)}) collective-permute-start(bf16[64,512]{1,0:T(8,128)(2,1)S(1)} %get-tuple-element.22), channel_id=1, source_target_pairs={{0,1},{1,0},{2,3},{3,2},{4,5},{5,4},{6,7},{7,6},{8,9},{9,8},{10,11... | collective-permute-start | bytes 196616 | tf_op jit(solution)/shard_map/ppermute | solution.py:231
  15.5 5.1 %copy-start = (bf16[32,1024]{1,0:T(8,128)(2,1)S(1)}, bf16[32,1024]{1,0:T(8,128)(2,1)}, u32[]{:S(2)}) copy-start(bf16[32,1024]{1,0:T(8,128)(2,1)} %up_ref.1) | copy-start | bytes 196612
  19.3 3.2 %collective-permute-start.2 = (f32[32,32]{1,0:T(8,128)S(1)}, f32[32,32]{1,0:T(8,128)S(1)}, u32[]{:S(2)}, u32[]{:S(2)}) collective-permute-start(f32[32,32]{1,0:T(8,128)S(1)} %get-tuple-element.24), channel_id=1, source_target_pairs={{0,17},{1,16},{2,19},{3,18},{4,21},{5,20},{6,23},{7,22},{8,25},{9,... | collective-permute-start | bytes 12296 | tf_op jit(solution)/shard_map/ppermute | solution.py:257
where the time goes:
time: 23.4 us; the launch traced here: 23.2 us
  starting transfers between devices  12.3 us (53%)
  waiting for transfers between devices  5.87 us (25%)
  Pallas kernels  3.65 us (16%)
  between operations  0.68 us (3%)
  other arithmetic  0.61 us (3%)
    all_to_all x1, starting transfers between devices, local(): lax.all_to_all(sent, 'mp', 0, 0, axis_index_groups=[group_order(mp)], til...  9.39 us
    all_to_all x1, waiting for transfers between devices, local(): lax.all_to_all(sent, 'mp', 0, 0, axis_index_groups=[group_order(mp)], til...  3.58 us
    pallas_call x1, Pallas kernels, local(): pl.pallas_call(attention_kernel, out_shape=[jax.ShapeDtypeStruct((HS, tgt...  2.48 us
    ppermute x1, starting transfers between devices, local(): lax.ppermute(turned, 'mp', route)  1.56 us
    ppermute x1, starting transfers between devices, local(): up_grad = up_grad + lax.ppermute(shares[s], ('dp', 'mp'), route)  1.25 us
    ppermute x1, waiting for transfers between devices, local(): arrived.append(lax.ppermute(pieces[s], 'mp', route))  1.17 us
    ppermute x1, waiting for transfers between devices, local(): up_grad = up_grad + lax.ppermute(shares[s], ('dp', 'mp'), route)  1.12 us
    pallas_call x1, Pallas kernels, local(): pl.pallas_call(owner_kernel, out_shape=[jax.ShapeDtypeStruct((rows, width...  0.86 us
  transfers between devices with their start and end apart: 4, of which 3 were waited for; matrix products, arithmetic and copies ran while one was open for 0% of the time, Pallas kernels for 4%

commit v1 on v0

--- a/solution.py
+++ b/solution.py
@@ -51,58 +51,90 @@
 
 
 def attention_kernel(
-    source_any, target_any, query_any, grad_any, kv_any, low_any, query_grad_ref, sent_ref, turned_ref,
-    source_ref, target_ref, query_ref, grad_ref, kv_ref, low_ref, sems,
+    source_any, target_any, query_any, grad_any, kv_any, low_any,
+    query_grad_any, sent_any, turned_any,
+    source_ref, target_ref, query_ref, grad_ref, kv_ref, low_ref,
+    expo_ref, dprob_ref, query_grad_ref, sent_ref, turned_ref, in_sems, out_sems,
 ):
+    tgt_count = query_ref.shape[1]
+    src_count = kv_ref.shape[0]
+    rows = low_ref.shape[0]
+    blocks = src_count // rows
+    per_chunk = LANES // rows
+    chunks = src_count // LANES
+    order = group_order(blocks)
     pairs = [
-        (kv_any, kv_ref), (query_any, query_ref), (grad_any, grad_ref),
+        (query_any, query_ref), (grad_any, grad_ref),
         (source_any, source_ref), (target_any, target_ref), (low_any, low_ref),
     ]
+    for chunk in range(chunks):
+        part = pl.ds(chunk * LANES, LANES)
+        pairs.append((kv_any.at[part, :], kv_ref.at[part, :]))
     copies = [
-        pltpu.make_async_copy(here, there, sems.at[i]) for i, (here, there) in enumerate(pairs)
+        pltpu.make_async_copy(here, there, in_sems.at[i]) for i, (here, there) in enumerate(pairs)
     ]
     for copy in copies:
         copy.start()
-    for copy in copies:
+    for copy in copies[:5]:
         copy.wait()
-    tgt_count = query_ref.shape[1]
-    both = kv_ref[...]
+
+    first, last = source_range(source_ref, target_ref, tgt_count)
     query_t = query_ref[...]
     grad_t = grad_ref[...]
     blank = jnp.zeros_like(query_t)
     query_wide = jnp.concatenate([query_t, blank], axis=0)
     grad_wide = jnp.concatenate([blank, grad_t], axis=0)
-    scores = jnp.dot(both, query_wide, preferred_element_type=jnp.float32)
-    dprob = jnp.dot(both, grad_wide, preferred_element_type=jnp.float32)
-    first, last = source_range(source_ref, target_ref, tgt_count)
-    position = lax.broadcasted_iota(jnp.int32, scores.shape, 0)
-    allowed = jnp.logical_and(position >= first, position < last)
-    expo = jnp.where(allowed, jnp.exp(scores), 0.0)
-    total = jnp.sum(expo, axis=0, keepdims=True)
-    delta = jnp.sum(expo * dprob, axis=0, keepdims=True) / total
-    prob = expo * (1.0 / total)
-    prob_low = prob.astype(jnp.bfloat16)
-    dscore = (prob * (dprob - delta)).astype(jnp.bfloat16)
-    both_grad = dot(dscore, query_wide, NT) + dot(prob_low, grad_wide, NT)
-    both_low = both_grad.astype(jnp.bfloat16)
+    wide = jnp.concatenate([query_wide, grad_wide], axis=1)
+    total = jnp.zeros((1, tgt_count), jnp.float32)
+    weighted = jnp.zeros((1, tgt_count), jnp.float32)
+    for chunk in range(chunks):
+        copies[5 + chunk].wait()
+        part = slice(chunk * LANES, (chunk + 1) * LANES)
+        product = jnp.dot(kv_ref[part, :], wide, preferred_element_type=jnp.float32)
+        dprob = product[:, tgt_count:]
+        position = chunk * LANES + lax.broadcasted_iota(jnp.int32, (LANES, tgt_count), 0)
+        allowed = jnp.logical_and(position >= first, position < last)
+        expo = jnp.where(allowed, jnp.exp(product[:, :tgt_count]), 0.0)
+        total += jnp.sum(expo, axis=0, keepdims=True)
+        weighted += jnp.sum(expo * dprob, axis=0, keepdims=True)
+        expo_ref[part, :] = expo
+        dprob_ref[part, :] = dprob
+    inverse = 1.0 / total
+    delta = weighted * inverse
+
     low = low_ref[...].astype(jnp.float32)
-    rows = low.shape[0]
-    blocks = sent_ref.shape[0]
     packed = jnp.concatenate([low[at:at + CUT] for at in range(0, rows, CUT)], axis=1)
     packed = packed.astype(jnp.bfloat16)
-    for at, block in enumerate(group_order(blocks)):
-        sent_ref[at, :rows, :] = both_low[block * rows:(block + 1) * rows]
-        sent_ref[at, rows:, :] = packed
-
-    wide = both_low.astype(jnp.float32)
-    parts = []
-    for start in range(0, rows, CUT):
-        for block in range(blocks):
-            parts.append(wide[block * rows + start:block * rows + start + CUT])
-    turned_ref[...] = jnp.concatenate(parts, axis=0).T.astype(jnp.bfloat16)
-
-    query_grad = dot(both, dscore, TN)
-    query_grad_ref[...] = query_grad[:HS].astype(jnp.bfloat16)
+    query_grad = jnp.zeros((2 * HS, tgt_count), jnp.float32)
+    sends = []
+    for chunk in range(chunks):
+        part = slice(chunk * LANES, (chunk + 1) * LANES)
+        prob = expo_ref[part, :] * inverse
+        dscore = (prob * (dprob_ref[part, :] - delta)).astype(jnp.bfloat16)
+        both = jnp.concatenate([dscore, prob.astype(jnp.bfloat16)], axis=1)
+        both_grad = dot(both, wide, NT)
+        both_low = both_grad.astype(jnp.bfloat16)
+        for at in range(per_chunk):
+            place = order.index(chunk * per_chunk + at)
+            sent_ref[place, :rows, :] = both_low[at * rows:(at + 1) * rows]
+            sent_ref[place, rows:, :] = packed
+            sends.append((sent_ref.at[place], sent_any.at[place]))
+        exact = both_low.astype(jnp.float32)
+        parts = [
+            exact[at * rows + start:at * rows + start + CUT]
+            for start in range(0, rows, CUT) for at in range(per_chunk)
+        ]
+        turned_ref[:, part] = jnp.concatenate(parts, axis=0).T.astype(jnp.bfloat16)
+        sends.append((turned_ref.at[:, part], turned_any.at[:, part]))
+        query_grad += dot(kv_ref[part, :], dscore, TN)
+        if chunk == chunks - 1:
+            query_grad_ref[...] = query_grad[:HS].astype(jnp.bfloat16)
+            sends.append((query_grad_ref, query_grad_any))
+        begun = chunk * (per_chunk + 1)
+        for i in range(begun, len(sends)):
+            pltpu.make_async_copy(*sends[i], out_sems.at[i]).start()
+    for i, pair in enumerate(sends):
+        pltpu.make_async_copy(*pair, out_sems.at[i]).wait()
 
 
 def split_kernel(turned_ref, *out_refs):
@@ -138,14 +170,15 @@
     lows = [
         got_ref[order.index(block), rows:, :].astype(jnp.float32) for block in range(blocks)
     ]
-    lows = jnp.concatenate(lows, axis=0).astype(jnp.bfloat16)
+    parts = []
+    per_chunk = LANES // rows
+    for at in range(0, blocks, per_chunk):
+        low = jnp.concatenate(lows[at:at + per_chunk], axis=0)
+        for cut in range(rows // CUT):
+            parts.append(low[:, cut * both_rank:(cut + 1) * both_rank])
+    lows = jnp.concatenate(parts, axis=0).astype(jnp.bfloat16)
     columns = jnp.concatenate([pieces_ref[e] for e in range(dp)], axis=0)
-    share = None
-    for cut in range(rows // CUT):
-        tokens = columns[:, cut * blocks * CUT:(cut + 1) * blocks * CUT]
-        product = jnp.dot(tokens, lows, preferred_element_type=jnp.float32)
-        part = product[:, cut * both_rank:(cut + 1) * both_rank]
-        share = part if share is None else share + part
+    share = jnp.dot(columns, lows, preferred_element_type=jnp.float32)
     step = piece_rows // 2
     column = lax.broadcasted_iota(jnp.int32, (step, both_rank), 1)
     shares = []
@@ -185,7 +218,7 @@
     rows, both_rank = low_rank.shape
     width = adapter_up_matrix.shape[1]
     step = HS // dp
-    assert rows // CUT * both_rank == LANES
+    assert rows // CUT * both_rank == LANES and mp * rows == src_count
     vmem = pl.BlockSpec(memory_space=pltpu.VMEM)
     hbm = pl.BlockSpec(memory_space=pl.ANY)
     params = pltpu.CompilerParams(vmem_limit_bytes=48 * 1024 * 1024)
@@ -201,7 +234,7 @@
             jax.ShapeDtypeStruct((2 * HS, src_count), jnp.bfloat16),
         ],
         in_specs=[hbm] * 6,
-        out_specs=[vmem] * 3,
+        out_specs=[hbm] * 3,
         scratch_shapes=[
             pltpu.SMEM(source_lengths.shape, jnp.int32),
             pltpu.SMEM(target_lengths.shape, jnp.int32),
@@ -209,7 +242,13 @@
             pltpu.VMEM(grad_t.shape, jnp.bfloat16),
             pltpu.VMEM(kv_cache.shape, jnp.bfloat16),
             pltpu.VMEM(low_rank.shape, jnp.bfloat16),
-            pltpu.SemaphoreType.DMA((6,)),
+            pltpu.VMEM((src_count, tgt_count), jnp.float32),
+            pltpu.VMEM((src_count, tgt_count), jnp.float32),
+            pltpu.VMEM(query_t.shape, jnp.bfloat16),
+            pltpu.VMEM((mp, rows + CUT, LANES), jnp.bfloat16),
+            pltpu.VMEM((2 * HS, src_count), jnp.bfloat16),
+            pltpu.SemaphoreType.DMA((5 + src_count // LANES,)),
+            pltpu.SemaphoreType.DMA((mp + src_count // LANES + 1,)),
         ],
         compiler_params=whole_vmem,
         name="attention_backward",

time: 23.4 us -> 23.9 us (1.021)
  Pallas kernels: 3.65 us -> 4.11 us
    pallas_call x1, Pallas kernels: 2.48 us -> 2.94 us  [local(): pl.pallas_call(attention_kernel, out_shape=[jax.ShapeDtypeStruct((HS, tgt...]
where the time goes in v1:
time: 23.9 us; the launch traced here: 23.6 us
  starting transfers between devices  12.3 us (51%)
  waiting for transfers between devices  5.87 us (25%)
  Pallas kernels  4.11 us (17%)
  between operations  0.68 us (3%)
  other arithmetic  0.61 us (3%)
    all_to_all x1, starting transfers between devices, local(): lax.all_to_all(sent, 'mp', 0, 0, axis_index_groups=[group_order(mp)], til...  9.38 us
    all_to_all x1, waiting for transfers between devices, local(): lax.all_to_all(sent, 'mp', 0, 0, axis_index_groups=[group_order(mp)], til...  3.58 us
    pallas_call x1, Pallas kernels, local(): pl.pallas_call(attention_kernel, out_shape=[jax.ShapeDtypeStruct((HS, tgt...  2.94 us
    ppermute x1, starting transfers between devices, local(): lax.ppermute(turned, 'mp', route)  1.56 us
    ppermute x1, starting transfers between devices, local(): up_grad = up_grad + lax.ppermute(shares[s], ('dp', 'mp'), route)  1.25 us
    ppermute x1, waiting for transfers between devices, local(): arrived.append(lax.ppermute(pieces[s], 'mp', route))  1.17 us
    ppermute x1, waiting for transfers between devices, local(): up_grad = up_grad + lax.ppermute(shares[s], ('dp', 'mp'), route)  1.12 us
    pallas_call x1, Pallas kernels, local(): pl.pallas_call(owner_kernel, out_shape=[jax.ShapeDtypeStruct((rows, width...  0.86 us
  transfers between devices with their start and end apart: 4, of which 3 were waited for; matrix products, arithmetic and copies ran while one was open for 0% of the time, Pallas kernels for 4%

profile of v1, /device:TPU:0, one launch (start us, length us, event | category | flops | bytes accessed | tf_op | source)
XLA Modules:
  0.0 23.6 jit_solution(1648075859716245072)
XLA Ops:
  0.6 2.9 %attention_backward.1 = (bf16[64,256]{1,0:T(8,128)(2,1)}, bf16[16,40,128]{2,1,0:T(8,128)(2,1)}, bf16[128,512]{1,0:T(8,128)(2,1)}) custom-call(s32[1,8]{1,0:T(1,128)} %source_any.1, s32[1,8]{1,0:T(1,128)} %target_any.1, bf16[64,256]{1,0:T(8,128)(2,1)} %bitcast.3, bf16[64,256]{1,0:T(8,128)(2,1)} %bitcast.4, bf16[512,128]{1,0:T(8,128)(2,1)} %kv_any.1, ...), custom_call_target="tpu_custom_call" | custom-call | tf_op jit(solution)/shard_map/attention_backward/pallas_call | solution.py:229
  3.6 1.6 %collective-permute-start = (bf16[128,512]{1,0:T(8,128)(2,1)}, bf16[128,512]{1,0:T(8,128)(2,1)S(1)}, u32[]{:S(2)}, u32[]{:S(2)}) collective-permute-start(bf16[128,512]{1,0:T(8,128)(2,1)} %get-tuple-element.20), channel_id=1, source_target_pairs={{0,0},{1,2},{2,4},{3,6},{4,8},{5,10},{6,12},{7,14},{8,1},{9,3},{10... | collective-permute-start | bytes 393224 | tf_op jit(solution)/shard_map/ppermute | solution.py:266
  5.1 9.4 %all-to-all-start = ((bf16[16,40,128]{2,1,0:T(8,128)(2,1)}), bf16[16,40,128]{2,1,0:T(8,128)(2,1)S(1)}, u32[]{:S(2)}, u32[]{:S(2)}) async-start(bf16[16,40,128]{2,1,0:T(8,128)(2,1)} %get-tuple-element.16), calls=%async_computation | async-start | bytes 327680 | tf_op jit(solution)/shard_map/all_to_all | solution.py:280
  14.5 0.0 collective-permute-done.turned_ref
  14.6 0.1 collective-permute-start.1
  14.7 1.2 %collective-permute-done.1.refs_1_ = bf16[64,512]{1,0:T(8,128)(2,1)S(1)} collective-permute-done((bf16[64,512]{1,0:T(8,128)(2,1)S(1)}, bf16[64,512]{1,0:T(8,128)(2,1)S(1)}, u32[]{:S(2)}, u32[]{:S(2)}) %collective-permute-start.1) | collective-permute-done | bytes 65568 | tf_op jit(solution)/shard_map/ppermute | solution.py:270
  15.9 0.0 copy-start
  15.9 3.6 %all-to-all-done.got_ref = bf16[16,40,128]{2,1,0:T(8,128)(2,1)S(1)} async-done(((bf16[16,40,128]{2,1,0:T(8,128)(2,1)}), bf16[16,40,128]{2,1,0:T(8,128)(2,1)S(1)}, u32[]{:S(2)}, u32[]{:S(2)}) %all-to-all-start) | async-done | bytes 163872 | tf_op jit(solution)/shard_map/all_to_all | solution.py:280
  19.5 0.3 %adapter_shares.1 = (f32[32,32]{1,0:T(8,128)S(1)}, f32[32,32]{1,0:T(8,128)S(1)}) custom-call(bf16[16,40,128]{2,1,0:T(8,128)(2,1)S(1)} %all-to-all-done.got_ref, bf16[2,64,512]{2,1,0:T(8,128)(2,1)S(1)} %order_pieces.1.pieces_ref), custom_call_target="tpu_custom_call" | custom-call | tf_op jit(solution)/shard_map/adapter_shares/pallas_call | solution.py:282
  19.8 1.3 %collective-permute-start.2 = (f32[32,32]{1,0:T(8,128)S(1)}, f32[32,32]{1,0:T(8,128)S(1)}, u32[]{:S(2)}, u32[]{:S(2)}) collective-permute-start(f32[32,32]{1,0:T(8,128)S(1)} %get-tuple-element.24), channel_id=1, source_target_pairs={{0,17},{1,16},{2,19},{3,18},{4,21},{5,20},{6,23},{7,22},{8,25},{9,... | collective-permute-start | bytes 12296 | tf_op jit(solution)/shard_map/ppermute | solution.py:296
  21.0 0.0 copy-done
  21.0 0.9 %owner_outputs.1 = (bf16[32,1024]{1,0:T(8,128)(2,1)}, bf16[32,1024]{1,0:T(8,128)(2,1)}, f32[32,32]{1,0:T(8,128)}) custom-call(bf16[16,40,128]{2,1,0:T(8,128)(2,1)S(1)} %all-to-all-done.got_ref, bf16[32,1024]{1,0:T(8,128)(2,1)S(1)} %copy-done), custom_call_target="tpu_custom_call" | custom-call | tf_op jit(solution)/shard_map/owner_outputs/pallas_call | solution.py:298
  21.9 1.1 %collective-permute-done.2 = f32[32,32]{1,0:T(8,128)S(1)} collective-permute-done((f32[32,32]{1,0:T(8,128)S(1)}, f32[32,32]{1,0:T(8,128)S(1)}, u32[]{:S(2)}, u32[]{:S(2)}) %collective-permute-start.2) | collective-permute-done | bytes 4128 | tf_op jit(solution)/shard_map/ppermute | solution.py:296
  23.0 0.6 %add.3 = f32[32,32]{1,0:T(8,128)} add(f32[32,32]{1,0:T(8,128)S(1)} %get-tuple-element.23, f32[32,32]{1,0:T(8,128)S(1)} %collective-permute-done.2) | non-fusion elementwise | flops 1024 | bytes 12288 | tf_op jit(solution)/shard_map/add | solution.py:296
  (2 shorter events, 0.1 us)
Async XLA Ops:
  3.6 10.9 %collective-permute-start = (bf16[128,512]{1,0:T(8,128)(2,1)}, bf16[128,512]{1,0:T(8,128)(2,1)S(1)}, u32[]{:S(2)}, u32[]{:S(2)}) collective-permute-start(bf16[128,512]{1,0:T(8,128)(2,1)} %get-tuple-element.20), channel_id=1, source_target_pairs={{0,0},{1,2},{2,4},{3,6},{4,8},{5,10},{6,12},{7,14},{8,1},{9,3},{10... | collective-permute-start | bytes 393224 | tf_op jit(solution)/shard_map/ppermute | solution.py:266
  5.1 14.4 %all-to-all-start = ((bf16[16,40,128]{2,1,0:T(8,128)(2,1)}), bf16[16,40,128]{2,1,0:T(8,128)(2,1)S(1)}, u32[]{:S(2)}, u32[]{:S(2)}) async-start(bf16[16,40,128]{2,1,0:T(8,128)(2,1)} %get-tuple-element.16), calls=%async_computation | async-start | bytes 327680 | tf_op jit(solution)/shard_map/all_to_all | solution.py:280
  14.6 1.3 %collective-permute-start.1 = (bf16[64,512]{1,0:T(8,128)(2,1)S(1)}, bf16[64,512]{1,0:T(8,128)(2,1)S(1)}, u32[]{:S(2)}, u32[]{:S(2)}) collective-permute-start(bf16[64,512]{1,0:T(8,128)(2,1)S(1)} %get-tuple-element.22), channel_id=1, source_target_pairs={{0,1},{1,0},{2,3},{3,2},{4,5},{5,4},{6,7},{7,6},{8,9},{9,8},{10,11... | collective-permute-start | bytes 196616 | tf_op jit(solution)/shard_map/ppermute | solution.py:270
  15.9 5.1 %copy-start = (bf16[32,1024]{1,0:T(8,128)(2,1)S(1)}, bf16[32,1024]{1,0:T(8,128)(2,1)}, u32[]{:S(2)}) copy-start(bf16[32,1024]{1,0:T(8,128)(2,1)} %up_ref.1) | copy-start | bytes 196612
  19.8 3.2 %collective-permute-start.2 = (f32[32,32]{1,0:T(8,128)S(1)}, f32[32,32]{1,0:T(8,128)S(1)}, u32[]{:S(2)}, u32[]{:S(2)}) collective-permute-start(f32[32,32]{1,0:T(8,128)S(1)} %get-tuple-element.24), channel_id=1, source_target_pairs={{0,17},{1,16},{2,19},{3,18},{4,21},{5,20},{6,23},{7,22},{8,25},{9,... | collective-permute-start | bytes 12296 | tf_op jit(solution)/shard_map/ppermute | solution.py:296

commit v2 on v0

--- a/solution.py
+++ b/solution.py
@@ -51,8 +51,10 @@
 
 
 def attention_kernel(
-    source_any, target_any, query_any, grad_any, kv_any, low_any, query_grad_ref, sent_ref, turned_ref,
-    source_ref, target_ref, query_ref, grad_ref, kv_ref, low_ref, sems,
+    source_any, target_any, query_any, grad_any, kv_any, low_any,
+    query_grad_any, sent_any, turned_any,
+    source_ref, target_ref, query_ref, grad_ref, kv_ref, low_ref,
+    query_grad_ref, sent_ref, turned_ref, sems, out_sems,
 ):
     pairs = [
         (kv_any, kv_ref), (query_any, query_ref), (grad_any, grad_ref),
@@ -72,18 +74,19 @@
     blank = jnp.zeros_like(query_t)
     query_wide = jnp.concatenate([query_t, blank], axis=0)
     grad_wide = jnp.concatenate([blank, grad_t], axis=0)
-    scores = jnp.dot(both, query_wide, preferred_element_type=jnp.float32)
-    dprob = jnp.dot(both, grad_wide, preferred_element_type=jnp.float32)
+    wide = jnp.concatenate([query_wide, grad_wide], axis=1)
+    product = jnp.dot(both, wide, preferred_element_type=jnp.float32)
+    scores = product[:, :tgt_count]
+    dprob = product[:, tgt_count:]
     first, last = source_range(source_ref, target_ref, tgt_count)
     position = lax.broadcasted_iota(jnp.int32, scores.shape, 0)
     allowed = jnp.logical_and(position >= first, position < last)
     expo = jnp.where(allowed, jnp.exp(scores), 0.0)
-    total = jnp.sum(expo, axis=0, keepdims=True)
-    delta = jnp.sum(expo * dprob, axis=0, keepdims=True) / total
-    prob = expo * (1.0 / total)
-    prob_low = prob.astype(jnp.bfloat16)
+    inverse = 1.0 / jnp.sum(expo, axis=0, keepdims=True)
+    delta = jnp.sum(expo * dprob, axis=0, keepdims=True) * inverse
+    prob = expo * inverse
     dscore = (prob * (dprob - delta)).astype(jnp.bfloat16)
-    both_grad = dot(dscore, query_wide, NT) + dot(prob_low, grad_wide, NT)
+    both_grad = dot(jnp.concatenate([dscore, prob.astype(jnp.bfloat16)], axis=1), wide, NT)
     both_low = both_grad.astype(jnp.bfloat16)
     low = low_ref[...].astype(jnp.float32)
     rows = low.shape[0]
@@ -93,16 +96,25 @@
     for at, block in enumerate(group_order(blocks)):
         sent_ref[at, :rows, :] = both_low[block * rows:(block + 1) * rows]
         sent_ref[at, rows:, :] = packed
-
-    wide = both_low.astype(jnp.float32)
+    sent_copy = pltpu.make_async_copy(sent_ref, sent_any, out_sems.at[0])
+    sent_copy.start()
+
+    exact = both_low.astype(jnp.float32)
     parts = []
     for start in range(0, rows, CUT):
         for block in range(blocks):
-            parts.append(wide[block * rows + start:block * rows + start + CUT])
+            parts.append(exact[block * rows + start:block * rows + start + CUT])
     turned_ref[...] = jnp.concatenate(parts, axis=0).T.astype(jnp.bfloat16)
+    turned_copy = pltpu.make_async_copy(turned_ref, turned_any, out_sems.at[1])
+    turned_copy.start()
 
     query_grad = dot(both, dscore, TN)
     query_grad_ref[...] = query_grad[:HS].astype(jnp.bfloat16)
+    query_copy = pltpu.make_async_copy(query_grad_ref, query_grad_any, out_sems.at[2])
+    query_copy.start()
+    sent_copy.wait()
+    turned_copy.wait()
+    query_copy.wait()
 
 
 def split_kernel(turned_ref, *out_refs):
@@ -201,7 +213,7 @@
             jax.ShapeDtypeStruct((2 * HS, src_count), jnp.bfloat16),
         ],
         in_specs=[hbm] * 6,
-        out_specs=[vmem] * 3,
+        out_specs=[hbm] * 3,
         scratch_shapes=[
             pltpu.SMEM(source_lengths.shape, jnp.int32),
             pltpu.SMEM(target_lengths.shape, jnp.int32),
@@ -209,7 +221,11 @@
             pltpu.VMEM(grad_t.shape, jnp.bfloat16),
             pltpu.VMEM(kv_cache.shape, jnp.bfloat16),
             pltpu.VMEM(low_rank.shape, jnp.bfloat16),
+            pltpu.VMEM(query_t.shape, jnp.bfloat16),
+            pltpu.VMEM((mp, rows + CUT, LANES), jnp.bfloat16),
+            pltpu.VMEM((2 * HS, src_count), jnp.bfloat16),
             pltpu.SemaphoreType.DMA((6,)),
+            pltpu.SemaphoreType.DMA((3,)),
         ],
         compiler_params=whole_vmem,
         name="attention_backward",

time: 23.4 us -> 23.6 us (level)
  no operation moved by 1% of the time
where the time goes in v2:
time: 23.6 us; the launch traced here: 23.3 us
  starting transfers between devices  12.3 us (52%)
  waiting for transfers between devices  5.87 us (25%)
  Pallas kernels  3.79 us (16%)
  between operations  0.68 us (3%)
  other arithmetic  0.61 us (3%)
    all_to_all x1, starting transfers between devices, local(): lax.all_to_all(sent, 'mp', 0, 0, axis_index_groups=[group_order(mp)], til...  9.38 us
    all_to_all x1, waiting for transfers between devices, local(): lax.all_to_all(sent, 'mp', 0, 0, axis_index_groups=[group_order(mp)], til...  3.58 us
    pallas_call x1, Pallas kernels, local(): pl.pallas_call(attention_kernel, out_shape=[jax.ShapeDtypeStruct((HS, tgt...  2.61 us
    ppermute x1, starting transfers between devices, local(): lax.ppermute(turned, 'mp', route)  1.56 us
    ppermute x1, starting transfers between devices, local(): up_grad = up_grad + lax.ppermute(shares[s], ('dp', 'mp'), route)  1.25 us
    ppermute x1, waiting for transfers between devices, local(): arrived.append(lax.ppermute(pieces[s], 'mp', route))  1.17 us
    ppermute x1, waiting for transfers between devices, local(): up_grad = up_grad + lax.ppermute(shares[s], ('dp', 'mp'), route)  1.12 us
    pallas_call x1, Pallas kernels, local(): pl.pallas_call(owner_kernel, out_shape=[jax.ShapeDtypeStruct((rows, width...  0.86 us
  transfers between devices with their start and end apart: 4, of which 3 were waited for; matrix products, arithmetic and copies ran while one was open for 0% of the time, Pallas kernels for 4%

profile of v2, /device:TPU:0, one launch (start us, length us, event | category | flops | bytes accessed | tf_op | source)
XLA Modules:
  0.0 23.3 jit_solution(13107269498748307287)
XLA Ops:
  0.6 2.6 %attention_backward.1 = (bf16[64,256]{1,0:T(8,128)(2,1)}, bf16[16,40,128]{2,1,0:T(8,128)(2,1)}, bf16[128,512]{1,0:T(8,128)(2,1)}) custom-call(s32[1,8]{1,0:T(1,128)} %source_any.1, s32[1,8]{1,0:T(1,128)} %target_any.1, bf16[64,256]{1,0:T(8,128)(2,1)} %bitcast.3, bf16[64,256]{1,0:T(8,128)(2,1)} %bitcast.4, bf16[512,128]{1,0:T(8,128)(2,1)} %kv_any.1, ...), custom_call_target="tpu_custom_call" | custom-call | tf_op jit(solution)/shard_map/attention_backward/pallas_call | solution.py:208
  3.3 1.6 %collective-permute-start = (bf16[128,512]{1,0:T(8,128)(2,1)}, bf16[128,512]{1,0:T(8,128)(2,1)S(1)}, u32[]{:S(2)}, u32[]{:S(2)}) collective-permute-start(bf16[128,512]{1,0:T(8,128)(2,1)} %get-tuple-element.20), channel_id=1, source_target_pairs={{0,0},{1,2},{2,4},{3,6},{4,8},{5,10},{6,12},{7,14},{8,1},{9,3},{10... | collective-permute-start | bytes 393224 | tf_op jit(solution)/shard_map/ppermute | solution.py:243
  4.8 9.4 %all-to-all-start = ((bf16[16,40,128]{2,1,0:T(8,128)(2,1)}), bf16[16,40,128]{2,1,0:T(8,128)(2,1)S(1)}, u32[]{:S(2)}, u32[]{:S(2)}) async-start(bf16[16,40,128]{2,1,0:T(8,128)(2,1)} %get-tuple-element.16), calls=%async_computation | async-start | bytes 327680 | tf_op jit(solution)/shard_map/all_to_all | solution.py:257
  14.2 0.0 collective-permute-done.turned_ref
  14.3 0.1 collective-permute-start.1
  14.4 1.2 %collective-permute-done.1.refs_1_ = bf16[64,512]{1,0:T(8,128)(2,1)S(1)} collective-permute-done((bf16[64,512]{1,0:T(8,128)(2,1)S(1)}, bf16[64,512]{1,0:T(8,128)(2,1)S(1)}, u32[]{:S(2)}, u32[]{:S(2)}) %collective-permute-start.1) | collective-permute-done | bytes 65568 | tf_op jit(solution)/shard_map/ppermute | solution.py:247
  15.6 0.0 copy-start
  15.6 3.6 %all-to-all-done.got_ref = bf16[16,40,128]{2,1,0:T(8,128)(2,1)S(1)} async-done(((bf16[16,40,128]{2,1,0:T(8,128)(2,1)}), bf16[16,40,128]{2,1,0:T(8,128)(2,1)S(1)}, u32[]{:S(2)}, u32[]{:S(2)}) %all-to-all-start) | async-done | bytes 163872 | tf_op jit(solution)/shard_map/all_to_all | solution.py:257
  19.2 0.3 %adapter_shares.1 = (f32[32,32]{1,0:T(8,128)S(1)}, f32[32,32]{1,0:T(8,128)S(1)}) custom-call(bf16[16,40,128]{2,1,0:T(8,128)(2,1)S(1)} %all-to-all-done.got_ref, bf16[2,64,512]{2,1,0:T(8,128)(2,1)S(1)} %order_pieces.1.pieces_ref), custom_call_target="tpu_custom_call" | custom-call | tf_op jit(solution)/shard_map/adapter_shares/pallas_call | solution.py:259
  19.4 1.3 %collective-permute-start.2 = (f32[32,32]{1,0:T(8,128)S(1)}, f32[32,32]{1,0:T(8,128)S(1)}, u32[]{:S(2)}, u32[]{:S(2)}) collective-permute-start(f32[32,32]{1,0:T(8,128)S(1)} %get-tuple-element.24), channel_id=1, source_target_pairs={{0,17},{1,16},{2,19},{3,18},{4,21},{5,20},{6,23},{7,22},{8,25},{9,... | collective-permute-start | bytes 12296 | tf_op jit(solution)/shard_map/ppermute | solution.py:273
  20.7 0.0 copy-done
  20.7 0.9 %owner_outputs.1 = (bf16[32,1024]{1,0:T(8,128)(2,1)}, bf16[32,1024]{1,0:T(8,128)(2,1)}, f32[32,32]{1,0:T(8,128)}) custom-call(bf16[16,40,128]{2,1,0:T(8,128)(2,1)S(1)} %all-to-all-done.got_ref, bf16[32,1024]{1,0:T(8,128)(2,1)S(1)} %copy-done), custom_call_target="tpu_custom_call" | custom-call | tf_op jit(solution)/shard_map/owner_outputs/pallas_call | solution.py:275
  21.6 1.1 %collective-permute-done.2 = f32[32,32]{1,0:T(8,128)S(1)} collective-permute-done((f32[32,32]{1,0:T(8,128)S(1)}, f32[32,32]{1,0:T(8,128)S(1)}, u32[]{:S(2)}, u32[]{:S(2)}) %collective-permute-start.2) | collective-permute-done | bytes 4128 | tf_op jit(solution)/shard_map/ppermute | solution.py:273
  22.7 0.6 %add.3 = f32[32,32]{1,0:T(8,128)} add(f32[32,32]{1,0:T(8,128)S(1)} %get-tuple-element.23, f32[32,32]{1,0:T(8,128)S(1)} %collective-permute-done.2) | non-fusion elementwise | flops 1024 | bytes 12288 | tf_op jit(solution)/shard_map/add | solution.py:273
  (2 shorter events, 0.1 us)
Async XLA Ops:
  3.3 10.9 %collective-permute-start = (bf16[128,512]{1,0:T(8,128)(2,1)}, bf16[128,512]{1,0:T(8,128)(2,1)S(1)}, u32[]{:S(2)}, u32[]{:S(2)}) collective-permute-start(bf16[128,512]{1,0:T(8,128)(2,1)} %get-tuple-element.20), channel_id=1, source_target_pairs={{0,0},{1,2},{2,4},{3,6},{4,8},{5,10},{6,12},{7,14},{8,1},{9,3},{10... | collective-permute-start | bytes 393224 | tf_op jit(solution)/shard_map/ppermute | solution.py:243
  4.8 14.4 %all-to-all-start = ((bf16[16,40,128]{2,1,0:T(8,128)(2,1)}), bf16[16,40,128]{2,1,0:T(8,128)(2,1)S(1)}, u32[]{:S(2)}, u32[]{:S(2)}) async-start(bf16[16,40,128]{2,1,0:T(8,128)(2,1)} %get-tuple-element.16), calls=%async_computation | async-start | bytes 327680 | tf_op jit(solution)/shard_map/all_to_all | solution.py:257
  14.3 1.3 %collective-permute-start.1 = (bf16[64,512]{1,0:T(8,128)(2,1)S(1)}, bf16[64,512]{1,0:T(8,128)(2,1)S(1)}, u32[]{:S(2)}, u32[]{:S(2)}) collective-permute-start(bf16[64,512]{1,0:T(8,128)(2,1)S(1)} %get-tuple-element.22), channel_id=1, source_target_pairs={{0,1},{1,0},{2,3},{3,2},{4,5},{5,4},{6,7},{7,6},{8,9},{9,8},{10,11... | collective-permute-start | bytes 196616 | tf_op jit(solution)/shard_map/ppermute | solution.py:247
  15.6 5.1 %copy-start = (bf16[32,1024]{1,0:T(8,128)(2,1)S(1)}, bf16[32,1024]{1,0:T(8,128)(2,1)}, u32[]{:S(2)}) copy-start(bf16[32,1024]{1,0:T(8,128)(2,1)} %up_ref.1) | copy-start | bytes 196612
  19.4 3.2 %collective-permute-start.2 = (f32[32,32]{1,0:T(8,128)S(1)}, f32[32,32]{1,0:T(8,128)S(1)}, u32[]{:S(2)}, u32[]{:S(2)}) collective-permute-start(f32[32,32]{1,0:T(8,128)S(1)} %get-tuple-element.24), channel_id=1, source_target_pairs={{0,17},{1,16},{2,19},{3,18},{4,21},{5,20},{6,23},{7,22},{8,25},{9,... | collective-permute-start | bytes 12296 | tf_op jit(solution)/shard_map/ppermute | solution.py:273

commit v3 on v0

--- a/solution.py
+++ b/solution.py
@@ -51,7 +51,7 @@
 
 
 def attention_kernel(
-    source_any, target_any, query_any, grad_any, kv_any, low_any, query_grad_ref, sent_ref, turned_ref,
+    source_any, target_any, query_any, grad_any, kv_any, low_any, query_grad_ref, sent_ref, both_grad_ref,
     source_ref, target_ref, query_ref, grad_ref, kv_ref, low_ref, sems,
 ):
     pairs = [
@@ -94,25 +94,24 @@
         sent_ref[at, :rows, :] = both_low[block * rows:(block + 1) * rows]
         sent_ref[at, rows:, :] = packed
 
-    wide = both_low.astype(jnp.float32)
+    both_grad_ref[...] = both_low
+    query_grad = dot(both, dscore, TN)
+    query_grad_ref[...] = query_grad[:HS].astype(jnp.bfloat16)
+
+
+def split_kernel(rows, both_grad_ref, *out_refs):
+    dp = len(out_refs)
+    step = HS // dp
+    exact = both_grad_ref[...].astype(jnp.float32)
     parts = []
     for start in range(0, rows, CUT):
-        for block in range(blocks):
-            parts.append(wide[block * rows + start:block * rows + start + CUT])
-    turned_ref[...] = jnp.concatenate(parts, axis=0).T.astype(jnp.bfloat16)
-
-    query_grad = dot(both, dscore, TN)
-    query_grad_ref[...] = query_grad[:HS].astype(jnp.bfloat16)
-
-
-def split_kernel(turned_ref, *out_refs):
-    dp = len(out_refs)
-    step = HS // dp
-    turned = turned_ref[...].astype(jnp.float32)
+        for block in range(0, exact.shape[0], rows):
+            parts.append(exact[block + start:block + start + CUT])
+    turned = jnp.concatenate(parts, axis=0).T
     pieces = []
     for j in range(dp):
-        rows = [turned[j * step:(j + 1) * step], turned[HS + j * step:HS + (j + 1) * step]]
-        pieces.append(jnp.concatenate(rows, axis=0))
+        halves = [turned[j * step:(j + 1) * step], turned[HS + j * step:HS + (j + 1) * step]]
+        pieces.append(jnp.concatenate(halves, axis=0))
     e = lax.rem(lax.axis_index("mp"), dp)
     pack = lax.axis_index("dp")
     for s, out_ref in enumerate(out_refs):
@@ -193,12 +192,12 @@
 
     query_t = query.T
     grad_t = out_grad.T
-    query_grad_t, sent, turned = pl.pallas_call(
+    query_grad_t, sent, both_grad = pl.pallas_call(
         attention_kernel,
         out_shape=[
             jax.ShapeDtypeStruct((HS, tgt_count), jnp.bfloat16),
             jax.ShapeDtypeStruct((mp, rows + CUT, LANES), jnp.bfloat16),
-            jax.ShapeDtypeStruct((2 * HS, src_count), jnp.bfloat16),
+            jax.ShapeDtypeStruct((src_count, 2 * HS), jnp.bfloat16),
         ],
         in_specs=[hbm] * 6,
         out_specs=[vmem] * 3,
@@ -217,14 +216,14 @@
 
     route = [(h, h * dp % mp + h * dp // mp) for h in range(mp)]
     pieces = pl.pallas_call(
-        split_kernel,
+        functools.partial(split_kernel, rows),
         out_shape=[jax.ShapeDtypeStruct((2 * step, src_count), jnp.bfloat16)] * dp,
         in_specs=[vmem],
         out_specs=[vmem] * dp,
         compiler_params=params,
         cost_estimate=pl.CostEstimate(flops=2 ** 36, bytes_accessed=2 ** 28, transcendentals=0),
         name="split_columns",
-    )(lax.ppermute(turned, "mp", route))
+    )(lax.ppermute(both_grad, "mp", route))
     arrived = [pieces[0]]
     for s in range(1, dp):
         route = [(m, m - m % dp + (m + s) % dp) for m in range(mp)]

time: 23.4 us -> 23.4 us (level)
  no operation moved by 1% of the time
where the time goes in v3:
time: 23.4 us; the launch traced here: 23.1 us
  starting transfers between devices  12.3 us (53%)
  waiting for transfers between devices  5.81 us (25%)
  Pallas kernels  3.7 us (16%)
  between operations  0.68 us (3%)
  other arithmetic  0.61 us (3%)
    all_to_all x1, starting transfers between devices, local(): lax.all_to_all(sent, 'mp', 0, 0, axis_index_groups=[group_order(mp)], til...  9.39 us
    all_to_all x1, waiting for transfers between devices, local(): lax.all_to_all(sent, 'mp', 0, 0, axis_index_groups=[group_order(mp)], til...  3.51 us
    pallas_call x1, Pallas kernels, local(): pl.pallas_call(attention_kernel, out_shape=[jax.ShapeDtypeStruct((HS, tgt...  2.46 us
    ppermute x1, starting transfers between devices, local(): lax.ppermute(both_grad, 'mp', route)  1.56 us
    ppermute x1, starting transfers between devices, local(): up_grad = up_grad + lax.ppermute(shares[s], ('dp', 'mp'), route)  1.25 us
    ppermute x1, waiting for transfers between devices, local(): arrived.append(lax.ppermute(pieces[s], 'mp', route))  1.17 us
    ppermute x1, waiting for transfers between devices, local(): up_grad = up_grad + lax.ppermute(shares[s], ('dp', 'mp'), route)  1.12 us
    pallas_call x1, Pallas kernels, local(): pl.pallas_call(owner_kernel, out_shape=[jax.ShapeDtypeStruct((rows, width...  0.86 us
  transfers between devices with their start and end apart: 4, of which 3 were waited for; matrix products, arithmetic and copies ran while one was open for 0% of the time, Pallas kernels for 4%

profile of v3, /device:TPU:0, one launch (start us, length us, event | category | flops | bytes accessed | tf_op | source)
XLA Modules:
  0.0 23.1 jit_solution(2812306285959508337)
XLA Ops:
  0.6 2.5 %attention_backward.1 = (bf16[64,256]{1,0:T(8,128)(2,1)}, bf16[16,40,128]{2,1,0:T(8,128)(2,1)}, bf16[512,128]{1,0:T(8,128)(2,1)}) custom-call(s32[1,8]{1,0:T(1,128)} %source_any.1, s32[1,8]{1,0:T(1,128)} %target_any.1, bf16[64,256]{1,0:T(8,128)(2,1)} %bitcast.3, bf16[64,256]{1,0:T(8,128)(2,1)} %bitcast.4, bf16[512,128]{1,0:T(8,128)(2,1)} %kv_any.1, ...), custom_call_target="tpu_custom_call" | custom-call | tf_op jit(solution)/shard_map/attention_backward/pallas_call | solution.py:195
  3.1 1.6 %collective-permute-start = (bf16[512,128]{1,0:T(8,128)(2,1)}, bf16[512,128]{1,0:T(8,128)(2,1)S(1)}, u32[]{:S(2)}, u32[]{:S(2)}) collective-permute-start(bf16[512,128]{1,0:T(8,128)(2,1)} %get-tuple-element.20), channel_id=1, source_target_pairs={{0,0},{1,2},{2,4},{3,6},{4,8},{5,10},{6,12},{7,14},{8,1},{9,3},{10... | collective-permute-start | bytes 393224 | tf_op jit(solution)/shard_map/ppermute | solution.py:226
  4.7 9.4 %all-to-all-start = ((bf16[16,40,128]{2,1,0:T(8,128)(2,1)}), bf16[16,40,128]{2,1,0:T(8,128)(2,1)S(1)}, u32[]{:S(2)}, u32[]{:S(2)}) async-start(bf16[16,40,128]{2,1,0:T(8,128)(2,1)} %get-tuple-element.16), calls=%async_computation | async-start | bytes 327680 | tf_op jit(solution)/shard_map/all_to_all | solution.py:240
  14.1 0.0 collective-permute-done.both_grad_ref
  14.1 0.1 split_columns.1
  14.2 0.1 collective-permute-start.1
  14.3 1.2 %collective-permute-done.1.refs_1_ = bf16[64,512]{1,0:T(8,128)(2,1)S(1)} collective-permute-done((bf16[64,512]{1,0:T(8,128)(2,1)S(1)}, bf16[64,512]{1,0:T(8,128)(2,1)S(1)}, u32[]{:S(2)}, u32[]{:S(2)}) %collective-permute-start.1) | collective-permute-done | bytes 65568 | tf_op jit(solution)/shard_map/ppermute | solution.py:230
  15.5 0.0 copy-start
  15.5 3.5 %all-to-all-done.got_ref = bf16[16,40,128]{2,1,0:T(8,128)(2,1)S(1)} async-done(((bf16[16,40,128]{2,1,0:T(8,128)(2,1)}), bf16[16,40,128]{2,1,0:T(8,128)(2,1)S(1)}, u32[]{:S(2)}, u32[]{:S(2)}) %all-to-all-start) | async-done | bytes 163872 | tf_op jit(solution)/shard_map/all_to_all | solution.py:240
  19.0 0.3 %adapter_shares.1 = (f32[32,32]{1,0:T(8,128)S(1)}, f32[32,32]{1,0:T(8,128)S(1)}) custom-call(bf16[16,40,128]{2,1,0:T(8,128)(2,1)S(1)} %all-to-all-done.got_ref, bf16[2,64,512]{2,1,0:T(8,128)(2,1)S(1)} %order_pieces.1.pieces_ref), custom_call_target="tpu_custom_call" | custom-call | tf_op jit(solution)/shard_map/adapter_shares/pallas_call | solution.py:242
  19.3 1.2 %collective-permute-start.2 = (f32[32,32]{1,0:T(8,128)S(1)}, f32[32,32]{1,0:T(8,128)S(1)}, u32[]{:S(2)}, u32[]{:S(2)}) collective-permute-start(f32[32,32]{1,0:T(8,128)S(1)} %get-tuple-element.24), channel_id=1, source_target_pairs={{0,17},{1,16},{2,19},{3,18},{4,21},{5,20},{6,23},{7,22},{8,25},{9,... | collective-permute-start | bytes 12296 | tf_op jit(solution)/shard_map/ppermute | solution.py:256
  20.6 0.0 copy-done
  20.6 0.9 %owner_outputs.1 = (bf16[32,1024]{1,0:T(8,128)(2,1)}, bf16[32,1024]{1,0:T(8,128)(2,1)}, f32[32,32]{1,0:T(8,128)}) custom-call(bf16[16,40,128]{2,1,0:T(8,128)(2,1)S(1)} %all-to-all-done.got_ref, bf16[32,1024]{1,0:T(8,128)(2,1)S(1)} %copy-done), custom_call_target="tpu_custom_call" | custom-call | tf_op jit(solution)/shard_map/owner_outputs/pallas_call | solution.py:258
  21.4 1.1 %collective-permute-done.2 = f32[32,32]{1,0:T(8,128)S(1)} collective-permute-done((f32[32,32]{1,0:T(8,128)S(1)}, f32[32,32]{1,0:T(8,128)S(1)}, u32[]{:S(2)}, u32[]{:S(2)}) %collective-permute-start.2) | collective-permute-done | bytes 4128 | tf_op jit(solution)/shard_map/ppermute | solution.py:256
  22.5 0.6 %add.3 = f32[32,32]{1,0:T(8,128)} add(f32[32,32]{1,0:T(8,128)S(1)} %get-tuple-element.23, f32[32,32]{1,0:T(8,128)S(1)} %collective-permute-done.2) | non-fusion elementwise | flops 1024 | bytes 12288 | tf_op jit(solution)/shard_map/add | solution.py:256
  (1 shorter events, 0.0 us)
Async XLA Ops:
  3.1 11.0 %collective-permute-start = (bf16[512,128]{1,0:T(8,128)(2,1)}, bf16[512,128]{1,0:T(8,128)(2,1)S(1)}, u32[]{:S(2)}, u32[]{:S(2)}) collective-permute-start(bf16[512,128]{1,0:T(8,128)(2,1)} %get-tuple-element.20), channel_id=1, source_target_pairs={{0,0},{1,2},{2,4},{3,6},{4,8},{5,10},{6,12},{7,14},{8,1},{9,3},{10... | collective-permute-start | bytes 393224 | tf_op jit(solution)/shard_map/ppermute | solution.py:226
  4.7 14.4 %all-to-all-start = ((bf16[16,40,128]{2,1,0:T(8,128)(2,1)}), bf16[16,40,128]{2,1,0:T(8,128)(2,1)S(1)}, u32[]{:S(2)}, u32[]{:S(2)}) async-start(bf16[16,40,128]{2,1,0:T(8,128)(2,1)} %get-tuple-element.16), calls=%async_computation | async-start | bytes 327680 | tf_op jit(solution)/shard_map/all_to_all | solution.py:240
  14.2 1.3 %collective-permute-start.1 = (bf16[64,512]{1,0:T(8,128)(2,1)S(1)}, bf16[64,512]{1,0:T(8,128)(2,1)S(1)}, u32[]{:S(2)}, u32[]{:S(2)}) collective-permute-start(bf16[64,512]{1,0:T(8,128)(2,1)S(1)} %get-tuple-element.22), channel_id=1, source_target_pairs={{0,1},{1,0},{2,3},{3,2},{4,5},{5,4},{6,7},{7,6},{8,9},{9,8},{10,11... | collective-permute-start | bytes 196616 | tf_op jit(solution)/shard_map/ppermute | solution.py:230
  15.5 5.0 %copy-start = (bf16[32,1024]{1,0:T(8,128)(2,1)S(1)}, bf16[32,1024]{1,0:T(8,128)(2,1)}, u32[]{:S(2)}) copy-start(bf16[32,1024]{1,0:T(8,128)(2,1)} %up_ref.1) | copy-start | bytes 196612
  19.3 3.2 %collective-permute-start.2 = (f32[32,32]{1,0:T(8,128)S(1)}, f32[32,32]{1,0:T(8,128)S(1)}, u32[]{:S(2)}, u32[]{:S(2)}) collective-permute-start(f32[32,32]{1,0:T(8,128)S(1)} %get-tuple-element.24), channel_id=1, source_target_pairs={{0,17},{1,16},{2,19},{3,18},{4,21},{5,20},{6,23},{7,22},{8,25},{9,... | collective-permute-start | bytes 12296 | tf_op jit(solution)/shard_map/ppermute | solution.py:256

commit v4 on v3

--- a/solution.py
+++ b/solution.py
@@ -50,12 +50,22 @@
     return first, last
 
 
+PARTS = 4
+
+
+def cut_copies(source, target):
+    size = target.shape[0] // PARTS
+    return [(source.at[pl.ds(i * size, size)], target.at[pl.ds(i * size, size)]) for i in range(PARTS)]
+
+
 def attention_kernel(
-    source_any, target_any, query_any, grad_any, kv_any, low_any, query_grad_ref, sent_ref, both_grad_ref,
-    source_ref, target_ref, query_ref, grad_ref, kv_ref, low_ref, sems,
+    source_any, target_any, query_any, grad_any, kv_any, low_any,
+    query_grad_any, sent_any, both_grad_any,
+    source_ref, target_ref, query_ref, grad_ref, kv_ref, low_ref,
+    query_grad_ref, sent_ref, both_grad_ref, sems, out_sems,
 ):
-    pairs = [
-        (kv_any, kv_ref), (query_any, query_ref), (grad_any, grad_ref),
+    pairs = cut_copies(kv_any, kv_ref) + [
+        (query_any, query_ref), (grad_any, grad_ref),
         (source_any, source_ref), (target_any, target_ref), (low_any, low_ref),
     ]
     copies = [
@@ -97,6 +107,15 @@
     both_grad_ref[...] = both_low
     query_grad = dot(both, dscore, TN)
     query_grad_ref[...] = query_grad[:HS].astype(jnp.bfloat16)
+    pairs = cut_copies(sent_ref, sent_any) + cut_copies(both_grad_ref, both_grad_any)
+    pairs.append((query_grad_ref, query_grad_any))
+    copies = [
+        pltpu.make_async_copy(here, there, out_sems.at[i]) for i, (here, there) in enumerate(pairs)
+    ]
+    for copy in copies:
+        copy.start()
+    for copy in copies:
+        copy.wait()
 
 
 def split_kernel(rows, both_grad_ref, *out_refs):
@@ -200,7 +219,7 @@
             jax.ShapeDtypeStruct((src_count, 2 * HS), jnp.bfloat16),
         ],
         in_specs=[hbm] * 6,
-        out_specs=[vmem] * 3,
+        out_specs=[hbm] * 3,
         scratch_shapes=[
             pltpu.SMEM(source_lengths.shape, jnp.int32),
             pltpu.SMEM(target_lengths.shape, jnp.int32),
@@ -208,7 +227,11 @@
             pltpu.VMEM(grad_t.shape, jnp.bfloat16),
             pltpu.VMEM(kv_cache.shape, jnp.bfloat16),
             pltpu.VMEM(low_rank.shape, jnp.bfloat16),
-            pltpu.SemaphoreType.DMA((6,)),
+            pltpu.VMEM(query_t.shape, jnp.bfloat16),
+            pltpu.VMEM((mp, rows + CUT, LANES), jnp.bfloat16),
+            pltpu.VMEM((src_count, 2 * HS), jnp.bfloat16),
+            pltpu.SemaphoreType.DMA((PARTS + 5,)),
+            pltpu.SemaphoreType.DMA((2 * PARTS + 1,)),
         ],
         compiler_params=whole_vmem,
         name="attention_backward",

time: 23.4 us -> 23.5 us (level)
  no operation moved by 1% of the time
where the time goes in v4:
time: 23.5 us; the launch traced here: 23.2 us
  starting transfers between devices  12.3 us (52%)
  waiting for transfers between devices  5.81 us (25%)
  Pallas kernels  3.75 us (16%)
  between operations  0.68 us (3%)
  other arithmetic  0.61 us (3%)
    all_to_all x1, starting transfers between devices, local(): lax.all_to_all(sent, 'mp', 0, 0, axis_index_groups=[group_order(mp)], til...  9.38 us
    all_to_all x1, waiting for transfers between devices, local(): lax.all_to_all(sent, 'mp', 0, 0, axis_index_groups=[group_order(mp)], til...  3.51 us
    pallas_call x1, Pallas kernels, local(): pl.pallas_call(attention_kernel, out_shape=[jax.ShapeDtypeStruct((HS, tgt...  2.51 us
    ppermute x1, starting transfers between devices, local(): lax.ppermute(both_grad, 'mp', route)  1.56 us
    ppermute x1, starting transfers between devices, local(): up_grad = up_grad + lax.ppermute(shares[s], ('dp', 'mp'), route)  1.25 us
    ppermute x1, waiting for transfers between devices, local(): arrived.append(lax.ppermute(pieces[s], 'mp', route))  1.17 us
    ppermute x1, waiting for transfers between devices, local(): up_grad = up_grad + lax.ppermute(shares[s], ('dp', 'mp'), route)  1.12 us
    pallas_call x1, Pallas kernels, local(): pl.pallas_call(owner_kernel, out_shape=[jax.ShapeDtypeStruct((rows, width...  0.86 us
  transfers between devices with their start and end apart: 4, of which 3 were waited for; matrix products, arithmetic and copies ran while one was open for 0% of the time, Pallas kernels for 4%

profile of v4, /device:TPU:0, one launch (start us, length us, event | category | flops | bytes accessed | tf_op | source)
XLA Modules:
  0.0 23.2 jit_solution(14644353699811191340)
XLA Ops:
  0.6 2.5 %attention_backward.1 = (bf16[64,256]{1,0:T(8,128)(2,1)}, bf16[16,40,128]{2,1,0:T(8,128)(2,1)}, bf16[512,128]{1,0:T(8,128)(2,1)}) custom-call(s32[1,8]{1,0:T(1,128)} %source_any.1, s32[1,8]{1,0:T(1,128)} %target_any.1, bf16[64,256]{1,0:T(8,128)(2,1)} %bitcast.3, bf16[64,256]{1,0:T(8,128)(2,1)} %bitcast.4, bf16[512,128]{1,0:T(8,128)(2,1)} %kv_any.1, ...), custom_call_target="tpu_custom_call" | custom-call | tf_op jit(solution)/shard_map/attention_backward/pallas_call | solution.py:214
  3.1 1.6 %collective-permute-start = (bf16[512,128]{1,0:T(8,128)(2,1)}, bf16[512,128]{1,0:T(8,128)(2,1)S(1)}, u32[]{:S(2)}, u32[]{:S(2)}) collective-permute-start(bf16[512,128]{1,0:T(8,128)(2,1)} %get-tuple-element.20), channel_id=1, source_target_pairs={{0,0},{1,2},{2,4},{3,6},{4,8},{5,10},{6,12},{7,14},{8,1},{9,3},{10... | collective-permute-start | bytes 393224 | tf_op jit(solution)/shard_map/ppermute | solution.py:249
  4.7 9.4 %all-to-all-start = ((bf16[16,40,128]{2,1,0:T(8,128)(2,1)}), bf16[16,40,128]{2,1,0:T(8,128)(2,1)S(1)}, u32[]{:S(2)}, u32[]{:S(2)}) async-start(bf16[16,40,128]{2,1,0:T(8,128)(2,1)} %get-tuple-element.16), calls=%async_computation | async-start | bytes 327680 | tf_op jit(solution)/shard_map/all_to_all | solution.py:263
  14.1 0.0 collective-permute-done.both_grad_ref
  14.1 0.1 split_columns.1
  14.2 0.1 collective-permute-start.1
  14.4 1.2 %collective-permute-done.1.refs_1_ = bf16[64,512]{1,0:T(8,128)(2,1)S(1)} collective-permute-done((bf16[64,512]{1,0:T(8,128)(2,1)S(1)}, bf16[64,512]{1,0:T(8,128)(2,1)S(1)}, u32[]{:S(2)}, u32[]{:S(2)}) %collective-permute-start.1) | collective-permute-done | bytes 65568 | tf_op jit(solution)/shard_map/ppermute | solution.py:253
  15.6 0.0 copy-start
  15.6 3.5 %all-to-all-done.got_ref = bf16[16,40,128]{2,1,0:T(8,128)(2,1)S(1)} async-done(((bf16[16,40,128]{2,1,0:T(8,128)(2,1)}), bf16[16,40,128]{2,1,0:T(8,128)(2,1)S(1)}, u32[]{:S(2)}, u32[]{:S(2)}) %all-to-all-start) | async-done | bytes 163872 | tf_op jit(solution)/shard_map/all_to_all | solution.py:263
  19.1 0.3 %adapter_shares.1 = (f32[32,32]{1,0:T(8,128)S(1)}, f32[32,32]{1,0:T(8,128)S(1)}) custom-call(bf16[16,40,128]{2,1,0:T(8,128)(2,1)S(1)} %all-to-all-done.got_ref, bf16[2,64,512]{2,1,0:T(8,128)(2,1)S(1)} %order_pieces.1.pieces_ref), custom_call_target="tpu_custom_call" | custom-call | tf_op jit(solution)/shard_map/adapter_shares/pallas_call | solution.py:265
  19.3 1.3 %collective-permute-start.2 = (f32[32,32]{1,0:T(8,128)S(1)}, f32[32,32]{1,0:T(8,128)S(1)}, u32[]{:S(2)}, u32[]{:S(2)}) collective-permute-start(f32[32,32]{1,0:T(8,128)S(1)} %get-tuple-element.24), channel_id=1, source_target_pairs={{0,17},{1,16},{2,19},{3,18},{4,21},{5,20},{6,23},{7,22},{8,25},{9,... | collective-permute-start | bytes 12296 | tf_op jit(solution)/shard_map/ppermute | solution.py:279
  20.6 0.0 copy-done
  20.6 0.9 %owner_outputs.1 = (bf16[32,1024]{1,0:T(8,128)(2,1)}, bf16[32,1024]{1,0:T(8,128)(2,1)}, f32[32,32]{1,0:T(8,128)}) custom-call(bf16[16,40,128]{2,1,0:T(8,128)(2,1)S(1)} %all-to-all-done.got_ref, bf16[32,1024]{1,0:T(8,128)(2,1)S(1)} %copy-done), custom_call_target="tpu_custom_call" | custom-call | tf_op jit(solution)/shard_map/owner_outputs/pallas_call | solution.py:281
  21.5 1.1 %collective-permute-done.2 = f32[32,32]{1,0:T(8,128)S(1)} collective-permute-done((f32[32,32]{1,0:T(8,128)S(1)}, f32[32,32]{1,0:T(8,128)S(1)}, u32[]{:S(2)}, u32[]{:S(2)}) %collective-permute-start.2) | collective-permute-done | bytes 4128 | tf_op jit(solution)/shard_map/ppermute | solution.py:279
  22.6 0.6 %add.3 = f32[32,32]{1,0:T(8,128)} add(f32[32,32]{1,0:T(8,128)S(1)} %get-tuple-element.23, f32[32,32]{1,0:T(8,128)S(1)} %collective-permute-done.2) | non-fusion elementwise | flops 1024 | bytes 12288 | tf_op jit(solution)/shard_map/add | solution.py:279
  (1 shorter events, 0.0 us)
Async XLA Ops:
  3.1 10.9 %collective-permute-start = (bf16[512,128]{1,0:T(8,128)(2,1)}, bf16[512,128]{1,0:T(8,128)(2,1)S(1)}, u32[]{:S(2)}, u32[]{:S(2)}) collective-permute-start(bf16[512,128]{1,0:T(8,128)(2,1)} %get-tuple-element.20), channel_id=1, source_target_pairs={{0,0},{1,2},{2,4},{3,6},{4,8},{5,10},{6,12},{7,14},{8,1},{9,3},{10... | collective-permute-start | bytes 393224 | tf_op jit(solution)/shard_map/ppermute | solution.py:249
  4.7 14.4 %all-to-all-start = ((bf16[16,40,128]{2,1,0:T(8,128)(2,1)}), bf16[16,40,128]{2,1,0:T(8,128)(2,1)S(1)}, u32[]{:S(2)}, u32[]{:S(2)}) async-start(bf16[16,40,128]{2,1,0:T(8,128)(2,1)} %get-tuple-element.16), calls=%async_computation | async-start | bytes 327680 | tf_op jit(solution)/shard_map/all_to_all | solution.py:263
  14.2 1.3 %collective-permute-start.1 = (bf16[64,512]{1,0:T(8,128)(2,1)S(1)}, bf16[64,512]{1,0:T(8,128)(2,1)S(1)}, u32[]{:S(2)}, u32[]{:S(2)}) collective-permute-start(bf16[64,512]{1,0:T(8,128)(2,1)S(1)} %get-tuple-element.22), channel_id=1, source_target_pairs={{0,1},{1,0},{2,3},{3,2},{4,5},{5,4},{6,7},{7,6},{8,9},{9,8},{10,11... | collective-permute-start | bytes 196616 | tf_op jit(solution)/shard_map/ppermute | solution.py:253
  15.6 5.0 %copy-start = (bf16[32,1024]{1,0:T(8,128)(2,1)S(1)}, bf16[32,1024]{1,0:T(8,128)(2,1)}, u32[]{:S(2)}) copy-start(bf16[32,1024]{1,0:T(8,128)(2,1)} %up_ref.1) | copy-start | bytes 196612
  19.3 3.2 %collective-permute-start.2 = (f32[32,32]{1,0:T(8,128)S(1)}, f32[32,32]{1,0:T(8,128)S(1)}, u32[]{:S(2)}, u32[]{:S(2)}) collective-permute-start(f32[32,32]{1,0:T(8,128)S(1)} %get-tuple-element.24), channel_id=1, source_target_pairs={{0,17},{1,16},{2,19},{3,18},{4,21},{5,20},{6,23},{7,22},{8,25},{9,... | collective-permute-start | bytes 12296 | tf_op jit(solution)/shard_map/ppermute | solution.py:279

commit v5 on v3

--- a/solution.py
+++ b/solution.py
@@ -72,19 +72,30 @@
     blank = jnp.zeros_like(query_t)
     query_wide = jnp.concatenate([query_t, blank], axis=0)
     grad_wide = jnp.concatenate([blank, grad_t], axis=0)
-    scores = jnp.dot(both, query_wide, preferred_element_type=jnp.float32)
-    dprob = jnp.dot(both, grad_wide, preferred_element_type=jnp.float32)
     first, last = source_range(source_ref, target_ref, tgt_count)
-    position = lax.broadcasted_iota(jnp.int32, scores.shape, 0)
-    allowed = jnp.logical_and(position >= first, position < last)
-    expo = jnp.where(allowed, jnp.exp(scores), 0.0)
-    total = jnp.sum(expo, axis=0, keepdims=True)
-    delta = jnp.sum(expo * dprob, axis=0, keepdims=True) / total
-    prob = expo * (1.0 / total)
-    prob_low = prob.astype(jnp.bfloat16)
-    dscore = (prob * (dprob - delta)).astype(jnp.bfloat16)
-    both_grad = dot(dscore, query_wide, NT) + dot(prob_low, grad_wide, NT)
-    both_low = both_grad.astype(jnp.bfloat16)
+    half = both.shape[0] // 2
+    parts = [both[:half], both[half:]]
+    scores = [jnp.dot(part, query_wide, preferred_element_type=jnp.float32) for part in parts]
+    dprobs = [jnp.dot(part, grad_wide, preferred_element_type=jnp.float32) for part in parts]
+    expos = []
+    for i, score in enumerate(scores):
+        position = i * half + lax.broadcasted_iota(jnp.int32, score.shape, 0)
+        allowed = jnp.logical_and(position >= first, position < last)
+        expos.append(jnp.where(allowed, jnp.exp(score), 0.0))
+    inverse = 1.0 / sum(jnp.sum(expo, axis=0, keepdims=True) for expo in expos)
+    weighted = sum(
+        jnp.sum(expo * dprob, axis=0, keepdims=True) for expo, dprob in zip(expos, dprobs)
+    )
+    delta = weighted * inverse
+    probs = [expo * inverse for expo in expos]
+    dscores = [
+        (prob * (dprob - delta)).astype(jnp.bfloat16) for prob, dprob in zip(probs, dprobs)
+    ]
+    both_low = jnp.concatenate([
+        (dot(dscore, query_wide, NT) + dot(prob.astype(jnp.bfloat16), grad_wide, NT))
+        .astype(jnp.bfloat16)
+        for dscore, prob in zip(dscores, probs)
+    ], axis=0)
     low = low_ref[...].astype(jnp.float32)
     rows = low.shape[0]
     blocks = sent_ref.shape[0]
@@ -95,7 +106,7 @@
         sent_ref[at, rows:, :] = packed
 
     both_grad_ref[...] = both_low
-    query_grad = dot(both, dscore, TN)
+    query_grad = sum(dot(part, dscore, TN) for part, dscore in zip(parts, dscores))
     query_grad_ref[...] = query_grad[:HS].astype(jnp.bfloat16)
 
 

time: 23.4 us -> 23.3 us (level)
  no operation moved by 1% of the time
where the time goes in v5:
time: 23.3 us; the launch traced here: 23 us
  starting transfers between devices  12.4 us (53%)
  waiting for transfers between devices  5.8 us (25%)
  Pallas kernels  3.6 us (15%)
  between operations  0.68 us (3%)
  other arithmetic  0.61 us (3%)
    all_to_all x1, starting transfers between devices, local(): lax.all_to_all(sent, 'mp', 0, 0, axis_index_groups=[group_order(mp)], til...  9.39 us
    all_to_all x1, waiting for transfers between devices, local(): lax.all_to_all(sent, 'mp', 0, 0, axis_index_groups=[group_order(mp)], til...  3.51 us
    pallas_call x1, Pallas kernels, local(): pl.pallas_call(attention_kernel, out_shape=[jax.ShapeDtypeStruct((HS, tgt...  2.36 us
    ppermute x1, starting transfers between devices, local(): lax.ppermute(both_grad, 'mp', route)  1.56 us
    ppermute x1, starting transfers between devices, local(): up_grad = up_grad + lax.ppermute(shares[s], ('dp', 'mp'), route)  1.26 us
    ppermute x1, waiting for transfers between devices, local(): arrived.append(lax.ppermute(pieces[s], 'mp', route))  1.17 us
    ppermute x1, waiting for transfers between devices, local(): up_grad = up_grad + lax.ppermute(shares[s], ('dp', 'mp'), route)  1.11 us
    pallas_call x1, Pallas kernels, local(): pl.pallas_call(owner_kernel, out_shape=[jax.ShapeDtypeStruct((rows, width...  0.86 us
  transfers between devices with their start and end apart: 4, of which 3 were waited for; matrix products, arithmetic and copies ran while one was open for 0% of the time, Pallas kernels for 4%

profile of v5, /device:TPU:0, one launch (start us, length us, event | category | flops | bytes accessed | tf_op | source)
XLA Modules:
  0.0 23.0 jit_solution(2740123150852536871)
XLA Ops:
  0.6 2.4 %attention_backward.1 = (bf16[64,256]{1,0:T(8,128)(2,1)}, bf16[16,40,128]{2,1,0:T(8,128)(2,1)}, bf16[512,128]{1,0:T(8,128)(2,1)}) custom-call(s32[1,8]{1,0:T(1,128)} %source_any.1, s32[1,8]{1,0:T(1,128)} %target_any.1, bf16[64,256]{1,0:T(8,128)(2,1)} %bitcast.3, bf16[64,256]{1,0:T(8,128)(2,1)} %bitcast.4, bf16[512,128]{1,0:T(8,128)(2,1)} %kv_any.1, ...), custom_call_target="tpu_custom_call" | custom-call | tf_op jit(solution)/shard_map/attention_backward/pallas_call | solution.py:206
  3.0 1.6 %collective-permute-start = (bf16[512,128]{1,0:T(8,128)(2,1)}, bf16[512,128]{1,0:T(8,128)(2,1)S(1)}, u32[]{:S(2)}, u32[]{:S(2)}) collective-permute-start(bf16[512,128]{1,0:T(8,128)(2,1)} %get-tuple-element.20), channel_id=1, source_target_pairs={{0,0},{1,2},{2,4},{3,6},{4,8},{5,10},{6,12},{7,14},{8,1},{9,3},{10... | collective-permute-start | bytes 393224 | tf_op jit(solution)/shard_map/ppermute | solution.py:237
  4.6 9.4 %all-to-all-start = ((bf16[16,40,128]{2,1,0:T(8,128)(2,1)}), bf16[16,40,128]{2,1,0:T(8,128)(2,1)S(1)}, u32[]{:S(2)}, u32[]{:S(2)}) async-start(bf16[16,40,128]{2,1,0:T(8,128)(2,1)} %get-tuple-element.16), calls=%async_computation | async-start | bytes 327680 | tf_op jit(solution)/shard_map/all_to_all | solution.py:251
  14.0 0.0 collective-permute-done.both_grad_ref
  14.0 0.1 split_columns.1
  14.1 0.1 collective-permute-start.1
  14.2 1.2 %collective-permute-done.1.refs_1_ = bf16[64,512]{1,0:T(8,128)(2,1)S(1)} collective-permute-done((bf16[64,512]{1,0:T(8,128)(2,1)S(1)}, bf16[64,512]{1,0:T(8,128)(2,1)S(1)}, u32[]{:S(2)}, u32[]{:S(2)}) %collective-permute-start.1) | collective-permute-done | bytes 65568 | tf_op jit(solution)/shard_map/ppermute | solution.py:241
  15.4 0.0 copy-start
  15.4 3.5 %all-to-all-done.got_ref = bf16[16,40,128]{2,1,0:T(8,128)(2,1)S(1)} async-done(((bf16[16,40,128]{2,1,0:T(8,128)(2,1)}), bf16[16,40,128]{2,1,0:T(8,128)(2,1)S(1)}, u32[]{:S(2)}, u32[]{:S(2)}) %all-to-all-start) | async-done | bytes 163872 | tf_op jit(solution)/shard_map/all_to_all | solution.py:251
  18.9 0.3 %adapter_shares.1 = (f32[32,32]{1,0:T(8,128)S(1)}, f32[32,32]{1,0:T(8,128)S(1)}) custom-call(bf16[16,40,128]{2,1,0:T(8,128)(2,1)S(1)} %all-to-all-done.got_ref, bf16[2,64,512]{2,1,0:T(8,128)(2,1)S(1)} %order_pieces.1.pieces_ref), custom_call_target="tpu_custom_call" | custom-call | tf_op jit(solution)/shard_map/adapter_shares/pallas_call | solution.py:253
  19.2 1.3 %collective-permute-start.2 = (f32[32,32]{1,0:T(8,128)S(1)}, f32[32,32]{1,0:T(8,128)S(1)}, u32[]{:S(2)}, u32[]{:S(2)}) collective-permute-start(f32[32,32]{1,0:T(8,128)S(1)} %get-tuple-element.24), channel_id=1, source_target_pairs={{0,17},{1,16},{2,19},{3,18},{4,21},{5,20},{6,23},{7,22},{8,25},{9,... | collective-permute-start | bytes 12296 | tf_op jit(solution)/shard_map/ppermute | solution.py:267
  20.5 0.0 copy-done
  20.5 0.9 %owner_outputs.1 = (bf16[32,1024]{1,0:T(8,128)(2,1)}, bf16[32,1024]{1,0:T(8,128)(2,1)}, f32[32,32]{1,0:T(8,128)}) custom-call(bf16[16,40,128]{2,1,0:T(8,128)(2,1)S(1)} %all-to-all-done.got_ref, bf16[32,1024]{1,0:T(8,128)(2,1)S(1)} %copy-done), custom_call_target="tpu_custom_call" | custom-call | tf_op jit(solution)/shard_map/owner_outputs/pallas_call | solution.py:269
  21.3 1.1 %collective-permute-done.2 = f32[32,32]{1,0:T(8,128)S(1)} collective-permute-done((f32[32,32]{1,0:T(8,128)S(1)}, f32[32,32]{1,0:T(8,128)S(1)}, u32[]{:S(2)}, u32[]{:S(2)}) %collective-permute-start.2) | collective-permute-done | bytes 4128 | tf_op jit(solution)/shard_map/ppermute | solution.py:267
  22.4 0.6 %add.3 = f32[32,32]{1,0:T(8,128)} add(f32[32,32]{1,0:T(8,128)S(1)} %get-tuple-element.23, f32[32,32]{1,0:T(8,128)S(1)} %collective-permute-done.2) | non-fusion elementwise | flops 1024 | bytes 12288 | tf_op jit(solution)/shard_map/add | solution.py:267
  (1 shorter events, 0.0 us)
Async XLA Ops:
  3.0 11.0 %collective-permute-start = (bf16[512,128]{1,0:T(8,128)(2,1)}, bf16[512,128]{1,0:T(8,128)(2,1)S(1)}, u32[]{:S(2)}, u32[]{:S(2)}) collective-permute-start(bf16[512,128]{1,0:T(8,128)(2,1)} %get-tuple-element.20), channel_id=1, source_target_pairs={{0,0},{1,2},{2,4},{3,6},{4,8},{5,10},{6,12},{7,14},{8,1},{9,3},{10... | collective-permute-start | bytes 393224 | tf_op jit(solution)/shard_map/ppermute | solution.py:237
  4.6 14.4 %all-to-all-start = ((bf16[16,40,128]{2,1,0:T(8,128)(2,1)}), bf16[16,40,128]{2,1,0:T(8,128)(2,1)S(1)}, u32[]{:S(2)}, u32[]{:S(2)}) async-start(bf16[16,40,128]{2,1,0:T(8,128)(2,1)} %get-tuple-element.16), calls=%async_computation | async-start | bytes 327680 | tf_op jit(solution)/shard_map/all_to_all | solution.py:251
  14.1 1.3 %collective-permute-start.1 = (bf16[64,512]{1,0:T(8,128)(2,1)S(1)}, bf16[64,512]{1,0:T(8,128)(2,1)S(1)}, u32[]{:S(2)}, u32[]{:S(2)}) collective-permute-start(bf16[64,512]{1,0:T(8,128)(2,1)S(1)} %get-tuple-element.22), channel_id=1, source_target_pairs={{0,1},{1,0},{2,3},{3,2},{4,5},{5,4},{6,7},{7,6},{8,9},{9,8},{10,11... | collective-permute-start | bytes 196616 | tf_op jit(solution)/shard_map/ppermute | solution.py:241
  15.4 5.1 %copy-start = (bf16[32,1024]{1,0:T(8,128)(2,1)S(1)}, bf16[32,1024]{1,0:T(8,128)(2,1)}, u32[]{:S(2)}) copy-start(bf16[32,1024]{1,0:T(8,128)(2,1)} %up_ref.1) | copy-start | bytes 196612
  19.2 3.2 %collective-permute-start.2 = (f32[32,32]{1,0:T(8,128)S(1)}, f32[32,32]{1,0:T(8,128)S(1)}, u32[]{:S(2)}, u32[]{:S(2)}) collective-permute-start(f32[32,32]{1,0:T(8,128)S(1)} %get-tuple-element.24), channel_id=1, source_target_pairs={{0,17},{1,16},{2,19},{3,18},{4,21},{5,20},{6,23},{7,22},{8,25},{9,... | collective-permute-start | bytes 12296 | tf_op jit(solution)/shard_map/ppermute | solution.py:267

commit v6 on v5

--- a/solution.py
+++ b/solution.py
@@ -29,8 +29,8 @@
     order = []
     for near, far in ((2, 3), (1, 0)):
         for i in range(quarter):
-            order.append(near * quarter + turned[quarter - 1 - i])
-            order.append(far * quarter + turned[(quarter - 1 - i) ^ 1])
+            order.append(near * quarter + (turned[quarter - 1 - i] ^ (quarter // 2)))
+            order.append(far * quarter + (turned[(quarter - 1 - i) ^ 1] ^ (quarter // 2)))
     return order
 
 

time: 23.3 us -> 24.4 us (1.047)
  waiting for transfers between devices: 5.8 us -> 7.61 us
  starting transfers between devices: 12.4 us -> 11.7 us
    all_to_all x1, waiting for transfers between devices: 3.51 us -> 4.52 us  [local(): lax.all_to_all(sent, 'mp', 0, 0, axis_index_groups=[group_order(mp)], til...]
    ppermute x1, waiting for transfers between devices: 1.11 us -> 1.91 us  [local(): up_grad = up_grad + lax.ppermute(shares[s], ('dp', 'mp'), route)]
    ppermute x1, starting transfers between devices: 1.26 us -> 0.55 us  [local(): up_grad = up_grad + lax.ppermute(shares[s], ('dp', 'mp'), route)]
where the time goes in v6:
time: 24.4 us; the launch traced here: 24.1 us
  starting transfers between devices  11.7 us (48%)
  waiting for transfers between devices  7.61 us (31%)
  Pallas kernels  3.6 us (15%)
  between operations  0.68 us (3%)
  other arithmetic  0.61 us (2%)
    all_to_all x1, starting transfers between devices, local(): lax.all_to_all(sent, 'mp', 0, 0, axis_index_groups=[group_order(mp)], til...  9.39 us
    all_to_all x1, waiting for transfers between devices, local(): lax.all_to_all(sent, 'mp', 0, 0, axis_index_groups=[group_order(mp)], til...  4.52 us
    pallas_call x1, Pallas kernels, local(): pl.pallas_call(attention_kernel, out_shape=[jax.ShapeDtypeStruct((HS, tgt...  2.36 us
    ppermute x1, waiting for transfers between devices, local(): up_grad = up_grad + lax.ppermute(shares[s], ('dp', 'mp'), route)  1.91 us
    ppermute x1, starting transfers between devices, local(): lax.ppermute(both_grad, 'mp', route)  1.56 us
    ppermute x1, waiting for transfers between devices, local(): arrived.append(lax.ppermute(pieces[s], 'mp', route))  1.17 us
    pallas_call x1, Pallas kernels, local(): pl.pallas_call(owner_kernel, out_shape=[jax.ShapeDtypeStruct((rows, width...  0.86 us
    add x1, other arithmetic, local(): up_grad = up_grad + lax.ppermute(shares[s], ('dp', 'mp'), route)  0.61 us
  transfers between devices with their start and end apart: 4, of which 3 were waited for; matrix products, arithmetic and copies ran while one was open for 0% of the time, Pallas kernels for 4%

profile of v6, /device:TPU:0, one launch (start us, length us, event | category | flops | bytes accessed | tf_op | source)
XLA Modules:
  0.0 24.1 jit_solution(11069961692818181518)
XLA Ops:
  0.6 2.4 %attention_backward.1 = (bf16[64,256]{1,0:T(8,128)(2,1)}, bf16[16,40,128]{2,1,0:T(8,128)(2,1)}, bf16[512,128]{1,0:T(8,128)(2,1)}) custom-call(s32[1,8]{1,0:T(1,128)} %source_any.1, s32[1,8]{1,0:T(1,128)} %target_any.1, bf16[64,256]{1,0:T(8,128)(2,1)} %bitcast.3, bf16[64,256]{1,0:T(8,128)(2,1)} %bitcast.4, bf16[512,128]{1,0:T(8,128)(2,1)} %kv_any.1, ...), custom_call_target="tpu_custom_call" | custom-call | tf_op jit(solution)/shard_map/attention_backward/pallas_call | solution.py:206
  3.0 1.6 %collective-permute-start = (bf16[512,128]{1,0:T(8,128)(2,1)}, bf16[512,128]{1,0:T(8,128)(2,1)S(1)}, u32[]{:S(2)}, u32[]{:S(2)}) collective-permute-start(bf16[512,128]{1,0:T(8,128)(2,1)} %get-tuple-element.20), channel_id=1, source_target_pairs={{0,0},{1,2},{2,4},{3,6},{4,8},{5,10},{6,12},{7,14},{8,1},{9,3},{10... | collective-permute-start | bytes 393224 | tf_op jit(solution)/shard_map/ppermute | solution.py:237
  4.6 9.4 %all-to-all-start = ((bf16[16,40,128]{2,1,0:T(8,128)(2,1)}), bf16[16,40,128]{2,1,0:T(8,128)(2,1)S(1)}, u32[]{:S(2)}, u32[]{:S(2)}) async-start(bf16[16,40,128]{2,1,0:T(8,128)(2,1)} %get-tuple-element.16), calls=%async_computation | async-start | bytes 327680 | tf_op jit(solution)/shard_map/all_to_all | solution.py:251
  14.0 0.0 collective-permute-done.both_grad_ref
  14.0 0.1 split_columns.1
  14.1 0.1 collective-permute-start.1
  14.2 1.2 %collective-permute-done.1.refs_1_ = bf16[64,512]{1,0:T(8,128)(2,1)S(1)} collective-permute-done((bf16[64,512]{1,0:T(8,128)(2,1)S(1)}, bf16[64,512]{1,0:T(8,128)(2,1)S(1)}, u32[]{:S(2)}, u32[]{:S(2)}) %collective-permute-start.1) | collective-permute-done | bytes 65568 | tf_op jit(solution)/shard_map/ppermute | solution.py:241
  15.4 0.0 copy-start
  15.4 4.5 %all-to-all-done.got_ref = bf16[16,40,128]{2,1,0:T(8,128)(2,1)S(1)} async-done(((bf16[16,40,128]{2,1,0:T(8,128)(2,1)}), bf16[16,40,128]{2,1,0:T(8,128)(2,1)S(1)}, u32[]{:S(2)}, u32[]{:S(2)}) %all-to-all-start) | async-done | bytes 163872 | tf_op jit(solution)/shard_map/all_to_all | solution.py:251
  19.9 0.3 %adapter_shares.1 = (f32[32,32]{1,0:T(8,128)S(1)}, f32[32,32]{1,0:T(8,128)S(1)}) custom-call(bf16[16,40,128]{2,1,0:T(8,128)(2,1)S(1)} %all-to-all-done.got_ref, bf16[2,64,512]{2,1,0:T(8,128)(2,1)S(1)} %order_pieces.1.pieces_ref), custom_call_target="tpu_custom_call" | custom-call | tf_op jit(solution)/shard_map/adapter_shares/pallas_call | solution.py:253
  20.2 0.6 %collective-permute-start.2 = (f32[32,32]{1,0:T(8,128)S(1)}, f32[32,32]{1,0:T(8,128)S(1)}, u32[]{:S(2)}, u32[]{:S(2)}) collective-permute-start(f32[32,32]{1,0:T(8,128)S(1)} %get-tuple-element.24), channel_id=1, source_target_pairs={{0,17},{1,16},{2,19},{3,18},{4,21},{5,20},{6,23},{7,22},{8,25},{9,... | collective-permute-start | bytes 12296 | tf_op jit(solution)/shard_map/ppermute | solution.py:267
  20.8 0.0 copy-done
  20.8 0.9 %owner_outputs.1 = (bf16[32,1024]{1,0:T(8,128)(2,1)}, bf16[32,1024]{1,0:T(8,128)(2,1)}, f32[32,32]{1,0:T(8,128)}) custom-call(bf16[16,40,128]{2,1,0:T(8,128)(2,1)S(1)} %all-to-all-done.got_ref, bf16[32,1024]{1,0:T(8,128)(2,1)S(1)} %copy-done), custom_call_target="tpu_custom_call" | custom-call | tf_op jit(solution)/shard_map/owner_outputs/pallas_call | solution.py:269
  21.6 1.9 %collective-permute-done.2 = f32[32,32]{1,0:T(8,128)S(1)} collective-permute-done((f32[32,32]{1,0:T(8,128)S(1)}, f32[32,32]{1,0:T(8,128)S(1)}, u32[]{:S(2)}, u32[]{:S(2)}) %collective-permute-start.2) | collective-permute-done | bytes 4128 | tf_op jit(solution)/shard_map/ppermute | solution.py:267
  23.5 0.6 %add.3 = f32[32,32]{1,0:T(8,128)} add(f32[32,32]{1,0:T(8,128)S(1)} %get-tuple-element.23, f32[32,32]{1,0:T(8,128)S(1)} %collective-permute-done.2) | non-fusion elementwise | flops 1024 | bytes 12288 | tf_op jit(solution)/shard_map/add | solution.py:267
  (1 shorter events, 0.0 us)
Async XLA Ops:
  3.0 11.0 %collective-permute-start = (bf16[512,128]{1,0:T(8,128)(2,1)}, bf16[512,128]{1,0:T(8,128)(2,1)S(1)}, u32[]{:S(2)}, u32[]{:S(2)}) collective-permute-start(bf16[512,128]{1,0:T(8,128)(2,1)} %get-tuple-element.20), channel_id=1, source_target_pairs={{0,0},{1,2},{2,4},{3,6},{4,8},{5,10},{6,12},{7,14},{8,1},{9,3},{10... | collective-permute-start | bytes 393224 | tf_op jit(solution)/shard_map/ppermute | solution.py:237
  4.6 15.4 %all-to-all-start = ((bf16[16,40,128]{2,1,0:T(8,128)(2,1)}), bf16[16,40,128]{2,1,0:T(8,128)(2,1)S(1)}, u32[]{:S(2)}, u32[]{:S(2)}) async-start(bf16[16,40,128]{2,1,0:T(8,128)(2,1)} %get-tuple-element.16), calls=%async_computation | async-start | bytes 327680 | tf_op jit(solution)/shard_map/all_to_all | solution.py:251
  14.1 1.3 %collective-permute-start.1 = (bf16[64,512]{1,0:T(8,128)(2,1)S(1)}, bf16[64,512]{1,0:T(8,128)(2,1)S(1)}, u32[]{:S(2)}, u32[]{:S(2)}) collective-permute-start(bf16[64,512]{1,0:T(8,128)(2,1)S(1)} %get-tuple-element.22), channel_id=1, source_target_pairs={{0,1},{1,0},{2,3},{3,2},{4,5},{5,4},{6,7},{7,6},{8,9},{9,8},{10,11... | collective-permute-start | bytes 196616 | tf_op jit(solution)/shard_map/ppermute | solution.py:241
  15.4 5.4 %copy-start = (bf16[32,1024]{1,0:T(8,128)(2,1)S(1)}, bf16[32,1024]{1,0:T(8,128)(2,1)}, u32[]{:S(2)}) copy-start(bf16[32,1024]{1,0:T(8,128)(2,1)} %up_ref.1) | copy-start | bytes 196612
  20.2 3.3 %collective-permute-start.2 = (f32[32,32]{1,0:T(8,128)S(1)}, f32[32,32]{1,0:T(8,128)S(1)}, u32[]{:S(2)}, u32[]{:S(2)}) collective-permute-start(f32[32,32]{1,0:T(8,128)S(1)} %get-tuple-element.24), channel_id=1, source_target_pairs={{0,17},{1,16},{2,19},{3,18},{4,21},{5,20},{6,23},{7,22},{8,25},{9,... | collective-permute-start | bytes 12296 | tf_op jit(solution)/shard_map/ppermute | solution.py:267

commit v7 on v5

--- a/solution.py
+++ b/solution.py
@@ -27,7 +27,7 @@
     assert count == 4 << bits
     turned = [sum(((i >> b) & 1) << (bits - 1 - b) for b in range(bits)) for i in range(quarter)]
     order = []
-    for near, far in ((2, 3), (1, 0)):
+    for near, far in ((3, 2), (0, 1)):
         for i in range(quarter):
             order.append(near * quarter + turned[quarter - 1 - i])
             order.append(far * quarter + turned[(quarter - 1 - i) ^ 1])

time: 23.3 us -> 24.5 us (1.052)
  starting transfers between devices: 12.4 us -> 13 us
  waiting for transfers between devices: 5.8 us -> 6.34 us
    all_to_all x1, starting transfers between devices: 9.39 us -> 10.3 us  [local(): lax.all_to_all(sent, 'mp', 0, 0, axis_index_groups=[group_order(mp)], til...]
    ppermute x1, waiting for transfers between devices: 1.11 us -> 1.43 us  [local(): up_grad = up_grad + lax.ppermute(shares[s], ('dp', 'mp'), route)]
where the time goes in v7:
time: 24.5 us; the launch traced here: 24.3 us
  starting transfers between devices  13 us (53%)
  waiting for transfers between devices  6.34 us (26%)
  Pallas kernels  3.59 us (15%)
  between operations  0.68 us (3%)
  other arithmetic  0.61 us (2%)
    all_to_all x1, starting transfers between devices, local(): lax.all_to_all(sent, 'mp', 0, 0, axis_index_groups=[group_order(mp)], til...  10.3 us
    all_to_all x1, waiting for transfers between devices, local(): lax.all_to_all(sent, 'mp', 0, 0, axis_index_groups=[group_order(mp)], til...  3.73 us
    pallas_call x1, Pallas kernels, local(): pl.pallas_call(attention_kernel, out_shape=[jax.ShapeDtypeStruct((HS, tgt...  2.36 us
    ppermute x1, starting transfers between devices, local(): lax.ppermute(both_grad, 'mp', route)  1.56 us
    ppermute x1, waiting for transfers between devices, local(): up_grad = up_grad + lax.ppermute(shares[s], ('dp', 'mp'), route)  1.43 us
    ppermute x1, waiting for transfers between devices, local(): arrived.append(lax.ppermute(pieces[s], 'mp', route))  1.17 us
    ppermute x1, starting transfers between devices, local(): up_grad = up_grad + lax.ppermute(shares[s], ('dp', 'mp'), route)  1.04 us
    pallas_call x1, Pallas kernels, local(): pl.pallas_call(owner_kernel, out_shape=[jax.ShapeDtypeStruct((rows, width...  0.85 us
  transfers between devices with their start and end apart: 4, of which 3 were waited for; matrix products, arithmetic and copies ran while one was open for 0% of the time, Pallas kernels for 4%

profile of v7, /device:TPU:0, one launch (start us, length us, event | category | flops | bytes accessed | tf_op | source)
XLA Modules:
  0.0 24.3 jit_solution(10367049028309309537)
XLA Ops:
  0.6 2.4 %attention_backward.1 = (bf16[64,256]{1,0:T(8,128)(2,1)}, bf16[16,40,128]{2,1,0:T(8,128)(2,1)}, bf16[512,128]{1,0:T(8,128)(2,1)}) custom-call(s32[1,8]{1,0:T(1,128)} %source_any.1, s32[1,8]{1,0:T(1,128)} %target_any.1, bf16[64,256]{1,0:T(8,128)(2,1)} %bitcast.3, bf16[64,256]{1,0:T(8,128)(2,1)} %bitcast.4, bf16[512,128]{1,0:T(8,128)(2,1)} %kv_any.1, ...), custom_call_target="tpu_custom_call" | custom-call | tf_op jit(solution)/shard_map/attention_backward/pallas_call | solution.py:206
  3.0 1.6 %collective-permute-start = (bf16[512,128]{1,0:T(8,128)(2,1)}, bf16[512,128]{1,0:T(8,128)(2,1)S(1)}, u32[]{:S(2)}, u32[]{:S(2)}) collective-permute-start(bf16[512,128]{1,0:T(8,128)(2,1)} %get-tuple-element.20), channel_id=1, source_target_pairs={{0,0},{1,2},{2,4},{3,6},{4,8},{5,10},{6,12},{7,14},{8,1},{9,3},{10... | collective-permute-start | bytes 393224 | tf_op jit(solution)/shard_map/ppermute | solution.py:237
  4.6 10.3 %all-to-all-start = ((bf16[16,40,128]{2,1,0:T(8,128)(2,1)}), bf16[16,40,128]{2,1,0:T(8,128)(2,1)S(1)}, u32[]{:S(2)}, u32[]{:S(2)}) async-start(bf16[16,40,128]{2,1,0:T(8,128)(2,1)} %get-tuple-element.16), calls=%async_computation | async-start | bytes 327680 | tf_op jit(solution)/shard_map/all_to_all | solution.py:251
  14.9 0.0 collective-permute-done.both_grad_ref
  14.9 0.1 split_columns.1
  15.0 0.1 collective-permute-start.1
  15.1 1.2 %collective-permute-done.1.refs_1_ = bf16[64,512]{1,0:T(8,128)(2,1)S(1)} collective-permute-done((bf16[64,512]{1,0:T(8,128)(2,1)S(1)}, bf16[64,512]{1,0:T(8,128)(2,1)S(1)}, u32[]{:S(2)}, u32[]{:S(2)}) %collective-permute-start.1) | collective-permute-done | bytes 65568 | tf_op jit(solution)/shard_map/ppermute | solution.py:241
  16.3 0.0 copy-start
  16.3 3.7 %all-to-all-done.got_ref = bf16[16,40,128]{2,1,0:T(8,128)(2,1)S(1)} async-done(((bf16[16,40,128]{2,1,0:T(8,128)(2,1)}), bf16[16,40,128]{2,1,0:T(8,128)(2,1)S(1)}, u32[]{:S(2)}, u32[]{:S(2)}) %all-to-all-start) | async-done | bytes 163872 | tf_op jit(solution)/shard_map/all_to_all | solution.py:251
  20.1 0.3 %adapter_shares.1 = (f32[32,32]{1,0:T(8,128)S(1)}, f32[32,32]{1,0:T(8,128)S(1)}) custom-call(bf16[16,40,128]{2,1,0:T(8,128)(2,1)S(1)} %all-to-all-done.got_ref, bf16[2,64,512]{2,1,0:T(8,128)(2,1)S(1)} %order_pieces.1.pieces_ref), custom_call_target="tpu_custom_call" | custom-call | tf_op jit(solution)/shard_map/adapter_shares/pallas_call | solution.py:253
  20.3 1.0 %collective-permute-start.2 = (f32[32,32]{1,0:T(8,128)S(1)}, f32[32,32]{1,0:T(8,128)S(1)}, u32[]{:S(2)}, u32[]{:S(2)}) collective-permute-start(f32[32,32]{1,0:T(8,128)S(1)} %get-tuple-element.24), channel_id=1, source_target_pairs={{0,17},{1,16},{2,19},{3,18},{4,21},{5,20},{6,23},{7,22},{8,25},{9,... | collective-permute-start | bytes 12296 | tf_op jit(solution)/shard_map/ppermute | solution.py:267
  21.4 0.0 copy-done
  21.4 0.9 %owner_outputs.1 = (bf16[32,1024]{1,0:T(8,128)(2,1)}, bf16[32,1024]{1,0:T(8,128)(2,1)}, f32[32,32]{1,0:T(8,128)}) custom-call(bf16[16,40,128]{2,1,0:T(8,128)(2,1)S(1)} %all-to-all-done.got_ref, bf16[32,1024]{1,0:T(8,128)(2,1)S(1)} %copy-done), custom_call_target="tpu_custom_call" | custom-call | tf_op jit(solution)/shard_map/owner_outputs/pallas_call | solution.py:269
  22.2 1.4 %collective-permute-done.2 = f32[32,32]{1,0:T(8,128)S(1)} collective-permute-done((f32[32,32]{1,0:T(8,128)S(1)}, f32[32,32]{1,0:T(8,128)S(1)}, u32[]{:S(2)}, u32[]{:S(2)}) %collective-permute-start.2) | collective-permute-done | bytes 4128 | tf_op jit(solution)/shard_map/ppermute | solution.py:267
  23.6 0.6 %add.3 = f32[32,32]{1,0:T(8,128)} add(f32[32,32]{1,0:T(8,128)S(1)} %get-tuple-element.23, f32[32,32]{1,0:T(8,128)S(1)} %collective-permute-done.2) | non-fusion elementwise | flops 1024 | bytes 12288 | tf_op jit(solution)/shard_map/add | solution.py:267
  (1 shorter events, 0.0 us)
Async XLA Ops:
  3.0 11.9 %collective-permute-start = (bf16[512,128]{1,0:T(8,128)(2,1)}, bf16[512,128]{1,0:T(8,128)(2,1)S(1)}, u32[]{:S(2)}, u32[]{:S(2)}) collective-permute-start(bf16[512,128]{1,0:T(8,128)(2,1)} %get-tuple-element.20), channel_id=1, source_target_pairs={{0,0},{1,2},{2,4},{3,6},{4,8},{5,10},{6,12},{7,14},{8,1},{9,3},{10... | collective-permute-start | bytes 393224 | tf_op jit(solution)/shard_map/ppermute | solution.py:237
  4.6 15.5 %all-to-all-start = ((bf16[16,40,128]{2,1,0:T(8,128)(2,1)}), bf16[16,40,128]{2,1,0:T(8,128)(2,1)S(1)}, u32[]{:S(2)}, u32[]{:S(2)}) async-start(bf16[16,40,128]{2,1,0:T(8,128)(2,1)} %get-tuple-element.16), calls=%async_computation | async-start | bytes 327680 | tf_op jit(solution)/shard_map/all_to_all | solution.py:251
  15.0 1.3 %collective-permute-start.1 = (bf16[64,512]{1,0:T(8,128)(2,1)S(1)}, bf16[64,512]{1,0:T(8,128)(2,1)S(1)}, u32[]{:S(2)}, u32[]{:S(2)}) collective-permute-start(bf16[64,512]{1,0:T(8,128)(2,1)S(1)} %get-tuple-element.22), channel_id=1, source_target_pairs={{0,1},{1,0},{2,3},{3,2},{4,5},{5,4},{6,7},{7,6},{8,9},{9,8},{10,11... | collective-permute-start | bytes 196616 | tf_op jit(solution)/shard_map/ppermute | solution.py:241
  16.3 5.1 %copy-start = (bf16[32,1024]{1,0:T(8,128)(2,1)S(1)}, bf16[32,1024]{1,0:T(8,128)(2,1)}, u32[]{:S(2)}) copy-start(bf16[32,1024]{1,0:T(8,128)(2,1)} %up_ref.1) | copy-start | bytes 196612
  20.3 3.3 %collective-permute-start.2 = (f32[32,32]{1,0:T(8,128)S(1)}, f32[32,32]{1,0:T(8,128)S(1)}, u32[]{:S(2)}, u32[]{:S(2)}) collective-permute-start(f32[32,32]{1,0:T(8,128)S(1)} %get-tuple-element.24), channel_id=1, source_target_pairs={{0,17},{1,16},{2,19},{3,18},{4,21},{5,20},{6,23},{7,22},{8,25},{9,... | collective-permute-start | bytes 12296 | tf_op jit(solution)/shard_map/ppermute | solution.py:267

commit v8 on v5

--- a/solution.py
+++ b/solution.py
@@ -123,10 +123,9 @@
     for j in range(dp):
         halves = [turned[j * step:(j + 1) * step], turned[HS + j * step:HS + (j + 1) * step]]
         pieces.append(jnp.concatenate(halves, axis=0))
-    e = lax.rem(lax.axis_index("mp"), dp)
     pack = lax.axis_index("dp")
     for s, out_ref in enumerate(out_refs):
-        turn = lax.rem(2 * e + s + dp - pack, dp)
+        turn = lax.rem(2 * dp - 1 + s - pack, dp)
         chosen = pieces[0]
         for j in range(1, dp):
             chosen = jnp.where(turn == j, pieces[j], chosen)
@@ -138,7 +137,7 @@
     dp = len(arrived_refs)
     mine = lax.rem(lax.axis_index("mp"), dp)
     for s, arrived_ref in enumerate(arrived_refs):
-        out_ref[lax.rem(mine + dp - s, dp)] = arrived_ref[...]
+        out_ref[dp - 1 - lax.rem(mine + dp - s, dp)] = arrived_ref[...]
 
 
 def share_kernel(rows, both_rank, got_ref, pieces_ref, *out_refs):
@@ -225,7 +224,7 @@
         name="attention_backward",
     )(source_lengths, target_lengths, query_t, grad_t, kv_cache, low_rank)
 
-    route = [(h, h * dp % mp + h * dp // mp) for h in range(mp)]
+    route = [(h, h * dp % mp + dp - 1 - h * dp // mp) for h in range(mp)]
     pieces = pl.pallas_call(
         functools.partial(split_kernel, rows),
         out_shape=[jax.ShapeDtypeStruct((2 * step, src_count), jnp.bfloat16)] * dp,

time: 23.3 us -> 21.1 us (0.906)
  starting transfers between devices: 12.4 us -> 10.1 us
    all_to_all x1, starting transfers between devices: 9.39 us -> 8.2 us  [local(): lax.all_to_all(sent, 'mp', 0, 0, axis_index_groups=[group_order(mp)], til...]
    ppermute x1, starting transfers between devices: 1.56 us -> 0.52 us  [local(): lax.ppermute(both_grad, 'mp', route)]
  transfers between devices with their start and end apart: 4 -> 4, of which waited for: 3 -> 3; matrix products, arithmetic and copies ran while one was open for 0% -> 0% of each run, Pallas kernels for 4% -> 5%
where the time goes in v8:
time: 21.1 us; the launch traced here: 20.8 us
  starting transfers between devices  10.1 us (48%)
  waiting for transfers between devices  5.81 us (28%)
  Pallas kernels  3.6 us (17%)
  between operations  0.68 us (3%)
  other arithmetic  0.61 us (3%)
    all_to_all x1, starting transfers between devices, local(): lax.all_to_all(sent, 'mp', 0, 0, axis_index_groups=[group_order(mp)], til...  8.2 us
    all_to_all x1, waiting for transfers between devices, local(): lax.all_to_all(sent, 'mp', 0, 0, axis_index_groups=[group_order(mp)], til...  3.51 us
    pallas_call x1, Pallas kernels, local(): pl.pallas_call(attention_kernel, out_shape=[jax.ShapeDtypeStruct((HS, tgt...  2.36 us
    ppermute x1, starting transfers between devices, local(): up_grad = up_grad + lax.ppermute(shares[s], ('dp', 'mp'), route)  1.25 us
    ppermute x1, waiting for transfers between devices, local(): arrived.append(lax.ppermute(pieces[s], 'mp', route))  1.17 us
    ppermute x1, waiting for transfers between devices, local(): up_grad = up_grad + lax.ppermute(shares[s], ('dp', 'mp'), route)  1.12 us
    pallas_call x1, Pallas kernels, local(): pl.pallas_call(owner_kernel, out_shape=[jax.ShapeDtypeStruct((rows, width...  0.86 us
    add x1, other arithmetic, local(): up_grad = up_grad + lax.ppermute(shares[s], ('dp', 'mp'), route)  0.61 us
  transfers between devices with their start and end apart: 4, of which 3 were waited for; matrix products, arithmetic and copies ran while one was open for 0% of the time, Pallas kernels for 5%

profile of v8, /device:TPU:0, one launch (start us, length us, event | category | flops | bytes accessed | tf_op | source)
XLA Modules:
  0.0 20.8 jit_solution(7236444081897122360)
XLA Ops:
  0.6 2.4 %attention_backward.1 = (bf16[64,256]{1,0:T(8,128)(2,1)}, bf16[16,40,128]{2,1,0:T(8,128)(2,1)}, bf16[512,128]{1,0:T(8,128)(2,1)}) custom-call(s32[1,8]{1,0:T(1,128)} %source_any.1, s32[1,8]{1,0:T(1,128)} %target_any.1, bf16[64,256]{1,0:T(8,128)(2,1)} %bitcast.3, bf16[64,256]{1,0:T(8,128)(2,1)} %bitcast.4, bf16[512,128]{1,0:T(8,128)(2,1)} %kv_any.1, ...), custom_call_target="tpu_custom_call" | custom-call | tf_op jit(solution)/shard_map/attention_backward/pallas_call | solution.py:205
  3.0 0.5 %collective-permute-start = (bf16[512,128]{1,0:T(8,128)(2,1)}, bf16[512,128]{1,0:T(8,128)(2,1)S(1)}, u32[]{:S(2)}, u32[]{:S(2)}) collective-permute-start(bf16[512,128]{1,0:T(8,128)(2,1)} %get-tuple-element.20), channel_id=1, source_target_pairs={{0,1},{1,3},{2,5},{3,7},{4,9},{5,11},{6,13},{7,15},{8,0},{9,2},{10... | collective-permute-start | bytes 393224 | tf_op jit(solution)/shard_map/ppermute | solution.py:236
  3.5 8.2 %all-to-all-start = ((bf16[16,40,128]{2,1,0:T(8,128)(2,1)}), bf16[16,40,128]{2,1,0:T(8,128)(2,1)S(1)}, u32[]{:S(2)}, u32[]{:S(2)}) async-start(bf16[16,40,128]{2,1,0:T(8,128)(2,1)} %get-tuple-element.16), calls=%async_computation | async-start | bytes 327680 | tf_op jit(solution)/shard_map/all_to_all | solution.py:250
  11.7 0.0 collective-permute-done.both_grad_ref
  11.7 0.1 split_columns.1
  11.8 0.1 collective-permute-start.1
  12.0 1.2 %collective-permute-done.1.refs_1_ = bf16[64,512]{1,0:T(8,128)(2,1)S(1)} collective-permute-done((bf16[64,512]{1,0:T(8,128)(2,1)S(1)}, bf16[64,512]{1,0:T(8,128)(2,1)S(1)}, u32[]{:S(2)}, u32[]{:S(2)}) %collective-permute-start.1) | collective-permute-done | bytes 65568 | tf_op jit(solution)/shard_map/ppermute | solution.py:240
  13.2 0.0 copy-start
  13.2 3.5 %all-to-all-done.got_ref = bf16[16,40,128]{2,1,0:T(8,128)(2,1)S(1)} async-done(((bf16[16,40,128]{2,1,0:T(8,128)(2,1)}), bf16[16,40,128]{2,1,0:T(8,128)(2,1)S(1)}, u32[]{:S(2)}, u32[]{:S(2)}) %all-to-all-start) | async-done | bytes 163872 | tf_op jit(solution)/shard_map/all_to_all | solution.py:250
  16.7 0.3 %adapter_shares.1 = (f32[32,32]{1,0:T(8,128)S(1)}, f32[32,32]{1,0:T(8,128)S(1)}) custom-call(bf16[16,40,128]{2,1,0:T(8,128)(2,1)S(1)} %all-to-all-done.got_ref, bf16[2,64,512]{2,1,0:T(8,128)(2,1)S(1)} %order_pieces.1.pieces_ref), custom_call_target="tpu_custom_call" | custom-call | tf_op jit(solution)/shard_map/adapter_shares/pallas_call | solution.py:252
  17.0 1.2 %collective-permute-start.2 = (f32[32,32]{1,0:T(8,128)S(1)}, f32[32,32]{1,0:T(8,128)S(1)}, u32[]{:S(2)}, u32[]{:S(2)}) collective-permute-start(f32[32,32]{1,0:T(8,128)S(1)} %get-tuple-element.24), channel_id=1, source_target_pairs={{0,17},{1,16},{2,19},{3,18},{4,21},{5,20},{6,23},{7,22},{8,25},{9,... | collective-permute-start | bytes 12296 | tf_op jit(solution)/shard_map/ppermute | solution.py:266
  18.2 0.0 copy-done
  18.2 0.9 %owner_outputs.1 = (bf16[32,1024]{1,0:T(8,128)(2,1)}, bf16[32,1024]{1,0:T(8,128)(2,1)}, f32[32,32]{1,0:T(8,128)}) custom-call(bf16[16,40,128]{2,1,0:T(8,128)(2,1)S(1)} %all-to-all-done.got_ref, bf16[32,1024]{1,0:T(8,128)(2,1)S(1)} %copy-done), custom_call_target="tpu_custom_call" | custom-call | tf_op jit(solution)/shard_map/owner_outputs/pallas_call | solution.py:268
  19.1 1.1 %collective-permute-done.2 = f32[32,32]{1,0:T(8,128)S(1)} collective-permute-done((f32[32,32]{1,0:T(8,128)S(1)}, f32[32,32]{1,0:T(8,128)S(1)}, u32[]{:S(2)}, u32[]{:S(2)}) %collective-permute-start.2) | collective-permute-done | bytes 4128 | tf_op jit(solution)/shard_map/ppermute | solution.py:266
  20.2 0.6 %add.3 = f32[32,32]{1,0:T(8,128)} add(f32[32,32]{1,0:T(8,128)S(1)} %get-tuple-element.23, f32[32,32]{1,0:T(8,128)S(1)} %collective-permute-done.2) | non-fusion elementwise | flops 1024 | bytes 12288 | tf_op jit(solution)/shard_map/add | solution.py:266
  (1 shorter events, 0.0 us)
Async XLA Ops:
  3.0 8.7 %collective-permute-start = (bf16[512,128]{1,0:T(8,128)(2,1)}, bf16[512,128]{1,0:T(8,128)(2,1)S(1)}, u32[]{:S(2)}, u32[]{:S(2)}) collective-permute-start(bf16[512,128]{1,0:T(8,128)(2,1)} %get-tuple-element.20), channel_id=1, source_target_pairs={{0,1},{1,3},{2,5},{3,7},{4,9},{5,11},{6,13},{7,15},{8,0},{9,2},{10... | collective-permute-start | bytes 393224 | tf_op jit(solution)/shard_map/ppermute | solution.py:236
  3.5 13.2 %all-to-all-start = ((bf16[16,40,128]{2,1,0:T(8,128)(2,1)}), bf16[16,40,128]{2,1,0:T(8,128)(2,1)S(1)}, u32[]{:S(2)}, u32[]{:S(2)}) async-start(bf16[16,40,128]{2,1,0:T(8,128)(2,1)} %get-tuple-element.16), calls=%async_computation | async-start | bytes 327680 | tf_op jit(solution)/shard_map/all_to_all | solution.py:250
  11.8 1.3 %collective-permute-start.1 = (bf16[64,512]{1,0:T(8,128)(2,1)S(1)}, bf16[64,512]{1,0:T(8,128)(2,1)S(1)}, u32[]{:S(2)}, u32[]{:S(2)}) collective-permute-start(bf16[64,512]{1,0:T(8,128)(2,1)S(1)} %get-tuple-element.22), channel_id=1, source_target_pairs={{0,1},{1,0},{2,3},{3,2},{4,5},{5,4},{6,7},{7,6},{8,9},{9,8},{10,11... | collective-permute-start | bytes 196616 | tf_op jit(solution)/shard_map/ppermute | solution.py:240
  13.2 5.0 %copy-start = (bf16[32,1024]{1,0:T(8,128)(2,1)S(1)}, bf16[32,1024]{1,0:T(8,128)(2,1)}, u32[]{:S(2)}) copy-start(bf16[32,1024]{1,0:T(8,128)(2,1)} %up_ref.1) | copy-start | bytes 196612
  17.0 3.2 %collective-permute-start.2 = (f32[32,32]{1,0:T(8,128)S(1)}, f32[32,32]{1,0:T(8,128)S(1)}, u32[]{:S(2)}, u32[]{:S(2)}) collective-permute-start(f32[32,32]{1,0:T(8,128)S(1)} %get-tuple-element.24), channel_id=1, source_target_pairs={{0,17},{1,16},{2,19},{3,18},{4,21},{5,20},{6,23},{7,22},{8,25},{9,... | collective-permute-start | bytes 12296 | tf_op jit(solution)/shard_map/ppermute | solution.py:266

commit v9 on v8

--- a/solution.py
+++ b/solution.py
@@ -73,13 +73,13 @@
     query_wide = jnp.concatenate([query_t, blank], axis=0)
     grad_wide = jnp.concatenate([blank, grad_t], axis=0)
     first, last = source_range(source_ref, target_ref, tgt_count)
-    half = both.shape[0] // 2
-    parts = [both[:half], both[half:]]
+    height = both.shape[0] // 4
+    parts = [both[at:at + height] for at in range(0, both.shape[0], height)]
     scores = [jnp.dot(part, query_wide, preferred_element_type=jnp.float32) for part in parts]
     dprobs = [jnp.dot(part, grad_wide, preferred_element_type=jnp.float32) for part in parts]
     expos = []
     for i, score in enumerate(scores):
-        position = i * half + lax.broadcasted_iota(jnp.int32, score.shape, 0)
+        position = i * height + lax.broadcasted_iota(jnp.int32, score.shape, 0)
         allowed = jnp.logical_and(position >= first, position < last)
         expos.append(jnp.where(allowed, jnp.exp(score), 0.0))
     inverse = 1.0 / sum(jnp.sum(expo, axis=0, keepdims=True) for expo in expos)

time: 21.1 us -> 21.1 us (level)
  no operation moved by 1% of the time
where the time goes in v9:
time: 21.1 us; the launch traced here: 20.9 us
  starting transfers between devices  10.1 us (48%)
  waiting for transfers between devices  5.81 us (28%)
  Pallas kernels  3.65 us (17%)
  between operations  0.68 us (3%)
  other arithmetic  0.61 us (3%)
    all_to_all x1, starting transfers between devices, local(): lax.all_to_all(sent, 'mp', 0, 0, axis_index_groups=[group_order(mp)], til...  8.2 us
    all_to_all x1, waiting for transfers between devices, local(): lax.all_to_all(sent, 'mp', 0, 0, axis_index_groups=[group_order(mp)], til...  3.51 us
    pallas_call x1, Pallas kernels, local(): pl.pallas_call(attention_kernel, out_shape=[jax.ShapeDtypeStruct((HS, tgt...  2.41 us
    ppermute x1, starting transfers between devices, local(): up_grad = up_grad + lax.ppermute(shares[s], ('dp', 'mp'), route)  1.25 us
    ppermute x1, waiting for transfers between devices, local(): arrived.append(lax.ppermute(pieces[s], 'mp', route))  1.17 us
    ppermute x1, waiting for transfers between devices, local(): up_grad = up_grad + lax.ppermute(shares[s], ('dp', 'mp'), route)  1.12 us
    pallas_call x1, Pallas kernels, local(): pl.pallas_call(owner_kernel, out_shape=[jax.ShapeDtypeStruct((rows, width...  0.86 us
    add x1, other arithmetic, local(): up_grad = up_grad + lax.ppermute(shares[s], ('dp', 'mp'), route)  0.61 us
  transfers between devices with their start and end apart: 4, of which 3 were waited for; matrix products, arithmetic and copies ran while one was open for 0% of the time, Pallas kernels for 5%

profile of v9, /device:TPU:0, one launch (start us, length us, event | category | flops | bytes accessed | tf_op | source)
XLA Modules:
  0.0 20.9 jit_solution(5430005050351325002)
XLA Ops:
  0.6 2.4 %attention_backward.1 = (bf16[64,256]{1,0:T(8,128)(2,1)}, bf16[16,40,128]{2,1,0:T(8,128)(2,1)}, bf16[512,128]{1,0:T(8,128)(2,1)}) custom-call(s32[1,8]{1,0:T(1,128)} %source_any.1, s32[1,8]{1,0:T(1,128)} %target_any.1, bf16[64,256]{1,0:T(8,128)(2,1)} %bitcast.3, bf16[64,256]{1,0:T(8,128)(2,1)} %bitcast.4, bf16[512,128]{1,0:T(8,128)(2,1)} %kv_any.1, ...), custom_call_target="tpu_custom_call" | custom-call | tf_op jit(solution)/shard_map/attention_backward/pallas_call | solution.py:205
  3.1 0.5 %collective-permute-start = (bf16[512,128]{1,0:T(8,128)(2,1)}, bf16[512,128]{1,0:T(8,128)(2,1)S(1)}, u32[]{:S(2)}, u32[]{:S(2)}) collective-permute-start(bf16[512,128]{1,0:T(8,128)(2,1)} %get-tuple-element.20), channel_id=1, source_target_pairs={{0,1},{1,3},{2,5},{3,7},{4,9},{5,11},{6,13},{7,15},{8,0},{9,2},{10... | collective-permute-start | bytes 393224 | tf_op jit(solution)/shard_map/ppermute | solution.py:236
  3.6 8.2 %all-to-all-start = ((bf16[16,40,128]{2,1,0:T(8,128)(2,1)}), bf16[16,40,128]{2,1,0:T(8,128)(2,1)S(1)}, u32[]{:S(2)}, u32[]{:S(2)}) async-start(bf16[16,40,128]{2,1,0:T(8,128)(2,1)} %get-tuple-element.16), calls=%async_computation | async-start | bytes 327680 | tf_op jit(solution)/shard_map/all_to_all | solution.py:250
  11.8 0.0 collective-permute-done.both_grad_ref
  11.8 0.1 split_columns.1
  11.9 0.1 collective-permute-start.1
  12.0 1.2 %collective-permute-done.1.refs_1_ = bf16[64,512]{1,0:T(8,128)(2,1)S(1)} collective-permute-done((bf16[64,512]{1,0:T(8,128)(2,1)S(1)}, bf16[64,512]{1,0:T(8,128)(2,1)S(1)}, u32[]{:S(2)}, u32[]{:S(2)}) %collective-permute-start.1) | collective-permute-done | bytes 65568 | tf_op jit(solution)/shard_map/ppermute | solution.py:240
  13.2 0.0 copy-start
  13.2 3.5 %all-to-all-done.got_ref = bf16[16,40,128]{2,1,0:T(8,128)(2,1)S(1)} async-done(((bf16[16,40,128]{2,1,0:T(8,128)(2,1)}), bf16[16,40,128]{2,1,0:T(8,128)(2,1)S(1)}, u32[]{:S(2)}, u32[]{:S(2)}) %all-to-all-start) | async-done | bytes 163872 | tf_op jit(solution)/shard_map/all_to_all | solution.py:250
  16.8 0.3 %adapter_shares.1 = (f32[32,32]{1,0:T(8,128)S(1)}, f32[32,32]{1,0:T(8,128)S(1)}) custom-call(bf16[16,40,128]{2,1,0:T(8,128)(2,1)S(1)} %all-to-all-done.got_ref, bf16[2,64,512]{2,1,0:T(8,128)(2,1)S(1)} %order_pieces.1.pieces_ref), custom_call_target="tpu_custom_call" | custom-call | tf_op jit(solution)/shard_map/adapter_shares/pallas_call | solution.py:252
  17.0 1.2 %collective-permute-start.2 = (f32[32,32]{1,0:T(8,128)S(1)}, f32[32,32]{1,0:T(8,128)S(1)}, u32[]{:S(2)}, u32[]{:S(2)}) collective-permute-start(f32[32,32]{1,0:T(8,128)S(1)} %get-tuple-element.24), channel_id=1, source_target_pairs={{0,17},{1,16},{2,19},{3,18},{4,21},{5,20},{6,23},{7,22},{8,25},{9,... | collective-permute-start | bytes 12296 | tf_op jit(solution)/shard_map/ppermute | solution.py:266
  18.3 0.0 copy-done
  18.3 0.9 %owner_outputs.1 = (bf16[32,1024]{1,0:T(8,128)(2,1)}, bf16[32,1024]{1,0:T(8,128)(2,1)}, f32[32,32]{1,0:T(8,128)}) custom-call(bf16[16,40,128]{2,1,0:T(8,128)(2,1)S(1)} %all-to-all-done.got_ref, bf16[32,1024]{1,0:T(8,128)(2,1)S(1)} %copy-done), custom_call_target="tpu_custom_call" | custom-call | tf_op jit(solution)/shard_map/owner_outputs/pallas_call | solution.py:268
  19.1 1.1 %collective-permute-done.2 = f32[32,32]{1,0:T(8,128)S(1)} collective-permute-done((f32[32,32]{1,0:T(8,128)S(1)}, f32[32,32]{1,0:T(8,128)S(1)}, u32[]{:S(2)}, u32[]{:S(2)}) %collective-permute-start.2) | collective-permute-done | bytes 4128 | tf_op jit(solution)/shard_map/ppermute | solution.py:266
  20.2 0.6 %add.3 = f32[32,32]{1,0:T(8,128)} add(f32[32,32]{1,0:T(8,128)S(1)} %get-tuple-element.23, f32[32,32]{1,0:T(8,128)S(1)} %collective-permute-done.2) | non-fusion elementwise | flops 1024 | bytes 12288 | tf_op jit(solution)/shard_map/add | solution.py:266
  (1 shorter events, 0.0 us)
Async XLA Ops:
  3.1 8.7 %collective-permute-start = (bf16[512,128]{1,0:T(8,128)(2,1)}, bf16[512,128]{1,0:T(8,128)(2,1)S(1)}, u32[]{:S(2)}, u32[]{:S(2)}) collective-permute-start(bf16[512,128]{1,0:T(8,128)(2,1)} %get-tuple-element.20), channel_id=1, source_target_pairs={{0,1},{1,3},{2,5},{3,7},{4,9},{5,11},{6,13},{7,15},{8,0},{9,2},{10... | collective-permute-start | bytes 393224 | tf_op jit(solution)/shard_map/ppermute | solution.py:236
  3.6 13.2 %all-to-all-start = ((bf16[16,40,128]{2,1,0:T(8,128)(2,1)}), bf16[16,40,128]{2,1,0:T(8,128)(2,1)S(1)}, u32[]{:S(2)}, u32[]{:S(2)}) async-start(bf16[16,40,128]{2,1,0:T(8,128)(2,1)} %get-tuple-element.16), calls=%async_computation | async-start | bytes 327680 | tf_op jit(solution)/shard_map/all_to_all | solution.py:250
  11.9 1.3 %collective-permute-start.1 = (bf16[64,512]{1,0:T(8,128)(2,1)S(1)}, bf16[64,512]{1,0:T(8,128)(2,1)S(1)}, u32[]{:S(2)}, u32[]{:S(2)}) collective-permute-start(bf16[64,512]{1,0:T(8,128)(2,1)S(1)} %get-tuple-element.22), channel_id=1, source_target_pairs={{0,1},{1,0},{2,3},{3,2},{4,5},{5,4},{6,7},{7,6},{8,9},{9,8},{10,11... | collective-permute-start | bytes 196616 | tf_op jit(solution)/shard_map/ppermute | solution.py:240
  13.2 5.0 %copy-start = (bf16[32,1024]{1,0:T(8,128)(2,1)S(1)}, bf16[32,1024]{1,0:T(8,128)(2,1)}, u32[]{:S(2)}) copy-start(bf16[32,1024]{1,0:T(8,128)(2,1)} %up_ref.1) | copy-start | bytes 196612
  17.0 3.2 %collective-permute-start.2 = (f32[32,32]{1,0:T(8,128)S(1)}, f32[32,32]{1,0:T(8,128)S(1)}, u32[]{:S(2)}, u32[]{:S(2)}) collective-permute-start(f32[32,32]{1,0:T(8,128)S(1)} %get-tuple-element.24), channel_id=1, source_target_pairs={{0,17},{1,16},{2,19},{3,18},{4,21},{5,20},{6,23},{7,22},{8,25},{9,... | collective-permute-start | bytes 12296 | tf_op jit(solution)/shard_map/ppermute | solution.py:266

commit v10 on v8

--- a/solution.py
+++ b/solution.py
@@ -51,9 +51,9 @@
 
 
 def attention_kernel(
-    source_any, target_any, query_any, grad_any, kv_any, low_any, query_grad_ref, sent_ref, both_grad_ref,
-    source_ref, target_ref, query_ref, grad_ref, kv_ref, low_ref, sems,
+    source_any, target_any, query_any, grad_any, kv_any, low_any, query_grad_ref, sent_ref, *refs
 ):
+    *piece_refs, source_ref, target_ref, query_ref, grad_ref, kv_ref, low_ref, pieces, sems = refs
     pairs = [
         (kv_any, kv_ref), (query_any, query_ref), (grad_any, grad_ref),
         (source_any, source_ref), (target_any, target_ref), (low_any, low_ref),
@@ -105,39 +105,34 @@
         sent_ref[at, :rows, :] = both_low[block * rows:(block + 1) * rows]
         sent_ref[at, rows:, :] = packed
 
-    both_grad_ref[...] = both_low
+    exact = both_low.astype(jnp.float32)
+    ordered = [
+        exact[block + start:block + start + CUT]
+        for start in range(0, rows, CUT) for block in range(0, exact.shape[0], rows)
+    ]
+    turned = jnp.concatenate(ordered, axis=0).T.astype(jnp.bfloat16)
+    dp = len(piece_refs)
+    step = HS // dp
+    for j in range(dp):
+        halves = [turned[j * step:(j + 1) * step], turned[HS + j * step:HS + (j + 1) * step]]
+        pieces[j] = jnp.concatenate(halves, axis=0)
+    e = lax.axis_index("mp") // (blocks // dp)
+    pack = lax.axis_index("dp")
+    for s, piece_ref in enumerate(piece_refs):
+        piece_ref[...] = pieces[lax.rem(2 * e + s + dp - pack, dp)]
     query_grad = sum(dot(part, dscore, TN) for part, dscore in zip(parts, dscores))
     query_grad_ref[...] = query_grad[:HS].astype(jnp.bfloat16)
 
 
-def split_kernel(rows, both_grad_ref, *out_refs):
-    dp = len(out_refs)
-    step = HS // dp
-    exact = both_grad_ref[...].astype(jnp.float32)
-    parts = []
-    for start in range(0, rows, CUT):
-        for block in range(0, exact.shape[0], rows):
-            parts.append(exact[block + start:block + start + CUT])
-    turned = jnp.concatenate(parts, axis=0).T
-    pieces = []
-    for j in range(dp):
-        halves = [turned[j * step:(j + 1) * step], turned[HS + j * step:HS + (j + 1) * step]]
-        pieces.append(jnp.concatenate(halves, axis=0))
-    pack = lax.axis_index("dp")
-    for s, out_ref in enumerate(out_refs):
-        turn = lax.rem(2 * dp - 1 + s - pack, dp)
-        chosen = pieces[0]
-        for j in range(1, dp):
-            chosen = jnp.where(turn == j, pieces[j], chosen)
-        out_ref[...] = chosen.astype(jnp.bfloat16)
-
-
-def order_kernel(*refs):
-    *arrived_refs, out_ref = refs
-    dp = len(arrived_refs)
-    mine = lax.rem(lax.axis_index("mp"), dp)
-    for s, arrived_ref in enumerate(arrived_refs):
-        out_ref[dp - 1 - lax.rem(mine + dp - s, dp)] = arrived_ref[...]
+def order_kernel(mp, *refs):
+    out_ref = refs[-1]
+    dp = (len(refs) - 1) // 2
+    me = lax.axis_index("mp")
+    place = lax.rem(me, dp)
+    for s in range(dp):
+        e = lax.rem(place + dp - s, dp)
+        source = (e * mp + me - place) // dp
+        out_ref[e] = jnp.where(source == me, refs[dp + s][...], refs[s][...])
 
 
 def share_kernel(rows, both_rank, got_ref, pieces_ref, *out_refs):
@@ -202,15 +197,14 @@
 
     query_t = query.T
     grad_t = out_grad.T
-    query_grad_t, sent, both_grad = pl.pallas_call(
+    query_grad_t, sent, *pieces = pl.pallas_call(
         attention_kernel,
         out_shape=[
             jax.ShapeDtypeStruct((HS, tgt_count), jnp.bfloat16),
             jax.ShapeDtypeStruct((mp, rows + CUT, LANES), jnp.bfloat16),
-            jax.ShapeDtypeStruct((src_count, 2 * HS), jnp.bfloat16),
-        ],
+        ] + [jax.ShapeDtypeStruct((2 * step, src_count), jnp.bfloat16)] * dp,
         in_specs=[hbm] * 6,
-        out_specs=[vmem] * 3,
+        out_specs=[vmem] * (2 + dp),
         scratch_shapes=[
             pltpu.SMEM(source_lengths.shape, jnp.int32),
             pltpu.SMEM(target_lengths.shape, jnp.int32),
@@ -218,36 +212,30 @@
             pltpu.VMEM(grad_t.shape, jnp.bfloat16),
             pltpu.VMEM(kv_cache.shape, jnp.bfloat16),
             pltpu.VMEM(low_rank.shape, jnp.bfloat16),
+            pltpu.VMEM((dp, 2 * step, src_count), jnp.bfloat16),
             pltpu.SemaphoreType.DMA((6,)),
         ],
         compiler_params=whole_vmem,
         name="attention_backward",
     )(source_lengths, target_lengths, query_t, grad_t, kv_cache, low_rank)
 
-    route = [(h, h * dp % mp + dp - 1 - h * dp // mp) for h in range(mp)]
-    pieces = pl.pallas_call(
-        functools.partial(split_kernel, rows),
-        out_shape=[jax.ShapeDtypeStruct((2 * step, src_count), jnp.bfloat16)] * dp,
-        in_specs=[vmem],
-        out_specs=[vmem] * dp,
-        compiler_params=params,
-        cost_estimate=pl.CostEstimate(flops=2 ** 36, bytes_accessed=2 ** 28, transcendentals=0),
-        name="split_columns",
-    )(lax.ppermute(both_grad, "mp", route))
-    arrived = [pieces[0]]
-    for s in range(1, dp):
-        route = [(m, m - m % dp + (m + s) % dp) for m in range(mp)]
+    got = lax.all_to_all(sent, "mp", 0, 0, axis_index_groups=[group_order(mp)], tiled=True)
+
+    arrived = []
+    for s in range(dp):
+        route = [
+            (h, h * dp % mp + (h * dp // mp + s) % dp) for h in range(mp)
+        ]
+        route = [pair for pair in route if pair[0] != pair[1]]
         arrived.append(lax.ppermute(pieces[s], "mp", route))
     ordered = pl.pallas_call(
-        order_kernel,
+        functools.partial(order_kernel, mp),
         out_shape=jax.ShapeDtypeStruct((dp, 2 * step, src_count), jnp.bfloat16),
-        in_specs=[vmem] * dp,
+        in_specs=[vmem] * (2 * dp),
         out_specs=vmem,
         compiler_params=params,
         name="order_pieces",
-    )(*arrived)
-
-    got = lax.all_to_all(sent, "mp", 0, 0, axis_index_groups=[group_order(mp)], tiled=True)
+    )(*arrived, *pieces)
 
     shares = pl.pallas_call(
         functools.partial(share_kernel, rows, both_rank),

time: 21.1 us -> 23.4 us (1.11)
  waiting for transfers between devices: 5.81 us -> 7.02 us
  starting transfers between devices: 10.1 us -> 10.7 us
  local copies, waits for them, and re-layouts: 0.01 us -> 0.45 us
    ppermute x1 -> x2, waiting for transfers between devices: 1.17 us -> 5.09 us  [local(): arrived.append(lax.ppermute(pieces[s], 'mp', route))]
    all_to_all x1, waiting for transfers between devices: 3.51 us -> 0.01 us  [local(): lax.all_to_all(sent, 'mp', 0, 0, axis_index_groups=[group_order(mp)], til...]
    ppermute x1 -> x2, starting transfers between devices: 0.15 us -> 2.66 us  [local(): arrived.append(lax.ppermute(pieces[s], 'mp', route))]
    ppermute x1, starting transfers between devices: 1.25 us -> 0.12 us  [local(): up_grad = up_grad + lax.ppermute(shares[s], ('dp', 'mp'), route)]
    ppermute x1, waiting for transfers between devices: 1.12 us -> 1.92 us  [local(): up_grad = up_grad + lax.ppermute(shares[s], ('dp', 'mp'), route)]
    ppermute x1 -> x0, starting transfers between devices: 0.52 us -> none  [local(): lax.ppermute(both_grad, 'mp', route)]
    unnamed x2 -> x6, local copies, waits for them, and re-layouts: 0.01 us -> 0.45 us
    all_to_all x1, starting transfers between devices: 8.2 us -> 7.95 us  [local(): lax.all_to_all(sent, 'mp', 0, 0, axis_index_groups=[group_order(mp)], til...]
  transfers between devices with their start and end apart: 4 -> 4, of which waited for: 3 -> 2; matrix products, arithmetic and copies ran while one was open for 0% -> 0% of each run, Pallas kernels for 5% -> 4%
where the time goes in v10:
time: 23.4 us; the launch traced here: 23.1 us
  starting transfers between devices  10.7 us (46%)
  waiting for transfers between devices  7.02 us (30%)
  Pallas kernels  3.55 us (15%)
  between operations  0.71 us (3%)
  other arithmetic  0.61 us (3%)
  local copies, waits for them, and re-layouts  0.45 us (2%)
    all_to_all x1, starting transfers between devices, local(): lax.all_to_all(sent, 'mp', 0, 0, axis_index_groups=[group_order(mp)], til...  7.95 us
    ppermute x2, waiting for transfers between devices, local(): arrived.append(lax.ppermute(pieces[s], 'mp', route))  5.09 us
    ppermute x2, starting transfers between devices, local(): arrived.append(lax.ppermute(pieces[s], 'mp', route))  2.66 us
    pallas_call x1, Pallas kernels, local(): pl.pallas_call(attention_kernel, out_shape=[jax.ShapeDtypeStruct((HS, tgt...  2.4 us
    ppermute x1, waiting for transfers between devices, local(): up_grad = up_grad + lax.ppermute(shares[s], ('dp', 'mp'), route)  1.92 us
    pallas_call x1, Pallas kernels, local(): pl.pallas_call(owner_kernel, out_shape=[jax.ShapeDtypeStruct((rows, width...  0.86 us
    add x1, other arithmetic, local(): up_grad = up_grad + lax.ppermute(shares[s], ('dp', 'mp'), route)  0.61 us
  transfers between devices with their start and end apart: 4, of which 2 were waited for; matrix products, arithmetic and copies ran while one was open for 0% of the time, Pallas kernels for 4%

profile of v10, /device:TPU:0, one launch (start us, length us, event | category | flops | bytes accessed | tf_op | source)
XLA Modules:
  0.0 23.1 jit_solution(5061206569883049792)
XLA Ops:
  0.6 2.4 %attention_backward.1 = (bf16[64,256]{1,0:T(8,128)(2,1)}, bf16[16,40,128]{2,1,0:T(8,128)(2,1)}, bf16[64,512]{1,0:T(8,128)(2,1)}, bf16[64,512]{1,0:T(8,128)(2,1)}) custom-call(s32[1,8]{1,0:T(1,128)} %source_any.1, s32[1,8]{1,0:T(1,128)} %target_any.1, bf16[64,256]{1,0:T(8,128)(2,1)} %bitcast.3, bf16[64,256]{1,0:T(8,128)(2,1)} %bitcast.4, ...), custom_call_target="tpu_custom_call" | custom-call | tf_op jit(solution)/shard_map/attention_backward/pallas_call | solution.py:200
  3.0 0.0 copy-start.1
  3.1 0.0 copy-start.2
  3.1 8.0 %all-to-all-start = ((bf16[16,40,128]{2,1,0:T(8,128)(2,1)}), bf16[16,40,128]{2,1,0:T(8,128)(2,1)S(1)}, u32[]{:S(2)}, u32[]{:S(2)}) async-start(bf16[16,40,128]{2,1,0:T(8,128)(2,1)} %get-tuple-element.15), calls=%async_computation | async-start | bytes 327680 | tf_op jit(solution)/shard_map/all_to_all | solution.py:222
  11.0 0.0 copy-done.1
  11.0 0.7 %collective-permute-start = (bf16[64,512]{1,0:T(8,128)(2,1)S(1)}, bf16[64,512]{1,0:T(8,128)(2,1)S(1)}, u32[]{:S(2)}, u32[]{:S(2)}) collective-permute-start(bf16[64,512]{1,0:T(8,128)(2,1)S(1)} %copy-done.1), channel_id=1, source_target_pairs={{1,2},{2,4},{3,6},{4,8},{5,10},{6,12},{7,14},{8,1},{9,3},{10,5},{1... | collective-permute-start | bytes 196616 | tf_op jit(solution)/shard_map/ppermute | solution.py:230
  11.7 0.0 copy-done.2
  11.7 2.0 %collective-permute-start.1 = (bf16[64,512]{1,0:T(8,128)(2,1)S(1)}, bf16[64,512]{1,0:T(8,128)(2,1)S(1)}, u32[]{:S(2)}, u32[]{:S(2)}) collective-permute-start(bf16[64,512]{1,0:T(8,128)(2,1)S(1)} %copy-done.2), channel_id=1, source_target_pairs={{0,1},{1,3},{2,5},{3,7},{4,9},{5,11},{6,13},{7,15},{8,0},{9,2},{10... | collective-permute-start | bytes 196616 | tf_op jit(solution)/shard_map/ppermute | solution.py:230
  13.7 0.0 collective-permute-done.refs_0_
  13.7 5.1 %collective-permute-done.1.refs_1_ = bf16[64,512]{1,0:T(8,128)(2,1)S(1)} collective-permute-done((bf16[64,512]{1,0:T(8,128)(2,1)S(1)}, bf16[64,512]{1,0:T(8,128)(2,1)S(1)}, u32[]{:S(2)}, u32[]{:S(2)}) %collective-permute-start.1) | collective-permute-done | bytes 65568 | tf_op jit(solution)/shard_map/ppermute | solution.py:230
  18.8 0.0 copy-start
  18.8 0.0 all-to-all-done.got_ref
  18.9 0.3 %adapter_shares.1 = (f32[32,32]{1,0:T(8,128)S(1)}, f32[32,32]{1,0:T(8,128)S(1)}) custom-call(bf16[16,40,128]{2,1,0:T(8,128)(2,1)S(1)} %all-to-all-done.got_ref, bf16[2,64,512]{2,1,0:T(8,128)(2,1)S(1)} %order_pieces.1.pieces_ref), custom_call_target="tpu_custom_call" | custom-call | tf_op jit(solution)/shard_map/adapter_shares/pallas_call | solution.py:240
  19.1 0.1 collective-permute-start.2
  19.2 0.4 %copy-done = bf16[32,1024]{1,0:T(8,128)(2,1)S(1)} copy-done((bf16[32,1024]{1,0:T(8,128)(2,1)S(1)}, bf16[32,1024]{1,0:T(8,128)(2,1)}, u32[]{:S(2)}) %copy-start) | copy-done | bytes 65560
  19.7 0.9 %owner_outputs.1 = (bf16[32,1024]{1,0:T(8,128)(2,1)}, bf16[32,1024]{1,0:T(8,128)(2,1)}, f32[32,32]{1,0:T(8,128)}) custom-call(bf16[16,40,128]{2,1,0:T(8,128)(2,1)S(1)} %all-to-all-done.got_ref, bf16[32,1024]{1,0:T(8,128)(2,1)S(1)} %copy-done), custom_call_target="tpu_custom_call" | custom-call | tf_op jit(solution)/shard_map/owner_outputs/pallas_call | solution.py:256
  20.5 1.9 %collective-permute-done.2 = f32[32,32]{1,0:T(8,128)S(1)} collective-permute-done((f32[32,32]{1,0:T(8,128)S(1)}, f32[32,32]{1,0:T(8,128)S(1)}, u32[]{:S(2)}, u32[]{:S(2)}) %collective-permute-start.2) | collective-permute-done | bytes 4128 | tf_op jit(solution)/shard_map/ppermute | solution.py:254
  22.5 0.6 %add.3 = f32[32,32]{1,0:T(8,128)} add(f32[32,32]{1,0:T(8,128)S(1)} %get-tuple-element.21, f32[32,32]{1,0:T(8,128)S(1)} %collective-permute-done.2) | non-fusion elementwise | flops 1024 | bytes 12288 | tf_op jit(solution)/shard_map/add | solution.py:254
  (1 shorter events, 0.0 us)
Async XLA Ops:
  3.0 8.0 %copy-start.1 = (bf16[64,512]{1,0:T(8,128)(2,1)S(1)}, bf16[64,512]{1,0:T(8,128)(2,1)}, u32[]{:S(2)}) copy-start(bf16[64,512]{1,0:T(8,128)(2,1)} %get-tuple-element.19.refs_2_) | copy-start | bytes 196612
  3.1 8.6 %copy-start.2 = (bf16[64,512]{1,0:T(8,128)(2,1)S(1)}, bf16[64,512]{1,0:T(8,128)(2,1)}, u32[]{:S(2)}) copy-start(bf16[64,512]{1,0:T(8,128)(2,1)} %get-tuple-element.20.refs_3_) | copy-start | bytes 196612
  3.1 15.8 %all-to-all-start = ((bf16[16,40,128]{2,1,0:T(8,128)(2,1)}), bf16[16,40,128]{2,1,0:T(8,128)(2,1)S(1)}, u32[]{:S(2)}, u32[]{:S(2)}) async-start(bf16[16,40,128]{2,1,0:T(8,128)(2,1)} %get-tuple-element.15), calls=%async_computation | async-start | bytes 327680 | tf_op jit(solution)/shard_map/all_to_all | solution.py:222
  11.0 2.7 %collective-permute-start = (bf16[64,512]{1,0:T(8,128)(2,1)S(1)}, bf16[64,512]{1,0:T(8,128)(2,1)S(1)}, u32[]{:S(2)}, u32[]{:S(2)}) collective-permute-start(bf16[64,512]{1,0:T(8,128)(2,1)S(1)} %copy-done.1), channel_id=1, source_target_pairs={{1,2},{2,4},{3,6},{4,8},{5,10},{6,12},{7,14},{8,1},{9,3},{10,5},{1... | collective-permute-start | bytes 196616 | tf_op jit(solution)/shard_map/ppermute | solution.py:230
  11.7 7.1 %collective-permute-start.1 = (bf16[64,512]{1,0:T(8,128)(2,1)S(1)}, bf16[64,512]{1,0:T(8,128)(2,1)S(1)}, u32[]{:S(2)}, u32[]{:S(2)}) collective-permute-start(bf16[64,512]{1,0:T(8,128)(2,1)S(1)} %copy-done.2), channel_id=1, source_target_pairs={{0,1},{1,3},{2,5},{3,7},{4,9},{5,11},{6,13},{7,15},{8,0},{9,2},{10... | collective-permute-start | bytes 196616 | tf_op jit(solution)/shard_map/ppermute | solution.py:230
  18.8 0.8 %copy-start = (bf16[32,1024]{1,0:T(8,128)(2,1)S(1)}, bf16[32,1024]{1,0:T(8,128)(2,1)}, u32[]{:S(2)}) copy-start(bf16[32,1024]{1,0:T(8,128)(2,1)} %up_ref.1) | copy-start | bytes 196612
  19.1 3.3 %collective-permute-start.2 = (f32[32,32]{1,0:T(8,128)S(1)}, f32[32,32]{1,0:T(8,128)S(1)}, u32[]{:S(2)}, u32[]{:S(2)}) collective-permute-start(f32[32,32]{1,0:T(8,128)S(1)} %get-tuple-element.22), channel_id=1, source_target_pairs={{0,17},{1,16},{2,19},{3,18},{4,21},{5,20},{6,23},{7,22},{8,25},{9,... | collective-permute-start | bytes 12296 | tf_op jit(solution)/shard_map/ppermute | solution.py:254

commit v11 on v8

--- a/solution.py
+++ b/solution.py
@@ -29,8 +29,8 @@
     order = []
     for near, far in ((2, 3), (1, 0)):
         for i in range(quarter):
-            order.append(near * quarter + turned[quarter - 1 - i])
-            order.append(far * quarter + turned[(quarter - 1 - i) ^ 1])
+            order.append(near * quarter + (turned[quarter - 1 - i] ^ 1))
+            order.append(far * quarter + (turned[(quarter - 1 - i) ^ 1] ^ 1))
     return order
 
 

time: 21.1 us -> 21.2 us (level)
  starting transfers between devices: 10.1 us -> 10.4 us
    all_to_all x1, starting transfers between devices: 8.2 us -> 8.45 us  [local(): lax.all_to_all(sent, 'mp', 0, 0, axis_index_groups=[group_order(mp)], til...]
where the time goes in v11:
time: 21.2 us; the launch traced here: 20.9 us
  starting transfers between devices  10.4 us (49%)
  waiting for transfers between devices  5.65 us (27%)
  Pallas kernels  3.6 us (17%)
  between operations  0.68 us (3%)
  other arithmetic  0.61 us (3%)
    all_to_all x1, starting transfers between devices, local(): lax.all_to_all(sent, 'mp', 0, 0, axis_index_groups=[group_order(mp)], til...  8.45 us
    all_to_all x1, waiting for transfers between devices, local(): lax.all_to_all(sent, 'mp', 0, 0, axis_index_groups=[group_order(mp)], til...  3.39 us
    pallas_call x1, Pallas kernels, local(): pl.pallas_call(attention_kernel, out_shape=[jax.ShapeDtypeStruct((HS, tgt...  2.36 us
    ppermute x1, starting transfers between devices, local(): up_grad = up_grad + lax.ppermute(shares[s], ('dp', 'mp'), route)  1.21 us
    ppermute x1, waiting for transfers between devices, local(): up_grad = up_grad + lax.ppermute(shares[s], ('dp', 'mp'), route)  1.16 us
    ppermute x1, waiting for transfers between devices, local(): arrived.append(lax.ppermute(pieces[s], 'mp', route))  1.11 us
    pallas_call x1, Pallas kernels, local(): pl.pallas_call(owner_kernel, out_shape=[jax.ShapeDtypeStruct((rows, width...  0.86 us
    add x1, other arithmetic, local(): up_grad = up_grad + lax.ppermute(shares[s], ('dp', 'mp'), route)  0.61 us
  transfers between devices with their start and end apart: 4, of which 3 were waited for; matrix products, arithmetic and copies ran while one was open for 0% of the time, Pallas kernels for 5%

profile of v11, /device:TPU:0, one launch (start us, length us, event | category | flops | bytes accessed | tf_op | source)
XLA Modules:
  0.0 20.9 jit_solution(7667951000012052)
XLA Ops:
  0.6 2.4 %attention_backward.1 = (bf16[64,256]{1,0:T(8,128)(2,1)}, bf16[16,40,128]{2,1,0:T(8,128)(2,1)}, bf16[512,128]{1,0:T(8,128)(2,1)}) custom-call(s32[1,8]{1,0:T(1,128)} %source_any.1, s32[1,8]{1,0:T(1,128)} %target_any.1, bf16[64,256]{1,0:T(8,128)(2,1)} %bitcast.3, bf16[64,256]{1,0:T(8,128)(2,1)} %bitcast.4, bf16[512,128]{1,0:T(8,128)(2,1)} %kv_any.1, ...), custom_call_target="tpu_custom_call" | custom-call | tf_op jit(solution)/shard_map/attention_backward/pallas_call | solution.py:205
  3.0 0.5 %collective-permute-start = (bf16[512,128]{1,0:T(8,128)(2,1)}, bf16[512,128]{1,0:T(8,128)(2,1)S(1)}, u32[]{:S(2)}, u32[]{:S(2)}) collective-permute-start(bf16[512,128]{1,0:T(8,128)(2,1)} %get-tuple-element.20), channel_id=1, source_target_pairs={{0,1},{1,3},{2,5},{3,7},{4,9},{5,11},{6,13},{7,15},{8,0},{9,2},{10... | collective-permute-start | bytes 393224 | tf_op jit(solution)/shard_map/ppermute | solution.py:236
  3.5 8.4 %all-to-all-start = ((bf16[16,40,128]{2,1,0:T(8,128)(2,1)}), bf16[16,40,128]{2,1,0:T(8,128)(2,1)S(1)}, u32[]{:S(2)}, u32[]{:S(2)}) async-start(bf16[16,40,128]{2,1,0:T(8,128)(2,1)} %get-tuple-element.16), calls=%async_computation | async-start | bytes 327680 | tf_op jit(solution)/shard_map/all_to_all | solution.py:250
  12.0 0.0 collective-permute-done.both_grad_ref
  12.0 0.1 split_columns.1
  12.1 0.2 %collective-permute-start.1 = (bf16[64,512]{1,0:T(8,128)(2,1)S(1)}, bf16[64,512]{1,0:T(8,128)(2,1)S(1)}, u32[]{:S(2)}, u32[]{:S(2)}) collective-permute-start(bf16[64,512]{1,0:T(8,128)(2,1)S(1)} %get-tuple-element.22), channel_id=1, source_target_pairs={{0,1},{1,0},{2,3},{3,2},{4,5},{5,4},{6,7},{7,6},{8,9},{9,8},{10,11... | collective-permute-start | bytes 196616 | tf_op jit(solution)/shard_map/ppermute | solution.py:240
  12.3 1.1 %collective-permute-done.1.refs_1_ = bf16[64,512]{1,0:T(8,128)(2,1)S(1)} collective-permute-done((bf16[64,512]{1,0:T(8,128)(2,1)S(1)}, bf16[64,512]{1,0:T(8,128)(2,1)S(1)}, u32[]{:S(2)}, u32[]{:S(2)}) %collective-permute-start.1) | collective-permute-done | bytes 65568 | tf_op jit(solution)/shard_map/ppermute | solution.py:240
  13.4 0.0 copy-start
  13.4 3.4 %all-to-all-done.got_ref = bf16[16,40,128]{2,1,0:T(8,128)(2,1)S(1)} async-done(((bf16[16,40,128]{2,1,0:T(8,128)(2,1)}), bf16[16,40,128]{2,1,0:T(8,128)(2,1)S(1)}, u32[]{:S(2)}, u32[]{:S(2)}) %all-to-all-start) | async-done | bytes 163872 | tf_op jit(solution)/shard_map/all_to_all | solution.py:250
  16.8 0.3 %adapter_shares.1 = (f32[32,32]{1,0:T(8,128)S(1)}, f32[32,32]{1,0:T(8,128)S(1)}) custom-call(bf16[16,40,128]{2,1,0:T(8,128)(2,1)S(1)} %all-to-all-done.got_ref, bf16[2,64,512]{2,1,0:T(8,128)(2,1)S(1)} %order_pieces.1.pieces_ref), custom_call_target="tpu_custom_call" | custom-call | tf_op jit(solution)/shard_map/adapter_shares/pallas_call | solution.py:252
  17.1 1.2 %collective-permute-start.2 = (f32[32,32]{1,0:T(8,128)S(1)}, f32[32,32]{1,0:T(8,128)S(1)}, u32[]{:S(2)}, u32[]{:S(2)}) collective-permute-start(f32[32,32]{1,0:T(8,128)S(1)} %get-tuple-element.24), channel_id=1, source_target_pairs={{0,17},{1,16},{2,19},{3,18},{4,21},{5,20},{6,23},{7,22},{8,25},{9,... | collective-permute-start | bytes 12296 | tf_op jit(solution)/shard_map/ppermute | solution.py:266
  18.3 0.0 copy-done
  18.3 0.9 %owner_outputs.1 = (bf16[32,1024]{1,0:T(8,128)(2,1)}, bf16[32,1024]{1,0:T(8,128)(2,1)}, f32[32,32]{1,0:T(8,128)}) custom-call(bf16[16,40,128]{2,1,0:T(8,128)(2,1)S(1)} %all-to-all-done.got_ref, bf16[32,1024]{1,0:T(8,128)(2,1)S(1)} %copy-done), custom_call_target="tpu_custom_call" | custom-call | tf_op jit(solution)/shard_map/owner_outputs/pallas_call | solution.py:268
  19.2 1.2 %collective-permute-done.2 = f32[32,32]{1,0:T(8,128)S(1)} collective-permute-done((f32[32,32]{1,0:T(8,128)S(1)}, f32[32,32]{1,0:T(8,128)S(1)}, u32[]{:S(2)}, u32[]{:S(2)}) %collective-permute-start.2) | collective-permute-done | bytes 4128 | tf_op jit(solution)/shard_map/ppermute | solution.py:266
  20.3 0.6 %add.3 = f32[32,32]{1,0:T(8,128)} add(f32[32,32]{1,0:T(8,128)S(1)} %get-tuple-element.23, f32[32,32]{1,0:T(8,128)S(1)} %collective-permute-done.2) | non-fusion elementwise | flops 1024 | bytes 12288 | tf_op jit(solution)/shard_map/add | solution.py:266
  (1 shorter events, 0.0 us)
Async XLA Ops:
  3.0 9.0 %collective-permute-start = (bf16[512,128]{1,0:T(8,128)(2,1)}, bf16[512,128]{1,0:T(8,128)(2,1)S(1)}, u32[]{:S(2)}, u32[]{:S(2)}) collective-permute-start(bf16[512,128]{1,0:T(8,128)(2,1)} %get-tuple-element.20), channel_id=1, source_target_pairs={{0,1},{1,3},{2,5},{3,7},{4,9},{5,11},{6,13},{7,15},{8,0},{9,2},{10... | collective-permute-start | bytes 393224 | tf_op jit(solution)/shard_map/ppermute | solution.py:236
  3.5 13.3 %all-to-all-start = ((bf16[16,40,128]{2,1,0:T(8,128)(2,1)}), bf16[16,40,128]{2,1,0:T(8,128)(2,1)S(1)}, u32[]{:S(2)}, u32[]{:S(2)}) async-start(bf16[16,40,128]{2,1,0:T(8,128)(2,1)} %get-tuple-element.16), calls=%async_computation | async-start | bytes 327680 | tf_op jit(solution)/shard_map/all_to_all | solution.py:250
  12.1 1.3 %collective-permute-start.1 = (bf16[64,512]{1,0:T(8,128)(2,1)S(1)}, bf16[64,512]{1,0:T(8,128)(2,1)S(1)}, u32[]{:S(2)}, u32[]{:S(2)}) collective-permute-start(bf16[64,512]{1,0:T(8,128)(2,1)S(1)} %get-tuple-element.22), channel_id=1, source_target_pairs={{0,1},{1,0},{2,3},{3,2},{4,5},{5,4},{6,7},{7,6},{8,9},{9,8},{10,11... | collective-permute-start | bytes 196616 | tf_op jit(solution)/shard_map/ppermute | solution.py:240
  13.4 4.9 %copy-start = (bf16[32,1024]{1,0:T(8,128)(2,1)S(1)}, bf16[32,1024]{1,0:T(8,128)(2,1)}, u32[]{:S(2)}) copy-start(bf16[32,1024]{1,0:T(8,128)(2,1)} %up_ref.1) | copy-start | bytes 196612
  17.1 3.2 %collective-permute-start.2 = (f32[32,32]{1,0:T(8,128)S(1)}, f32[32,32]{1,0:T(8,128)S(1)}, u32[]{:S(2)}, u32[]{:S(2)}) collective-permute-start(f32[32,32]{1,0:T(8,128)S(1)} %get-tuple-element.24), channel_id=1, source_target_pairs={{0,17},{1,16},{2,19},{3,18},{4,21},{5,20},{6,23},{7,22},{8,25},{9,... | collective-permute-start | bytes 12296 | tf_op jit(solution)/shard_map/ppermute | solution.py:266

commit v12 on v11

--- a/solution.py
+++ b/solution.py
@@ -27,10 +27,9 @@
     assert count == 4 << bits
     turned = [sum(((i >> b) & 1) << (bits - 1 - b) for b in range(bits)) for i in range(quarter)]
     order = []
-    for near, far in ((2, 3), (1, 0)):
-        for i in range(quarter):
-            order.append(near * quarter + (turned[quarter - 1 - i] ^ 1))
-            order.append(far * quarter + (turned[(quarter - 1 - i) ^ 1] ^ 1))
+    for place in reversed(turned):
+        other = place ^ (quarter // 2)
+        order += [2 * quarter + place, other, 3 * quarter + place, quarter + other]
     return order
 
 

time: 21.2 us -> 21.3 us (level)
  waiting for transfers between devices: 5.65 us -> 6.73 us
  starting transfers between devices: 10.4 us -> 9.43 us
    ppermute x1, waiting for transfers between devices: 1.16 us -> 1.9 us  [local(): up_grad = up_grad + lax.ppermute(shares[s], ('dp', 'mp'), route)]
    ppermute x1, starting transfers between devices: 1.21 us -> 0.57 us  [local(): up_grad = up_grad + lax.ppermute(shares[s], ('dp', 'mp'), route)]
    all_to_all x1, waiting for transfers between devices: 3.39 us -> 3.65 us  [local(): lax.all_to_all(sent, 'mp', 0, 0, axis_index_groups=[group_order(mp)], til...]
    all_to_all x1, starting transfers between devices: 8.45 us -> 8.2 us  [local(): lax.all_to_all(sent, 'mp', 0, 0, axis_index_groups=[group_order(mp)], til...]
where the time goes in v12:
time: 21.3 us; the launch traced here: 21 us
  starting transfers between devices  9.43 us (44%)
  waiting for transfers between devices  6.73 us (32%)
  Pallas kernels  3.6 us (17%)
  between operations  0.68 us (3%)
  other arithmetic  0.61 us (3%)
    all_to_all x1, starting transfers between devices, local(): lax.all_to_all(sent, 'mp', 0, 0, axis_index_groups=[group_order(mp)], til...  8.2 us
    all_to_all x1, waiting for transfers between devices, local(): lax.all_to_all(sent, 'mp', 0, 0, axis_index_groups=[group_order(mp)], til...  3.65 us
    pallas_call x1, Pallas kernels, local(): pl.pallas_call(attention_kernel, out_shape=[jax.ShapeDtypeStruct((HS, tgt...  2.36 us
    ppermute x1, waiting for transfers between devices, local(): up_grad = up_grad + lax.ppermute(shares[s], ('dp', 'mp'), route)  1.9 us
    ppermute x1, waiting for transfers between devices, local(): arrived.append(lax.ppermute(pieces[s], 'mp', route))  1.17 us
    pallas_call x1, Pallas kernels, local(): pl.pallas_call(owner_kernel, out_shape=[jax.ShapeDtypeStruct((rows, width...  0.86 us
    add x1, other arithmetic, local(): up_grad = up_grad + lax.ppermute(shares[s], ('dp', 'mp'), route)  0.61 us
    ppermute x1, starting transfers between devices, local(): up_grad = up_grad + lax.ppermute(shares[s], ('dp', 'mp'), route)  0.57 us
  transfers between devices with their start and end apart: 4, of which 3 were waited for; matrix products, arithmetic and copies ran while one was open for 0% of the time, Pallas kernels for 5%

profile of v12, /device:TPU:0, one launch (start us, length us, event | category | flops | bytes accessed | tf_op | source)
XLA Modules:
  0.0 21.0 jit_solution(17070655781923887942)
XLA Ops:
  0.6 2.4 %attention_backward.1 = (bf16[64,256]{1,0:T(8,128)(2,1)}, bf16[16,40,128]{2,1,0:T(8,128)(2,1)}, bf16[512,128]{1,0:T(8,128)(2,1)}) custom-call(s32[1,8]{1,0:T(1,128)} %source_any.1, s32[1,8]{1,0:T(1,128)} %target_any.1, bf16[64,256]{1,0:T(8,128)(2,1)} %bitcast.3, bf16[64,256]{1,0:T(8,128)(2,1)} %bitcast.4, bf16[512,128]{1,0:T(8,128)(2,1)} %kv_any.1, ...), custom_call_target="tpu_custom_call" | custom-call | tf_op jit(solution)/shard_map/attention_backward/pallas_call | solution.py:204
  3.0 0.5 %collective-permute-start = (bf16[512,128]{1,0:T(8,128)(2,1)}, bf16[512,128]{1,0:T(8,128)(2,1)S(1)}, u32[]{:S(2)}, u32[]{:S(2)}) collective-permute-start(bf16[512,128]{1,0:T(8,128)(2,1)} %get-tuple-element.20), channel_id=1, source_target_pairs={{0,1},{1,3},{2,5},{3,7},{4,9},{5,11},{6,13},{7,15},{8,0},{9,2},{10... | collective-permute-start | bytes 393224 | tf_op jit(solution)/shard_map/ppermute | solution.py:235
  3.5 8.2 %all-to-all-start = ((bf16[16,40,128]{2,1,0:T(8,128)(2,1)}), bf16[16,40,128]{2,1,0:T(8,128)(2,1)S(1)}, u32[]{:S(2)}, u32[]{:S(2)}) async-start(bf16[16,40,128]{2,1,0:T(8,128)(2,1)} %get-tuple-element.16), calls=%async_computation | async-start | bytes 327680 | tf_op jit(solution)/shard_map/all_to_all | solution.py:249
  11.7 0.0 collective-permute-done.both_grad_ref
  11.7 0.1 split_columns.1
  11.8 0.1 collective-permute-start.1
  12.0 1.2 %collective-permute-done.1.refs_1_ = bf16[64,512]{1,0:T(8,128)(2,1)S(1)} collective-permute-done((bf16[64,512]{1,0:T(8,128)(2,1)S(1)}, bf16[64,512]{1,0:T(8,128)(2,1)S(1)}, u32[]{:S(2)}, u32[]{:S(2)}) %collective-permute-start.1) | collective-permute-done | bytes 65568 | tf_op jit(solution)/shard_map/ppermute | solution.py:239
  13.2 0.0 copy-start
  13.2 3.6 %all-to-all-done.got_ref = bf16[16,40,128]{2,1,0:T(8,128)(2,1)S(1)} async-done(((bf16[16,40,128]{2,1,0:T(8,128)(2,1)}), bf16[16,40,128]{2,1,0:T(8,128)(2,1)S(1)}, u32[]{:S(2)}, u32[]{:S(2)}) %all-to-all-start) | async-done | bytes 163872 | tf_op jit(solution)/shard_map/all_to_all | solution.py:249
  16.8 0.3 %adapter_shares.1 = (f32[32,32]{1,0:T(8,128)S(1)}, f32[32,32]{1,0:T(8,128)S(1)}) custom-call(bf16[16,40,128]{2,1,0:T(8,128)(2,1)S(1)} %all-to-all-done.got_ref, bf16[2,64,512]{2,1,0:T(8,128)(2,1)S(1)} %order_pieces.1.pieces_ref), custom_call_target="tpu_custom_call" | custom-call | tf_op jit(solution)/shard_map/adapter_shares/pallas_call | solution.py:251
  17.1 0.6 %collective-permute-start.2 = (f32[32,32]{1,0:T(8,128)S(1)}, f32[32,32]{1,0:T(8,128)S(1)}, u32[]{:S(2)}, u32[]{:S(2)}) collective-permute-start(f32[32,32]{1,0:T(8,128)S(1)} %get-tuple-element.24), channel_id=1, source_target_pairs={{0,17},{1,16},{2,19},{3,18},{4,21},{5,20},{6,23},{7,22},{8,25},{9,... | collective-permute-start | bytes 12296 | tf_op jit(solution)/shard_map/ppermute | solution.py:265
  17.7 0.0 copy-done
  17.7 0.9 %owner_outputs.1 = (bf16[32,1024]{1,0:T(8,128)(2,1)}, bf16[32,1024]{1,0:T(8,128)(2,1)}, f32[32,32]{1,0:T(8,128)}) custom-call(bf16[16,40,128]{2,1,0:T(8,128)(2,1)S(1)} %all-to-all-done.got_ref, bf16[32,1024]{1,0:T(8,128)(2,1)S(1)} %copy-done), custom_call_target="tpu_custom_call" | custom-call | tf_op jit(solution)/shard_map/owner_outputs/pallas_call | solution.py:267
  18.5 1.9 %collective-permute-done.2 = f32[32,32]{1,0:T(8,128)S(1)} collective-permute-done((f32[32,32]{1,0:T(8,128)S(1)}, f32[32,32]{1,0:T(8,128)S(1)}, u32[]{:S(2)}, u32[]{:S(2)}) %collective-permute-start.2) | collective-permute-done | bytes 4128 | tf_op jit(solution)/shard_map/ppermute | solution.py:265
  20.4 0.6 %add.3 = f32[32,32]{1,0:T(8,128)} add(f32[32,32]{1,0:T(8,128)S(1)} %get-tuple-element.23, f32[32,32]{1,0:T(8,128)S(1)} %collective-permute-done.2) | non-fusion elementwise | flops 1024 | bytes 12288 | tf_op jit(solution)/shard_map/add | solution.py:265
  (1 shorter events, 0.0 us)
Async XLA Ops:
  3.0 8.7 %collective-permute-start = (bf16[512,128]{1,0:T(8,128)(2,1)}, bf16[512,128]{1,0:T(8,128)(2,1)S(1)}, u32[]{:S(2)}, u32[]{:S(2)}) collective-permute-start(bf16[512,128]{1,0:T(8,128)(2,1)} %get-tuple-element.20), channel_id=1, source_target_pairs={{0,1},{1,3},{2,5},{3,7},{4,9},{5,11},{6,13},{7,15},{8,0},{9,2},{10... | collective-permute-start | bytes 393224 | tf_op jit(solution)/shard_map/ppermute | solution.py:235
  3.5 13.3 %all-to-all-start = ((bf16[16,40,128]{2,1,0:T(8,128)(2,1)}), bf16[16,40,128]{2,1,0:T(8,128)(2,1)S(1)}, u32[]{:S(2)}, u32[]{:S(2)}) async-start(bf16[16,40,128]{2,1,0:T(8,128)(2,1)} %get-tuple-element.16), calls=%async_computation | async-start | bytes 327680 | tf_op jit(solution)/shard_map/all_to_all | solution.py:249
  11.8 1.3 %collective-permute-start.1 = (bf16[64,512]{1,0:T(8,128)(2,1)S(1)}, bf16[64,512]{1,0:T(8,128)(2,1)S(1)}, u32[]{:S(2)}, u32[]{:S(2)}) collective-permute-start(bf16[64,512]{1,0:T(8,128)(2,1)S(1)} %get-tuple-element.22), channel_id=1, source_target_pairs={{0,1},{1,0},{2,3},{3,2},{4,5},{5,4},{6,7},{7,6},{8,9},{9,8},{10,11... | collective-permute-start | bytes 196616 | tf_op jit(solution)/shard_map/ppermute | solution.py:239
  13.2 4.5 %copy-start = (bf16[32,1024]{1,0:T(8,128)(2,1)S(1)}, bf16[32,1024]{1,0:T(8,128)(2,1)}, u32[]{:S(2)}) copy-start(bf16[32,1024]{1,0:T(8,128)(2,1)} %up_ref.1) | copy-start | bytes 196612
  17.1 3.3 %collective-permute-start.2 = (f32[32,32]{1,0:T(8,128)S(1)}, f32[32,32]{1,0:T(8,128)S(1)}, u32[]{:S(2)}, u32[]{:S(2)}) collective-permute-start(f32[32,32]{1,0:T(8,128)S(1)} %get-tuple-element.24), channel_id=1, source_target_pairs={{0,17},{1,16},{2,19},{3,18},{4,21},{5,20},{6,23},{7,22},{8,25},{9,... | collective-permute-start | bytes 12296 | tf_op jit(solution)/shard_map/ppermute | solution.py:265

commit v13 on v12

--- a/solution.py
+++ b/solution.py
@@ -27,9 +27,8 @@
     assert count == 4 << bits
     turned = [sum(((i >> b) & 1) << (bits - 1 - b) for b in range(bits)) for i in range(quarter)]
     order = []
-    for place in reversed(turned):
-        other = place ^ (quarter // 2)
-        order += [2 * quarter + place, other, 3 * quarter + place, quarter + other]
+    for i, place in enumerate(reversed(turned)):
+        order += [2 * quarter + place, 2 * i, 3 * quarter + place, 2 * i + 1]
     return order
 
 

time: 21.3 us -> 20.8 us (0.977)
  waiting for transfers between devices: 6.73 us -> 5.42 us
  starting transfers between devices: 9.43 us -> 10.2 us
    ppermute x1, waiting for transfers between devices: 1.9 us -> 1.07 us  [local(): up_grad = up_grad + lax.ppermute(shares[s], ('dp', 'mp'), route)]
    ppermute x1, starting transfers between devices: 0.57 us -> 1.3 us  [local(): up_grad = up_grad + lax.ppermute(shares[s], ('dp', 'mp'), route)]
    all_to_all x1, waiting for transfers between devices: 3.65 us -> 3.24 us  [local(): lax.all_to_all(sent, 'mp', 0, 0, axis_index_groups=[group_order(mp)], til...]
where the time goes in v13:
time: 20.8 us; the launch traced here: 20.5 us
  starting transfers between devices  10.2 us (49%)
  waiting for transfers between devices  5.42 us (26%)
  Pallas kernels  3.6 us (17%)
  between operations  0.68 us (3%)
  other arithmetic  0.61 us (3%)
    all_to_all x1, starting transfers between devices, local(): lax.all_to_all(sent, 'mp', 0, 0, axis_index_groups=[group_order(mp)], til...  8.16 us
    all_to_all x1, waiting for transfers between devices, local(): lax.all_to_all(sent, 'mp', 0, 0, axis_index_groups=[group_order(mp)], til...  3.24 us
    pallas_call x1, Pallas kernels, local(): pl.pallas_call(attention_kernel, out_shape=[jax.ShapeDtypeStruct((HS, tgt...  2.36 us
    ppermute x1, starting transfers between devices, local(): up_grad = up_grad + lax.ppermute(shares[s], ('dp', 'mp'), route)  1.3 us
    ppermute x1, waiting for transfers between devices, local(): arrived.append(lax.ppermute(pieces[s], 'mp', route))  1.11 us
    ppermute x1, waiting for transfers between devices, local(): up_grad = up_grad + lax.ppermute(shares[s], ('dp', 'mp'), route)  1.07 us
    pallas_call x1, Pallas kernels, local(): pl.pallas_call(owner_kernel, out_shape=[jax.ShapeDtypeStruct((rows, width...  0.86 us
    add x1, other arithmetic, local(): up_grad = up_grad + lax.ppermute(shares[s], ('dp', 'mp'), route)  0.61 us
  transfers between devices with their start and end apart: 4, of which 3 were waited for; matrix products, arithmetic and copies ran while one was open for 0% of the time, Pallas kernels for 5%

profile of v13, /device:TPU:0, one launch (start us, length us, event | category | flops | bytes accessed | tf_op | source)
XLA Modules:
  0.0 20.5 jit_solution(10065462488834563975)
XLA Ops:
  0.6 2.4 %attention_backward.1 = (bf16[64,256]{1,0:T(8,128)(2,1)}, bf16[16,40,128]{2,1,0:T(8,128)(2,1)}, bf16[512,128]{1,0:T(8,128)(2,1)}) custom-call(s32[1,8]{1,0:T(1,128)} %source_any.1, s32[1,8]{1,0:T(1,128)} %target_any.1, bf16[64,256]{1,0:T(8,128)(2,1)} %bitcast.3, bf16[64,256]{1,0:T(8,128)(2,1)} %bitcast.4, bf16[512,128]{1,0:T(8,128)(2,1)} %kv_any.1, ...), custom_call_target="tpu_custom_call" | custom-call | tf_op jit(solution)/shard_map/attention_backward/pallas_call | solution.py:203
  3.0 0.5 %collective-permute-start = (bf16[512,128]{1,0:T(8,128)(2,1)}, bf16[512,128]{1,0:T(8,128)(2,1)S(1)}, u32[]{:S(2)}, u32[]{:S(2)}) collective-permute-start(bf16[512,128]{1,0:T(8,128)(2,1)} %get-tuple-element.20), channel_id=1, source_target_pairs={{0,1},{1,3},{2,5},{3,7},{4,9},{5,11},{6,13},{7,15},{8,0},{9,2},{10... | collective-permute-start | bytes 393224 | tf_op jit(solution)/shard_map/ppermute | solution.py:234
  3.5 8.2 %all-to-all-start = ((bf16[16,40,128]{2,1,0:T(8,128)(2,1)}), bf16[16,40,128]{2,1,0:T(8,128)(2,1)S(1)}, u32[]{:S(2)}, u32[]{:S(2)}) async-start(bf16[16,40,128]{2,1,0:T(8,128)(2,1)} %get-tuple-element.16), calls=%async_computation | async-start | bytes 327680 | tf_op jit(solution)/shard_map/all_to_all | solution.py:248
  11.7 0.0 collective-permute-done.both_grad_ref
  11.7 0.1 split_columns.1
  11.8 0.2 %collective-permute-start.1 = (bf16[64,512]{1,0:T(8,128)(2,1)S(1)}, bf16[64,512]{1,0:T(8,128)(2,1)S(1)}, u32[]{:S(2)}, u32[]{:S(2)}) collective-permute-start(bf16[64,512]{1,0:T(8,128)(2,1)S(1)} %get-tuple-element.22), channel_id=1, source_target_pairs={{0,1},{1,0},{2,3},{3,2},{4,5},{5,4},{6,7},{7,6},{8,9},{9,8},{10,11... | collective-permute-start | bytes 196616 | tf_op jit(solution)/shard_map/ppermute | solution.py:238
  12.0 1.1 %collective-permute-done.1.refs_1_ = bf16[64,512]{1,0:T(8,128)(2,1)S(1)} collective-permute-done((bf16[64,512]{1,0:T(8,128)(2,1)S(1)}, bf16[64,512]{1,0:T(8,128)(2,1)S(1)}, u32[]{:S(2)}, u32[]{:S(2)}) %collective-permute-start.1) | collective-permute-done | bytes 65568 | tf_op jit(solution)/shard_map/ppermute | solution.py:238
  13.1 0.0 copy-start
  13.2 3.2 %all-to-all-done.got_ref = bf16[16,40,128]{2,1,0:T(8,128)(2,1)S(1)} async-done(((bf16[16,40,128]{2,1,0:T(8,128)(2,1)}), bf16[16,40,128]{2,1,0:T(8,128)(2,1)S(1)}, u32[]{:S(2)}, u32[]{:S(2)}) %all-to-all-start) | async-done | bytes 163872 | tf_op jit(solution)/shard_map/all_to_all | solution.py:248
  16.4 0.3 %adapter_shares.1 = (f32[32,32]{1,0:T(8,128)S(1)}, f32[32,32]{1,0:T(8,128)S(1)}) custom-call(bf16[16,40,128]{2,1,0:T(8,128)(2,1)S(1)} %all-to-all-done.got_ref, bf16[2,64,512]{2,1,0:T(8,128)(2,1)S(1)} %order_pieces.1.pieces_ref), custom_call_target="tpu_custom_call" | custom-call | tf_op jit(solution)/shard_map/adapter_shares/pallas_call | solution.py:250
  16.7 1.3 %collective-permute-start.2 = (f32[32,32]{1,0:T(8,128)S(1)}, f32[32,32]{1,0:T(8,128)S(1)}, u32[]{:S(2)}, u32[]{:S(2)}) collective-permute-start(f32[32,32]{1,0:T(8,128)S(1)} %get-tuple-element.24), channel_id=1, source_target_pairs={{0,17},{1,16},{2,19},{3,18},{4,21},{5,20},{6,23},{7,22},{8,25},{9,... | collective-permute-start | bytes 12296 | tf_op jit(solution)/shard_map/ppermute | solution.py:264
  18.0 0.0 copy-done
  18.0 0.9 %owner_outputs.1 = (bf16[32,1024]{1,0:T(8,128)(2,1)}, bf16[32,1024]{1,0:T(8,128)(2,1)}, f32[32,32]{1,0:T(8,128)}) custom-call(bf16[16,40,128]{2,1,0:T(8,128)(2,1)S(1)} %all-to-all-done.got_ref, bf16[32,1024]{1,0:T(8,128)(2,1)S(1)} %copy-done), custom_call_target="tpu_custom_call" | custom-call | tf_op jit(solution)/shard_map/owner_outputs/pallas_call | solution.py:266
  18.8 1.1 %collective-permute-done.2 = f32[32,32]{1,0:T(8,128)S(1)} collective-permute-done((f32[32,32]{1,0:T(8,128)S(1)}, f32[32,32]{1,0:T(8,128)S(1)}, u32[]{:S(2)}, u32[]{:S(2)}) %collective-permute-start.2) | collective-permute-done | bytes 4128 | tf_op jit(solution)/shard_map/ppermute | solution.py:264
  19.9 0.6 %add.3 = f32[32,32]{1,0:T(8,128)} add(f32[32,32]{1,0:T(8,128)S(1)} %get-tuple-element.23, f32[32,32]{1,0:T(8,128)S(1)} %collective-permute-done.2) | non-fusion elementwise | flops 1024 | bytes 12288 | tf_op jit(solution)/shard_map/add | solution.py:264
  (1 shorter events, 0.0 us)
Async XLA Ops:
  3.0 8.7 %collective-permute-start = (bf16[512,128]{1,0:T(8,128)(2,1)}, bf16[512,128]{1,0:T(8,128)(2,1)S(1)}, u32[]{:S(2)}, u32[]{:S(2)}) collective-permute-start(bf16[512,128]{1,0:T(8,128)(2,1)} %get-tuple-element.20), channel_id=1, source_target_pairs={{0,1},{1,3},{2,5},{3,7},{4,9},{5,11},{6,13},{7,15},{8,0},{9,2},{10... | collective-permute-start | bytes 393224 | tf_op jit(solution)/shard_map/ppermute | solution.py:234
  3.5 12.9 %all-to-all-start = ((bf16[16,40,128]{2,1,0:T(8,128)(2,1)}), bf16[16,40,128]{2,1,0:T(8,128)(2,1)S(1)}, u32[]{:S(2)}, u32[]{:S(2)}) async-start(bf16[16,40,128]{2,1,0:T(8,128)(2,1)} %get-tuple-element.16), calls=%async_computation | async-start | bytes 327680 | tf_op jit(solution)/shard_map/all_to_all | solution.py:248
  11.8 1.3 %collective-permute-start.1 = (bf16[64,512]{1,0:T(8,128)(2,1)S(1)}, bf16[64,512]{1,0:T(8,128)(2,1)S(1)}, u32[]{:S(2)}, u32[]{:S(2)}) collective-permute-start(bf16[64,512]{1,0:T(8,128)(2,1)S(1)} %get-tuple-element.22), channel_id=1, source_target_pairs={{0,1},{1,0},{2,3},{3,2},{4,5},{5,4},{6,7},{7,6},{8,9},{9,8},{10,11... | collective-permute-start | bytes 196616 | tf_op jit(solution)/shard_map/ppermute | solution.py:238
  13.1 4.8 %copy-start = (bf16[32,1024]{1,0:T(8,128)(2,1)S(1)}, bf16[32,1024]{1,0:T(8,128)(2,1)}, u32[]{:S(2)}) copy-start(bf16[32,1024]{1,0:T(8,128)(2,1)} %up_ref.1) | copy-start | bytes 196612
  16.7 3.2 %collective-permute-start.2 = (f32[32,32]{1,0:T(8,128)S(1)}, f32[32,32]{1,0:T(8,128)S(1)}, u32[]{:S(2)}, u32[]{:S(2)}) collective-permute-start(f32[32,32]{1,0:T(8,128)S(1)} %get-tuple-element.24), channel_id=1, source_target_pairs={{0,17},{1,16},{2,19},{3,18},{4,21},{5,20},{6,23},{7,22},{8,25},{9,... | collective-permute-start | bytes 12296 | tf_op jit(solution)/shard_map/ppermute | solution.py:264

commit v14 on v13

--- a/solution.py
+++ b/solution.py
@@ -147,12 +147,17 @@
     ]
     lows = jnp.concatenate(lows, axis=0).astype(jnp.bfloat16)
     columns = jnp.concatenate([pieces_ref[e] for e in range(dp)], axis=0)
-    share = None
-    for cut in range(rows // CUT):
-        tokens = columns[:, cut * blocks * CUT:(cut + 1) * blocks * CUT]
-        product = jnp.dot(tokens, lows, preferred_element_type=jnp.float32)
-        part = product[:, cut * both_rank:(cut + 1) * both_rank]
-        share = part if share is None else share + part
+    cuts = rows // CUT
+    width = blocks * CUT
+    stacked = [columns[:, cut * width:(cut + 1) * width] for cut in range(cuts)]
+    product = jnp.dot(
+        jnp.concatenate(stacked, axis=0), lows, preferred_element_type=jnp.float32
+    )
+    height = dp * piece_rows
+    share = sum(
+        product[cut * height:(cut + 1) * height, cut * both_rank:(cut + 1) * both_rank]
+        for cut in range(cuts)
+    )
     step = piece_rows // 2
     column = lax.broadcasted_iota(jnp.int32, (step, both_rank), 1)
     shares = []

time: 20.8 us -> 20.8 us (level)
  no operation moved by 1% of the time
where the time goes in v14:
time: 20.8 us; the launch traced here: 20.5 us
  starting transfers between devices  10.2 us (49%)
  waiting for transfers between devices  5.42 us (26%)
  Pallas kernels  3.6 us (17%)
  between operations  0.68 us (3%)
  other arithmetic  0.61 us (3%)
    all_to_all x1, starting transfers between devices, local(): lax.all_to_all(sent, 'mp', 0, 0, axis_index_groups=[group_order(mp)], til...  8.16 us
    all_to_all x1, waiting for transfers between devices, local(): lax.all_to_all(sent, 'mp', 0, 0, axis_index_groups=[group_order(mp)], til...  3.24 us
    pallas_call x1, Pallas kernels, local(): pl.pallas_call(attention_kernel, out_shape=[jax.ShapeDtypeStruct((HS, tgt...  2.36 us
    ppermute x1, starting transfers between devices, local(): up_grad = up_grad + lax.ppermute(shares[s], ('dp', 'mp'), route)  1.3 us
    ppermute x1, waiting for transfers between devices, local(): arrived.append(lax.ppermute(pieces[s], 'mp', route))  1.11 us
    ppermute x1, waiting for transfers between devices, local(): up_grad = up_grad + lax.ppermute(shares[s], ('dp', 'mp'), route)  1.07 us
    pallas_call x1, Pallas kernels, local(): pl.pallas_call(owner_kernel, out_shape=[jax.ShapeDtypeStruct((rows, width...  0.86 us
    add x1, other arithmetic, local(): up_grad = up_grad + lax.ppermute(shares[s], ('dp', 'mp'), route)  0.61 us
  transfers between devices with their start and end apart: 4, of which 3 were waited for; matrix products, arithmetic and copies ran while one was open for 0% of the time, Pallas kernels for 5%

profile of v14, /device:TPU:0, one launch (start us, length us, event | category | flops | bytes accessed | tf_op | source)
XLA Modules:
  0.0 20.5 jit_solution(4286259999100875958)
XLA Ops:
  0.6 2.4 %attention_backward.1 = (bf16[64,256]{1,0:T(8,128)(2,1)}, bf16[16,40,128]{2,1,0:T(8,128)(2,1)}, bf16[512,128]{1,0:T(8,128)(2,1)}) custom-call(s32[1,8]{1,0:T(1,128)} %source_any.1, s32[1,8]{1,0:T(1,128)} %target_any.1, bf16[64,256]{1,0:T(8,128)(2,1)} %bitcast.3, bf16[64,256]{1,0:T(8,128)(2,1)} %bitcast.4, bf16[512,128]{1,0:T(8,128)(2,1)} %kv_any.1, ...), custom_call_target="tpu_custom_call" | custom-call | tf_op jit(solution)/shard_map/attention_backward/pallas_call | solution.py:208
  3.0 0.5 %collective-permute-start = (bf16[512,128]{1,0:T(8,128)(2,1)}, bf16[512,128]{1,0:T(8,128)(2,1)S(1)}, u32[]{:S(2)}, u32[]{:S(2)}) collective-permute-start(bf16[512,128]{1,0:T(8,128)(2,1)} %get-tuple-element.20), channel_id=1, source_target_pairs={{0,1},{1,3},{2,5},{3,7},{4,9},{5,11},{6,13},{7,15},{8,0},{9,2},{10... | collective-permute-start | bytes 393224 | tf_op jit(solution)/shard_map/ppermute | solution.py:239
  3.5 8.2 %all-to-all-start = ((bf16[16,40,128]{2,1,0:T(8,128)(2,1)}), bf16[16,40,128]{2,1,0:T(8,128)(2,1)S(1)}, u32[]{:S(2)}, u32[]{:S(2)}) async-start(bf16[16,40,128]{2,1,0:T(8,128)(2,1)} %get-tuple-element.16), calls=%async_computation | async-start | bytes 327680 | tf_op jit(solution)/shard_map/all_to_all | solution.py:253
  11.7 0.0 collective-permute-done.both_grad_ref
  11.7 0.1 split_columns.1
  11.8 0.2 %collective-permute-start.1 = (bf16[64,512]{1,0:T(8,128)(2,1)S(1)}, bf16[64,512]{1,0:T(8,128)(2,1)S(1)}, u32[]{:S(2)}, u32[]{:S(2)}) collective-permute-start(bf16[64,512]{1,0:T(8,128)(2,1)S(1)} %get-tuple-element.22), channel_id=1, source_target_pairs={{0,1},{1,0},{2,3},{3,2},{4,5},{5,4},{6,7},{7,6},{8,9},{9,8},{10,11... | collective-permute-start | bytes 196616 | tf_op jit(solution)/shard_map/ppermute | solution.py:243
  12.0 1.1 %collective-permute-done.1.refs_1_ = bf16[64,512]{1,0:T(8,128)(2,1)S(1)} collective-permute-done((bf16[64,512]{1,0:T(8,128)(2,1)S(1)}, bf16[64,512]{1,0:T(8,128)(2,1)S(1)}, u32[]{:S(2)}, u32[]{:S(2)}) %collective-permute-start.1) | collective-permute-done | bytes 65568 | tf_op jit(solution)/shard_map/ppermute | solution.py:243
  13.1 0.0 copy-start
  13.2 3.2 %all-to-all-done.got_ref = bf16[16,40,128]{2,1,0:T(8,128)(2,1)S(1)} async-done(((bf16[16,40,128]{2,1,0:T(8,128)(2,1)}), bf16[16,40,128]{2,1,0:T(8,128)(2,1)S(1)}, u32[]{:S(2)}, u32[]{:S(2)}) %all-to-all-start) | async-done | bytes 163872 | tf_op jit(solution)/shard_map/all_to_all | solution.py:253
  16.4 0.3 %adapter_shares.1 = (f32[32,32]{1,0:T(8,128)S(1)}, f32[32,32]{1,0:T(8,128)S(1)}) custom-call(bf16[16,40,128]{2,1,0:T(8,128)(2,1)S(1)} %all-to-all-done.got_ref, bf16[2,64,512]{2,1,0:T(8,128)(2,1)S(1)} %order_pieces.1.pieces_ref), custom_call_target="tpu_custom_call" | custom-call | tf_op jit(solution)/shard_map/adapter_shares/pallas_call | solution.py:255
  16.7 1.3 %collective-permute-start.2 = (f32[32,32]{1,0:T(8,128)S(1)}, f32[32,32]{1,0:T(8,128)S(1)}, u32[]{:S(2)}, u32[]{:S(2)}) collective-permute-start(f32[32,32]{1,0:T(8,128)S(1)} %get-tuple-element.24), channel_id=1, source_target_pairs={{0,17},{1,16},{2,19},{3,18},{4,21},{5,20},{6,23},{7,22},{8,25},{9,... | collective-permute-start | bytes 12296 | tf_op jit(solution)/shard_map/ppermute | solution.py:269
  18.0 0.0 copy-done
  18.0 0.9 %owner_outputs.1 = (bf16[32,1024]{1,0:T(8,128)(2,1)}, bf16[32,1024]{1,0:T(8,128)(2,1)}, f32[32,32]{1,0:T(8,128)}) custom-call(bf16[16,40,128]{2,1,0:T(8,128)(2,1)S(1)} %all-to-all-done.got_ref, bf16[32,1024]{1,0:T(8,128)(2,1)S(1)} %copy-done), custom_call_target="tpu_custom_call" | custom-call | tf_op jit(solution)/shard_map/owner_outputs/pallas_call | solution.py:271
  18.8 1.1 %collective-permute-done.2 = f32[32,32]{1,0:T(8,128)S(1)} collective-permute-done((f32[32,32]{1,0:T(8,128)S(1)}, f32[32,32]{1,0:T(8,128)S(1)}, u32[]{:S(2)}, u32[]{:S(2)}) %collective-permute-start.2) | collective-permute-done | bytes 4128 | tf_op jit(solution)/shard_map/ppermute | solution.py:269
  19.9 0.6 %add.3 = f32[32,32]{1,0:T(8,128)} add(f32[32,32]{1,0:T(8,128)S(1)} %get-tuple-element.23, f32[32,32]{1,0:T(8,128)S(1)} %collective-permute-done.2) | non-fusion elementwise | flops 1024 | bytes 12288 | tf_op jit(solution)/shard_map/add | solution.py:269
  (1 shorter events, 0.0 us)
Async XLA Ops:
  3.0 8.7 %collective-permute-start = (bf16[512,128]{1,0:T(8,128)(2,1)}, bf16[512,128]{1,0:T(8,128)(2,1)S(1)}, u32[]{:S(2)}, u32[]{:S(2)}) collective-permute-start(bf16[512,128]{1,0:T(8,128)(2,1)} %get-tuple-element.20), channel_id=1, source_target_pairs={{0,1},{1,3},{2,5},{3,7},{4,9},{5,11},{6,13},{7,15},{8,0},{9,2},{10... | collective-permute-start | bytes 393224 | tf_op jit(solution)/shard_map/ppermute | solution.py:239
  3.5 12.9 %all-to-all-start = ((bf16[16,40,128]{2,1,0:T(8,128)(2,1)}), bf16[16,40,128]{2,1,0:T(8,128)(2,1)S(1)}, u32[]{:S(2)}, u32[]{:S(2)}) async-start(bf16[16,40,128]{2,1,0:T(8,128)(2,1)} %get-tuple-element.16), calls=%async_computation | async-start | bytes 327680 | tf_op jit(solution)/shard_map/all_to_all | solution.py:253
  11.8 1.3 %collective-permute-start.1 = (bf16[64,512]{1,0:T(8,128)(2,1)S(1)}, bf16[64,512]{1,0:T(8,128)(2,1)S(1)}, u32[]{:S(2)}, u32[]{:S(2)}) collective-permute-start(bf16[64,512]{1,0:T(8,128)(2,1)S(1)} %get-tuple-element.22), channel_id=1, source_target_pairs={{0,1},{1,0},{2,3},{3,2},{4,5},{5,4},{6,7},{7,6},{8,9},{9,8},{10,11... | collective-permute-start | bytes 196616 | tf_op jit(solution)/shard_map/ppermute | solution.py:243
  13.1 4.8 %copy-start = (bf16[32,1024]{1,0:T(8,128)(2,1)S(1)}, bf16[32,1024]{1,0:T(8,128)(2,1)}, u32[]{:S(2)}) copy-start(bf16[32,1024]{1,0:T(8,128)(2,1)} %up_ref.1) | copy-start | bytes 196612
  16.7 3.2 %collective-permute-start.2 = (f32[32,32]{1,0:T(8,128)S(1)}, f32[32,32]{1,0:T(8,128)S(1)}, u32[]{:S(2)}, u32[]{:S(2)}) collective-permute-start(f32[32,32]{1,0:T(8,128)S(1)} %get-tuple-element.24), channel_id=1, source_target_pairs={{0,17},{1,16},{2,19},{3,18},{4,21},{5,20},{6,23},{7,22},{8,25},{9,... | collective-permute-start | bytes 12296 | tf_op jit(solution)/shard_map/ppermute | solution.py:269

commit v15 on v14

--- a/solution.py
+++ b/solution.py
@@ -49,7 +49,7 @@
 
 
 def attention_kernel(
-    source_any, target_any, query_any, grad_any, kv_any, low_any, query_grad_ref, sent_ref, both_grad_ref,
+    source_any, target_any, query_any, grad_any, kv_any, low_any, query_grad_ref, sent_ref,
     source_ref, target_ref, query_ref, grad_ref, kv_ref, low_ref, sems,
 ):
     pairs = [
@@ -103,19 +103,18 @@
         sent_ref[at, :rows, :] = both_low[block * rows:(block + 1) * rows]
         sent_ref[at, rows:, :] = packed
 
-    both_grad_ref[...] = both_low
     query_grad = sum(dot(part, dscore, TN) for part, dscore in zip(parts, dscores))
     query_grad_ref[...] = query_grad[:HS].astype(jnp.bfloat16)
 
 
-def split_kernel(rows, both_grad_ref, *out_refs):
+def split_kernel(rows, blocks_ref, *out_refs):
     dp = len(out_refs)
     step = HS // dp
-    exact = both_grad_ref[...].astype(jnp.float32)
-    parts = []
-    for start in range(0, rows, CUT):
-        for block in range(0, exact.shape[0], rows):
-            parts.append(exact[block + start:block + start + CUT])
+    order = group_order(blocks_ref.shape[0])
+    exact = [
+        blocks_ref[order.index(block), :rows, :].astype(jnp.float32) for block in range(len(order))
+    ]
+    parts = [part[start:start + CUT] for start in range(0, rows, CUT) for part in exact]
     turned = jnp.concatenate(parts, axis=0).T
     pieces = []
     for j in range(dp):
@@ -205,15 +204,14 @@
 
     query_t = query.T
     grad_t = out_grad.T
-    query_grad_t, sent, both_grad = pl.pallas_call(
+    query_grad_t, sent = pl.pallas_call(
         attention_kernel,
         out_shape=[
             jax.ShapeDtypeStruct((HS, tgt_count), jnp.bfloat16),
             jax.ShapeDtypeStruct((mp, rows + CUT, LANES), jnp.bfloat16),
-            jax.ShapeDtypeStruct((src_count, 2 * HS), jnp.bfloat16),
         ],
         in_specs=[hbm] * 6,
-        out_specs=[vmem] * 3,
+        out_specs=[vmem] * 2,
         scratch_shapes=[
             pltpu.SMEM(source_lengths.shape, jnp.int32),
             pltpu.SMEM(target_lengths.shape, jnp.int32),
@@ -236,7 +234,7 @@
         compiler_params=params,
         cost_estimate=pl.CostEstimate(flops=2 ** 36, bytes_accessed=2 ** 28, transcendentals=0),
         name="split_columns",
-    )(lax.ppermute(both_grad, "mp", route))
+    )(lax.ppermute(sent, "mp", route))
     arrived = [pieces[0]]
     for s in range(1, dp):
         route = [(m, m - m % dp + (m + s) % dp) for m in range(mp)]

time: 20.8 us -> 20.7 us (level)
  transfers between devices with their start and end apart: 4 -> 4, of which waited for: 3 -> 4; matrix products, arithmetic and copies ran while one was open for 0% -> 0% of each run, Pallas kernels for 5% -> 5%
where the time goes in v15:
time: 20.7 us; the launch traced here: 20.5 us
  starting transfers between devices  10.1 us (49%)
  waiting for transfers between devices  5.49 us (27%)
  Pallas kernels  3.54 us (17%)
  between operations  0.67 us (3%)
  other arithmetic  0.61 us (3%)
    all_to_all x1, starting transfers between devices, local(): lax.all_to_all(sent, 'mp', 0, 0, axis_index_groups=[group_order(mp)], til...  8.16 us
    all_to_all x1, waiting for transfers between devices, local(): lax.all_to_all(sent, 'mp', 0, 0, axis_index_groups=[group_order(mp)], til...  3.19 us
    pallas_call x1, Pallas kernels, local(): pl.pallas_call(attention_kernel, out_shape=[jax.ShapeDtypeStruct((HS, tgt...  2.31 us
    ppermute x1, starting transfers between devices, local(): up_grad = up_grad + lax.ppermute(shares[s], ('dp', 'mp'), route)  1.3 us
    ppermute x1, waiting for transfers between devices, local(): arrived.append(lax.ppermute(pieces[s], 'mp', route))  1.16 us
    ppermute x1, waiting for transfers between devices, local(): up_grad = up_grad + lax.ppermute(shares[s], ('dp', 'mp'), route)  1.07 us
    pallas_call x1, Pallas kernels, local(): pl.pallas_call(owner_kernel, out_shape=[jax.ShapeDtypeStruct((rows, width...  0.85 us
    add x1, other arithmetic, local(): up_grad = up_grad + lax.ppermute(shares[s], ('dp', 'mp'), route)  0.61 us
  transfers between devices with their start and end apart: 4, of which 4 were waited for; matrix products, arithmetic and copies ran while one was open for 0% of the time, Pallas kernels for 5%

profile of v15, /device:TPU:0, one launch (start us, length us, event | category | flops | bytes accessed | tf_op | source)
XLA Modules:
  0.0 20.5 jit_solution(14462501066050471322)
XLA Ops:
  0.6 2.3 %attention_backward.1 = (bf16[64,256]{1,0:T(8,128)(2,1)}, bf16[16,40,128]{2,1,0:T(8,128)(2,1)}) custom-call(s32[1,8]{1,0:T(1,128)} %source_any.1, s32[1,8]{1,0:T(1,128)} %target_any.1, bf16[64,256]{1,0:T(8,128)(2,1)} %bitcast.3, bf16[64,256]{1,0:T(8,128)(2,1)} %bitcast.4, bf16[512,128]{1,0:T(8,128)(2,1)} %kv_any.1, bf16[32,32]{1,0:T(8,128)(2,1)} %low_any.1), custom_call_target="tpu_custom_call" | custom-call | tf_op jit(solution)/shard_map/attention_backward/pallas_call | solution.py:207
  3.0 0.5 %collective-permute-start = (bf16[16,40,128]{2,1,0:T(8,128)(2,1)}, bf16[16,40,128]{2,1,0:T(8,128)(2,1)S(1)}, u32[]{:S(2)}, u32[]{:S(2)}) collective-permute-start(bf16[16,40,128]{2,1,0:T(8,128)(2,1)} %get-tuple-element.15), channel_id=1, source_target_pairs={{0,1},{1,3},{2,5},{3,7},{4,9},{5,11},{6,13},{7,15},{8,0},{9,2},{10... | collective-permute-start | bytes 491528 | tf_op jit(solution)/shard_map/ppermute | solution.py:237
  3.5 8.2 %all-to-all-start = ((bf16[16,40,128]{2,1,0:T(8,128)(2,1)}), bf16[16,40,128]{2,1,0:T(8,128)(2,1)S(1)}, u32[]{:S(2)}, u32[]{:S(2)}) async-start(bf16[16,40,128]{2,1,0:T(8,128)(2,1)} %get-tuple-element.15), calls=%async_computation | async-start | bytes 327680 | tf_op jit(solution)/shard_map/all_to_all | solution.py:251
  11.6 0.1 collective-permute-done.blocks_ref
  11.7 0.1 split_columns.1
  11.8 0.2 collective-permute-start.1
  12.0 1.2 %collective-permute-done.1.refs_1_ = bf16[64,512]{1,0:T(8,128)(2,1)S(1)} collective-permute-done((bf16[64,512]{1,0:T(8,128)(2,1)S(1)}, bf16[64,512]{1,0:T(8,128)(2,1)S(1)}, u32[]{:S(2)}, u32[]{:S(2)}) %collective-permute-start.1) | collective-permute-done | bytes 65568 | tf_op jit(solution)/shard_map/ppermute | solution.py:241
  13.2 0.0 copy-start
  13.2 3.2 %all-to-all-done.got_ref = bf16[16,40,128]{2,1,0:T(8,128)(2,1)S(1)} async-done(((bf16[16,40,128]{2,1,0:T(8,128)(2,1)}), bf16[16,40,128]{2,1,0:T(8,128)(2,1)S(1)}, u32[]{:S(2)}, u32[]{:S(2)}) %all-to-all-start) | async-done | bytes 163872 | tf_op jit(solution)/shard_map/all_to_all | solution.py:251
  16.3 0.3 %adapter_shares.1 = (f32[32,32]{1,0:T(8,128)S(1)}, f32[32,32]{1,0:T(8,128)S(1)}) custom-call(bf16[16,40,128]{2,1,0:T(8,128)(2,1)S(1)} %all-to-all-done.got_ref, bf16[2,64,512]{2,1,0:T(8,128)(2,1)S(1)} %order_pieces.1.pieces_ref), custom_call_target="tpu_custom_call" | custom-call | tf_op jit(solution)/shard_map/adapter_shares/pallas_call | solution.py:253
  16.6 1.3 %collective-permute-start.2 = (f32[32,32]{1,0:T(8,128)S(1)}, f32[32,32]{1,0:T(8,128)S(1)}, u32[]{:S(2)}, u32[]{:S(2)}) collective-permute-start(f32[32,32]{1,0:T(8,128)S(1)} %get-tuple-element.22), channel_id=1, source_target_pairs={{0,17},{1,16},{2,19},{3,18},{4,21},{5,20},{6,23},{7,22},{8,25},{9,... | collective-permute-start | bytes 12296 | tf_op jit(solution)/shard_map/ppermute | solution.py:267
  17.9 0.0 copy-done
  17.9 0.9 %owner_outputs.1 = (bf16[32,1024]{1,0:T(8,128)(2,1)}, bf16[32,1024]{1,0:T(8,128)(2,1)}, f32[32,32]{1,0:T(8,128)}) custom-call(bf16[16,40,128]{2,1,0:T(8,128)(2,1)S(1)} %all-to-all-done.got_ref, bf16[32,1024]{1,0:T(8,128)(2,1)S(1)} %copy-done), custom_call_target="tpu_custom_call" | custom-call | tf_op jit(solution)/shard_map/owner_outputs/pallas_call | solution.py:269
  18.8 1.1 %collective-permute-done.2 = f32[32,32]{1,0:T(8,128)S(1)} collective-permute-done((f32[32,32]{1,0:T(8,128)S(1)}, f32[32,32]{1,0:T(8,128)S(1)}, u32[]{:S(2)}, u32[]{:S(2)}) %collective-permute-start.2) | collective-permute-done | bytes 4128 | tf_op jit(solution)/shard_map/ppermute | solution.py:267
  19.8 0.6 %add.3 = f32[32,32]{1,0:T(8,128)} add(f32[32,32]{1,0:T(8,128)S(1)} %get-tuple-element.21, f32[32,32]{1,0:T(8,128)S(1)} %collective-permute-done.2) | non-fusion elementwise | flops 1024 | bytes 12288 | tf_op jit(solution)/shard_map/add | solution.py:267
  (1 shorter events, 0.0 us)
Async XLA Ops:
  3.0 8.7 %collective-permute-start = (bf16[16,40,128]{2,1,0:T(8,128)(2,1)}, bf16[16,40,128]{2,1,0:T(8,128)(2,1)S(1)}, u32[]{:S(2)}, u32[]{:S(2)}) collective-permute-start(bf16[16,40,128]{2,1,0:T(8,128)(2,1)} %get-tuple-element.15), channel_id=1, source_target_pairs={{0,1},{1,3},{2,5},{3,7},{4,9},{5,11},{6,13},{7,15},{8,0},{9,2},{10... | collective-permute-start | bytes 491528 | tf_op jit(solution)/shard_map/ppermute | solution.py:237
  3.5 12.9 %all-to-all-start = ((bf16[16,40,128]{2,1,0:T(8,128)(2,1)}), bf16[16,40,128]{2,1,0:T(8,128)(2,1)S(1)}, u32[]{:S(2)}, u32[]{:S(2)}) async-start(bf16[16,40,128]{2,1,0:T(8,128)(2,1)} %get-tuple-element.15), calls=%async_computation | async-start | bytes 327680 | tf_op jit(solution)/shard_map/all_to_all | solution.py:251
  11.8 1.3 %collective-permute-start.1 = (bf16[64,512]{1,0:T(8,128)(2,1)S(1)}, bf16[64,512]{1,0:T(8,128)(2,1)S(1)}, u32[]{:S(2)}, u32[]{:S(2)}) collective-permute-start(bf16[64,512]{1,0:T(8,128)(2,1)S(1)} %get-tuple-element.20), channel_id=1, source_target_pairs={{0,1},{1,0},{2,3},{3,2},{4,5},{5,4},{6,7},{7,6},{8,9},{9,8},{10,11... | collective-permute-start | bytes 196616 | tf_op jit(solution)/shard_map/ppermute | solution.py:241
  13.2 4.8 %copy-start = (bf16[32,1024]{1,0:T(8,128)(2,1)S(1)}, bf16[32,1024]{1,0:T(8,128)(2,1)}, u32[]{:S(2)}) copy-start(bf16[32,1024]{1,0:T(8,128)(2,1)} %up_ref.1) | copy-start | bytes 196612
  16.6 3.2 %collective-permute-start.2 = (f32[32,32]{1,0:T(8,128)S(1)}, f32[32,32]{1,0:T(8,128)S(1)}, u32[]{:S(2)}, u32[]{:S(2)}) collective-permute-start(f32[32,32]{1,0:T(8,128)S(1)} %get-tuple-element.22), channel_id=1, source_target_pairs={{0,17},{1,16},{2,19},{3,18},{4,21},{5,20},{6,23},{7,22},{8,25},{9,... | collective-permute-start | bytes 12296 | tf_op jit(solution)/shard_map/ppermute | solution.py:267

commit v16 on v15

--- a/solution.py
+++ b/solution.py
@@ -170,7 +170,22 @@
         chosen = shares[0]
         for e in range(1, dp):
             chosen = jnp.where(turn == e, shares[e], chosen)
+        if s > 0:
+            height = out_ref.shape[0]
+            chosen = [chosen[at:at + height] for at in range(0, step, height)]
+            chosen = jnp.concatenate(chosen, axis=1)
         out_ref[...] = chosen
+
+
+def add_kernel(own_ref, *refs):
+    *arrived_refs, out_ref = refs
+    both_rank = own_ref.shape[1]
+    total = own_ref[...]
+    for arrived_ref in arrived_refs:
+        arrived = arrived_ref[...]
+        parts = [arrived[:, at:at + both_rank] for at in range(0, LANES, both_rank)]
+        total += jnp.concatenate(parts, axis=0)
+    out_ref[...] = total
 
 
 def owner_kernel(got_ref, up_ref, key_ref, value_ref, low_grad_ref):
@@ -252,19 +267,28 @@
 
     shares = pl.pallas_call(
         functools.partial(share_kernel, rows, both_rank),
-        out_shape=[jax.ShapeDtypeStruct((step, both_rank), jnp.float32)] * dp,
+        out_shape=[jax.ShapeDtypeStruct((step, both_rank), jnp.float32)]
+        + [jax.ShapeDtypeStruct((step * both_rank // LANES, LANES), jnp.float32)] * (dp - 1),
         in_specs=[vmem] * 2,
         out_specs=[vmem] * dp,
         compiler_params=params,
         name="adapter_shares",
     )(got, ordered)
-    up_grad = shares[0]
+    crossed = []
     for s in range(1, dp):
         route = [
             (d * mp + m, (d + s) % dp * mp + m - m % dp + (m + s) % dp)
             for d in range(dp) for m in range(mp)
         ]
-        up_grad = up_grad + lax.ppermute(shares[s], ("dp", "mp"), route)
+        crossed.append(lax.ppermute(shares[s], ("dp", "mp"), route))
+    up_grad = pl.pallas_call(
+        add_kernel,
+        out_shape=jax.ShapeDtypeStruct((step, both_rank), jnp.float32),
+        in_specs=[vmem] * dp,
+        out_specs=vmem,
+        compiler_params=params,
+        name="add_shares",
+    )(shares[0], *crossed)
 
     key_gradient, value_grad, low_grad = pl.pallas_call(
         owner_kernel,

time: 20.7 us -> 20.7 us (level)
  Pallas kernels: 3.54 us -> 4.28 us
  other arithmetic: 0.61 us -> 0 us
    pallas_call x0 -> x1, Pallas kernels: none -> 0.68 us  [local(): pl.pallas_call(add_kernel, out_shape=jax.ShapeDtypeStruct((step, both_ran...]
    add x1 -> x0, other arithmetic: 0.61 us -> none  [local(): up_grad = up_grad + lax.ppermute(shares[s], ('dp', 'mp'), route)]
where the time goes in v16:
time: 20.7 us; the launch traced here: 20.4 us
  starting transfers between devices  10.1 us (49%)
  waiting for transfers between devices  5.35 us (26%)
  Pallas kernels  4.28 us (21%)
  between operations  0.67 us (3%)
    all_to_all x1, starting transfers between devices, local(): lax.all_to_all(sent, 'mp', 0, 0, axis_index_groups=[group_order(mp)], til...  8.16 us
    all_to_all x1, waiting for transfers between devices, local(): lax.all_to_all(sent, 'mp', 0, 0, axis_index_groups=[group_order(mp)], til...  3.19 us
    pallas_call x1, Pallas kernels, local(): pl.pallas_call(attention_kernel, out_shape=[jax.ShapeDtypeStruct((HS, tgt...  2.31 us
    ppermute x1, starting transfers between devices, local(): crossed.append(lax.ppermute(shares[s], ('dp', 'mp'), route))  1.26 us
    ppermute x1, waiting for transfers between devices, local(): arrived.append(lax.ppermute(pieces[s], 'mp', route))  1.16 us
    ppermute x1, waiting for transfers between devices, local(): crossed.append(lax.ppermute(shares[s], ('dp', 'mp'), route))  0.94 us
    pallas_call x1, Pallas kernels, local(): pl.pallas_call(owner_kernel, out_shape=[jax.ShapeDtypeStruct((rows, width...  0.86 us
    pallas_call x1, Pallas kernels, local(): pl.pallas_call(add_kernel, out_shape=jax.ShapeDtypeStruct((step, both_ran...  0.68 us
  transfers between devices with their start and end apart: 4, of which 4 were waited for; matrix products, arithmetic and copies ran while one was open for 0% of the time, Pallas kernels for 5%

profile of v16, /device:TPU:0, one launch (start us, length us, event | category | flops | bytes accessed | tf_op | source)
XLA Modules:
  0.0 20.4 jit_solution(2632217217134975656)
XLA Ops:
  0.6 2.3 %attention_backward.1 = (bf16[64,256]{1,0:T(8,128)(2,1)}, bf16[16,40,128]{2,1,0:T(8,128)(2,1)}) custom-call(s32[1,8]{1,0:T(1,128)} %source_any.1, s32[1,8]{1,0:T(1,128)} %target_any.1, bf16[64,256]{1,0:T(8,128)(2,1)} %bitcast.3, bf16[64,256]{1,0:T(8,128)(2,1)} %bitcast.4, bf16[512,128]{1,0:T(8,128)(2,1)} %kv_any.1, bf16[32,32]{1,0:T(8,128)(2,1)} %low_any.1), custom_call_target="tpu_custom_call" | custom-call | tf_op jit(solution)/shard_map/attention_backward/pallas_call | solution.py:222
  3.0 0.5 %collective-permute-start = (bf16[16,40,128]{2,1,0:T(8,128)(2,1)}, bf16[16,40,128]{2,1,0:T(8,128)(2,1)S(1)}, u32[]{:S(2)}, u32[]{:S(2)}) collective-permute-start(bf16[16,40,128]{2,1,0:T(8,128)(2,1)} %get-tuple-element.15), channel_id=1, source_target_pairs={{0,1},{1,3},{2,5},{3,7},{4,9},{5,11},{6,13},{7,15},{8,0},{9,2},{10... | collective-permute-start | bytes 491528 | tf_op jit(solution)/shard_map/ppermute | solution.py:252
  3.5 8.2 %all-to-all-start = ((bf16[16,40,128]{2,1,0:T(8,128)(2,1)}), bf16[16,40,128]{2,1,0:T(8,128)(2,1)S(1)}, u32[]{:S(2)}, u32[]{:S(2)}) async-start(bf16[16,40,128]{2,1,0:T(8,128)(2,1)} %get-tuple-element.15), calls=%async_computation | async-start | bytes 327680 | tf_op jit(solution)/shard_map/all_to_all | solution.py:266
  11.6 0.1 collective-permute-done.blocks_ref
  11.7 0.1 split_columns.1
  11.8 0.2 collective-permute-start.1
  12.0 1.2 %collective-permute-done.1.refs_1_ = bf16[64,512]{1,0:T(8,128)(2,1)S(1)} collective-permute-done((bf16[64,512]{1,0:T(8,128)(2,1)S(1)}, bf16[64,512]{1,0:T(8,128)(2,1)S(1)}, u32[]{:S(2)}, u32[]{:S(2)}) %collective-permute-start.1) | collective-permute-done | bytes 65568 | tf_op jit(solution)/shard_map/ppermute | solution.py:256
  13.2 0.0 copy-start
  13.2 3.2 %all-to-all-done.got_ref = bf16[16,40,128]{2,1,0:T(8,128)(2,1)S(1)} async-done(((bf16[16,40,128]{2,1,0:T(8,128)(2,1)}), bf16[16,40,128]{2,1,0:T(8,128)(2,1)S(1)}, u32[]{:S(2)}, u32[]{:S(2)}) %all-to-all-start) | async-done | bytes 163872 | tf_op jit(solution)/shard_map/all_to_all | solution.py:266
  16.3 0.3 %adapter_shares.1 = (f32[32,32]{1,0:T(8,128)S(1)}, f32[8,128]{1,0:T(8,128)S(1)}) custom-call(bf16[16,40,128]{2,1,0:T(8,128)(2,1)S(1)} %all-to-all-done.got_ref, bf16[2,64,512]{2,1,0:T(8,128)(2,1)S(1)} %order_pieces.1.pieces_ref), custom_call_target="tpu_custom_call" | custom-call | tf_op jit(solution)/shard_map/adapter_shares/pallas_call | solution.py:268
  16.7 1.3 %collective-permute-start.2 = (f32[8,128]{1,0:T(8,128)S(1)}, f32[8,128]{1,0:T(8,128)S(1)}, u32[]{:S(2)}, u32[]{:S(2)}) collective-permute-start(f32[8,128]{1,0:T(8,128)S(1)} %get-tuple-element.22), channel_id=1, source_target_pairs={{0,17},{1,16},{2,19},{3,18},{4,21},{5,20},{6,23},{7,22},{8,25},{9,... | collective-permute-start | bytes 12296 | tf_op jit(solution)/shard_map/ppermute | solution.py:283
  17.9 0.0 copy-done
  17.9 0.9 %owner_outputs.1 = (bf16[32,1024]{1,0:T(8,128)(2,1)}, bf16[32,1024]{1,0:T(8,128)(2,1)}, f32[32,32]{1,0:T(8,128)}) custom-call(bf16[16,40,128]{2,1,0:T(8,128)(2,1)S(1)} %all-to-all-done.got_ref, bf16[32,1024]{1,0:T(8,128)(2,1)S(1)} %copy-done), custom_call_target="tpu_custom_call" | custom-call | tf_op jit(solution)/shard_map/owner_outputs/pallas_call | solution.py:293
  18.8 0.9 %collective-permute-done.2.refs_0_ = f32[8,128]{1,0:T(8,128)S(1)} collective-permute-done((f32[8,128]{1,0:T(8,128)S(1)}, f32[8,128]{1,0:T(8,128)S(1)}, u32[]{:S(2)}, u32[]{:S(2)}) %collective-permute-start.2) | collective-permute-done | bytes 4128 | tf_op jit(solution)/shard_map/ppermute | solution.py:283
  19.7 0.7 %add_shares.1 = f32[32,32]{1,0:T(8,128)} custom-call(f32[32,32]{1,0:T(8,128)S(1)} %get-tuple-element.21.own_ref, f32[8,128]{1,0:T(8,128)S(1)} %collective-permute-done.2.refs_0_), custom_call_target="tpu_custom_call" | custom-call | tf_op jit(solution)/shard_map/add_shares/pallas_call | solution.py:284
  (1 shorter events, 0.0 us)
Async XLA Ops:
  3.0 8.7 %collective-permute-start = (bf16[16,40,128]{2,1,0:T(8,128)(2,1)}, bf16[16,40,128]{2,1,0:T(8,128)(2,1)S(1)}, u32[]{:S(2)}, u32[]{:S(2)}) collective-permute-start(bf16[16,40,128]{2,1,0:T(8,128)(2,1)} %get-tuple-element.15), channel_id=1, source_target_pairs={{0,1},{1,3},{2,5},{3,7},{4,9},{5,11},{6,13},{7,15},{8,0},{9,2},{10... | collective-permute-start | bytes 491528 | tf_op jit(solution)/shard_map/ppermute | solution.py:252
  3.5 12.9 %all-to-all-start = ((bf16[16,40,128]{2,1,0:T(8,128)(2,1)}), bf16[16,40,128]{2,1,0:T(8,128)(2,1)S(1)}, u32[]{:S(2)}, u32[]{:S(2)}) async-start(bf16[16,40,128]{2,1,0:T(8,128)(2,1)} %get-tuple-element.15), calls=%async_computation | async-start | bytes 327680 | tf_op jit(solution)/shard_map/all_to_all | solution.py:266
  11.8 1.3 %collective-permute-start.1 = (bf16[64,512]{1,0:T(8,128)(2,1)S(1)}, bf16[64,512]{1,0:T(8,128)(2,1)S(1)}, u32[]{:S(2)}, u32[]{:S(2)}) collective-permute-start(bf16[64,512]{1,0:T(8,128)(2,1)S(1)} %get-tuple-element.20), channel_id=1, source_target_pairs={{0,1},{1,0},{2,3},{3,2},{4,5},{5,4},{6,7},{7,6},{8,9},{9,8},{10,11... | collective-permute-start | bytes 196616 | tf_op jit(solution)/shard_map/ppermute | solution.py:256
  13.2 4.8 %copy-start = (bf16[32,1024]{1,0:T(8,128)(2,1)S(1)}, bf16[32,1024]{1,0:T(8,128)(2,1)}, u32[]{:S(2)}) copy-start(bf16[32,1024]{1,0:T(8,128)(2,1)} %up_ref.1) | copy-start | bytes 196612
  16.7 3.1 %collective-permute-start.2 = (f32[8,128]{1,0:T(8,128)S(1)}, f32[8,128]{1,0:T(8,128)S(1)}, u32[]{:S(2)}, u32[]{:S(2)}) collective-permute-start(f32[8,128]{1,0:T(8,128)S(1)} %get-tuple-element.22), channel_id=1, source_target_pairs={{0,17},{1,16},{2,19},{3,18},{4,21},{5,20},{6,23},{7,22},{8,25},{9,... | collective-permute-start | bytes 12296 | tf_op jit(solution)/shard_map/ppermute | solution.py:283

commit v17 on v15

--- a/solution.py
+++ b/solution.py
@@ -28,7 +28,7 @@
     turned = [sum(((i >> b) & 1) << (bits - 1 - b) for b in range(bits)) for i in range(quarter)]
     order = []
     for i, place in enumerate(reversed(turned)):
-        order += [2 * quarter + place, 2 * i, 3 * quarter + place, 2 * i + 1]
+        order += [2 * quarter + place, 2 * i, 2 * i + 1, 3 * quarter + place]
     return order
 
 

time: 20.7 us -> 21.4 us (1.034)
  waiting for transfers between devices: 5.49 us -> 6.98 us
  starting transfers between devices: 10.1 us -> 9.29 us
    ppermute x1, waiting for transfers between devices: 1.07 us -> 2.01 us  [local(): up_grad = up_grad + lax.ppermute(shares[s], ('dp', 'mp'), route)]
    ppermute x1, starting transfers between devices: 1.3 us -> 0.46 us  [local(): up_grad = up_grad + lax.ppermute(shares[s], ('dp', 'mp'), route)]
    all_to_all x1, waiting for transfers between devices: 3.19 us -> 3.74 us  [local(): lax.all_to_all(sent, 'mp', 0, 0, axis_index_groups=[group_order(mp)], til...]
where the time goes in v17:
time: 21.4 us; the launch traced here: 21.1 us
  starting transfers between devices  9.29 us (43%)
  waiting for transfers between devices  6.98 us (33%)
  Pallas kernels  3.55 us (17%)
  between operations  0.67 us (3%)
  other arithmetic  0.61 us (3%)
    all_to_all x1, starting transfers between devices, local(): lax.all_to_all(sent, 'mp', 0, 0, axis_index_groups=[group_order(mp)], til...  8.16 us
    all_to_all x1, waiting for transfers between devices, local(): lax.all_to_all(sent, 'mp', 0, 0, axis_index_groups=[group_order(mp)], til...  3.74 us
    pallas_call x1, Pallas kernels, local(): pl.pallas_call(attention_kernel, out_shape=[jax.ShapeDtypeStruct((HS, tgt...  2.31 us
    ppermute x1, waiting for transfers between devices, local(): up_grad = up_grad + lax.ppermute(shares[s], ('dp', 'mp'), route)  2.01 us
    ppermute x1, waiting for transfers between devices, local(): arrived.append(lax.ppermute(pieces[s], 'mp', route))  1.16 us
    pallas_call x1, Pallas kernels, local(): pl.pallas_call(owner_kernel, out_shape=[jax.ShapeDtypeStruct((rows, width...  0.86 us
    add x1, other arithmetic, local(): up_grad = up_grad + lax.ppermute(shares[s], ('dp', 'mp'), route)  0.61 us
    ppermute x1, starting transfers between devices, local(): lax.ppermute(sent, 'mp', route)  0.52 us
  transfers between devices with their start and end apart: 4, of which 4 were waited for; matrix products, arithmetic and copies ran while one was open for 0% of the time, Pallas kernels for 5%

profile of v17, /device:TPU:0, one launch (start us, length us, event | category | flops | bytes accessed | tf_op | source)
XLA Modules:
  0.0 21.1 jit_solution(8722257947253910511)
XLA Ops:
  0.6 2.3 %attention_backward.1 = (bf16[64,256]{1,0:T(8,128)(2,1)}, bf16[16,40,128]{2,1,0:T(8,128)(2,1)}) custom-call(s32[1,8]{1,0:T(1,128)} %source_any.1, s32[1,8]{1,0:T(1,128)} %target_any.1, bf16[64,256]{1,0:T(8,128)(2,1)} %bitcast.3, bf16[64,256]{1,0:T(8,128)(2,1)} %bitcast.4, bf16[512,128]{1,0:T(8,128)(2,1)} %kv_any.1, bf16[32,32]{1,0:T(8,128)(2,1)} %low_any.1), custom_call_target="tpu_custom_call" | custom-call | tf_op jit(solution)/shard_map/attention_backward/pallas_call | solution.py:207
  3.0 0.5 %collective-permute-start = (bf16[16,40,128]{2,1,0:T(8,128)(2,1)}, bf16[16,40,128]{2,1,0:T(8,128)(2,1)S(1)}, u32[]{:S(2)}, u32[]{:S(2)}) collective-permute-start(bf16[16,40,128]{2,1,0:T(8,128)(2,1)} %get-tuple-element.15), channel_id=1, source_target_pairs={{0,1},{1,3},{2,5},{3,7},{4,9},{5,11},{6,13},{7,15},{8,0},{9,2},{10... | collective-permute-start | bytes 491528 | tf_op jit(solution)/shard_map/ppermute | solution.py:237
  3.5 8.2 %all-to-all-start = ((bf16[16,40,128]{2,1,0:T(8,128)(2,1)}), bf16[16,40,128]{2,1,0:T(8,128)(2,1)S(1)}, u32[]{:S(2)}, u32[]{:S(2)}) async-start(bf16[16,40,128]{2,1,0:T(8,128)(2,1)} %get-tuple-element.15), calls=%async_computation | async-start | bytes 327680 | tf_op jit(solution)/shard_map/all_to_all | solution.py:251
  11.6 0.1 collective-permute-done.blocks_ref
  11.7 0.1 split_columns.1
  11.8 0.2 collective-permute-start.1
  12.0 1.2 %collective-permute-done.1.refs_1_ = bf16[64,512]{1,0:T(8,128)(2,1)S(1)} collective-permute-done((bf16[64,512]{1,0:T(8,128)(2,1)S(1)}, bf16[64,512]{1,0:T(8,128)(2,1)S(1)}, u32[]{:S(2)}, u32[]{:S(2)}) %collective-permute-start.1) | collective-permute-done | bytes 65568 | tf_op jit(solution)/shard_map/ppermute | solution.py:241
  13.2 0.0 copy-start
  13.2 3.7 %all-to-all-done.got_ref = bf16[16,40,128]{2,1,0:T(8,128)(2,1)S(1)} async-done(((bf16[16,40,128]{2,1,0:T(8,128)(2,1)}), bf16[16,40,128]{2,1,0:T(8,128)(2,1)S(1)}, u32[]{:S(2)}, u32[]{:S(2)}) %all-to-all-start) | async-done | bytes 163872 | tf_op jit(solution)/shard_map/all_to_all | solution.py:251
  16.9 0.3 %adapter_shares.1 = (f32[32,32]{1,0:T(8,128)S(1)}, f32[32,32]{1,0:T(8,128)S(1)}) custom-call(bf16[16,40,128]{2,1,0:T(8,128)(2,1)S(1)} %all-to-all-done.got_ref, bf16[2,64,512]{2,1,0:T(8,128)(2,1)S(1)} %order_pieces.1.pieces_ref), custom_call_target="tpu_custom_call" | custom-call | tf_op jit(solution)/shard_map/adapter_shares/pallas_call | solution.py:253
  17.2 0.5 %collective-permute-start.2 = (f32[32,32]{1,0:T(8,128)S(1)}, f32[32,32]{1,0:T(8,128)S(1)}, u32[]{:S(2)}, u32[]{:S(2)}) collective-permute-start(f32[32,32]{1,0:T(8,128)S(1)} %get-tuple-element.22), channel_id=1, source_target_pairs={{0,17},{1,16},{2,19},{3,18},{4,21},{5,20},{6,23},{7,22},{8,25},{9,... | collective-permute-start | bytes 12296 | tf_op jit(solution)/shard_map/ppermute | solution.py:267
  17.6 0.0 copy-done
  17.6 0.9 %owner_outputs.1 = (bf16[32,1024]{1,0:T(8,128)(2,1)}, bf16[32,1024]{1,0:T(8,128)(2,1)}, f32[32,32]{1,0:T(8,128)}) custom-call(bf16[16,40,128]{2,1,0:T(8,128)(2,1)S(1)} %all-to-all-done.got_ref, bf16[32,1024]{1,0:T(8,128)(2,1)S(1)} %copy-done), custom_call_target="tpu_custom_call" | custom-call | tf_op jit(solution)/shard_map/owner_outputs/pallas_call | solution.py:269
  18.5 2.0 %collective-permute-done.2 = f32[32,32]{1,0:T(8,128)S(1)} collective-permute-done((f32[32,32]{1,0:T(8,128)S(1)}, f32[32,32]{1,0:T(8,128)S(1)}, u32[]{:S(2)}, u32[]{:S(2)}) %collective-permute-start.2) | collective-permute-done | bytes 4128 | tf_op jit(solution)/shard_map/ppermute | solution.py:267
  20.5 0.6 %add.3 = f32[32,32]{1,0:T(8,128)} add(f32[32,32]{1,0:T(8,128)S(1)} %get-tuple-element.21, f32[32,32]{1,0:T(8,128)S(1)} %collective-permute-done.2) | non-fusion elementwise | flops 1024 | bytes 12288 | tf_op jit(solution)/shard_map/add | solution.py:267
  (1 shorter events, 0.0 us)
Async XLA Ops:
  3.0 8.7 %collective-permute-start = (bf16[16,40,128]{2,1,0:T(8,128)(2,1)}, bf16[16,40,128]{2,1,0:T(8,128)(2,1)S(1)}, u32[]{:S(2)}, u32[]{:S(2)}) collective-permute-start(bf16[16,40,128]{2,1,0:T(8,128)(2,1)} %get-tuple-element.15), channel_id=1, source_target_pairs={{0,1},{1,3},{2,5},{3,7},{4,9},{5,11},{6,13},{7,15},{8,0},{9,2},{10... | collective-permute-start | bytes 491528 | tf_op jit(solution)/shard_map/ppermute | solution.py:237
  3.5 13.4 %all-to-all-start = ((bf16[16,40,128]{2,1,0:T(8,128)(2,1)}), bf16[16,40,128]{2,1,0:T(8,128)(2,1)S(1)}, u32[]{:S(2)}, u32[]{:S(2)}) async-start(bf16[16,40,128]{2,1,0:T(8,128)(2,1)} %get-tuple-element.15), calls=%async_computation | async-start | bytes 327680 | tf_op jit(solution)/shard_map/all_to_all | solution.py:251
  11.8 1.3 %collective-permute-start.1 = (bf16[64,512]{1,0:T(8,128)(2,1)S(1)}, bf16[64,512]{1,0:T(8,128)(2,1)S(1)}, u32[]{:S(2)}, u32[]{:S(2)}) collective-permute-start(bf16[64,512]{1,0:T(8,128)(2,1)S(1)} %get-tuple-element.20), channel_id=1, source_target_pairs={{0,1},{1,0},{2,3},{3,2},{4,5},{5,4},{6,7},{7,6},{8,9},{9,8},{10,11... | collective-permute-start | bytes 196616 | tf_op jit(solution)/shard_map/ppermute | solution.py:241
  13.2 4.5 %copy-start = (bf16[32,1024]{1,0:T(8,128)(2,1)S(1)}, bf16[32,1024]{1,0:T(8,128)(2,1)}, u32[]{:S(2)}) copy-start(bf16[32,1024]{1,0:T(8,128)(2,1)} %up_ref.1) | copy-start | bytes 196612
  17.2 3.3 %collective-permute-start.2 = (f32[32,32]{1,0:T(8,128)S(1)}, f32[32,32]{1,0:T(8,128)S(1)}, u32[]{:S(2)}, u32[]{:S(2)}) collective-permute-start(f32[32,32]{1,0:T(8,128)S(1)} %get-tuple-element.22), channel_id=1, source_target_pairs={{0,17},{1,16},{2,19},{3,18},{4,21},{5,20},{6,23},{7,22},{8,25},{9,... | collective-permute-start | bytes 12296 | tf_op jit(solution)/shard_map/ppermute | solution.py:267

commit v18 on v17

--- a/solution.py
+++ b/solution.py
@@ -28,7 +28,8 @@
     turned = [sum(((i >> b) & 1) << (bits - 1 - b) for b in range(bits)) for i in range(quarter)]
     order = []
     for i, place in enumerate(reversed(turned)):
-        order += [2 * quarter + place, 2 * i, 2 * i + 1, 3 * quarter + place]
+        lower = 4 * (i // 2) + i % 2
+        order += [2 * quarter + place, lower, 3 * quarter + place, lower + 2]
     return order
 
 

time: 21.4 us -> 20.7 us (0.967)
  waiting for transfers between devices: 6.98 us -> 5.49 us
  starting transfers between devices: 9.29 us -> 10.1 us
    ppermute x1, waiting for transfers between devices: 2.01 us -> 1.07 us  [local(): up_grad = up_grad + lax.ppermute(shares[s], ('dp', 'mp'), route)]
    ppermute x1, starting transfers between devices: 0.46 us -> 1.3 us  [local(): up_grad = up_grad + lax.ppermute(shares[s], ('dp', 'mp'), route)]
    all_to_all x1, waiting for transfers between devices: 3.74 us -> 3.19 us  [local(): lax.all_to_all(sent, 'mp', 0, 0, axis_index_groups=[group_order(mp)], til...]
where the time goes in v18:
time: 20.7 us; the launch traced here: 20.5 us
  starting transfers between devices  10.1 us (49%)
  waiting for transfers between devices  5.49 us (27%)
  Pallas kernels  3.54 us (17%)
  between operations  0.67 us (3%)
  other arithmetic  0.61 us (3%)
    all_to_all x1, starting transfers between devices, local(): lax.all_to_all(sent, 'mp', 0, 0, axis_index_groups=[group_order(mp)], til...  8.16 us
    all_to_all x1, waiting for transfers between devices, local(): lax.all_to_all(sent, 'mp', 0, 0, axis_index_groups=[group_order(mp)], til...  3.19 us
    pallas_call x1, Pallas kernels, local(): pl.pallas_call(attention_kernel, out_shape=[jax.ShapeDtypeStruct((HS, tgt...  2.31 us
    ppermute x1, starting transfers between devices, local(): up_grad = up_grad + lax.ppermute(shares[s], ('dp', 'mp'), route)  1.3 us
    ppermute x1, waiting for transfers between devices, local(): arrived.append(lax.ppermute(pieces[s], 'mp', route))  1.16 us
    ppermute x1, waiting for transfers between devices, local(): up_grad = up_grad + lax.ppermute(shares[s], ('dp', 'mp'), route)  1.07 us
    pallas_call x1, Pallas kernels, local(): pl.pallas_call(owner_kernel, out_shape=[jax.ShapeDtypeStruct((rows, width...  0.85 us
    add x1, other arithmetic, local(): up_grad = up_grad + lax.ppermute(shares[s], ('dp', 'mp'), route)  0.61 us
  transfers between devices with their start and end apart: 4, of which 4 were waited for; matrix products, arithmetic and copies ran while one was open for 0% of the time, Pallas kernels for 5%

profile of v18, /device:TPU:0, one launch (start us, length us, event | category | flops | bytes accessed | tf_op | source)
XLA Modules:
  0.0 20.5 jit_solution(3715613959454430493)
XLA Ops:
  0.6 2.3 %attention_backward.1 = (bf16[64,256]{1,0:T(8,128)(2,1)}, bf16[16,40,128]{2,1,0:T(8,128)(2,1)}) custom-call(s32[1,8]{1,0:T(1,128)} %source_any.1, s32[1,8]{1,0:T(1,128)} %target_any.1, bf16[64,256]{1,0:T(8,128)(2,1)} %bitcast.3, bf16[64,256]{1,0:T(8,128)(2,1)} %bitcast.4, bf16[512,128]{1,0:T(8,128)(2,1)} %kv_any.1, bf16[32,32]{1,0:T(8,128)(2,1)} %low_any.1), custom_call_target="tpu_custom_call" | custom-call | tf_op jit(solution)/shard_map/attention_backward/pallas_call | solution.py:208
  3.0 0.5 %collective-permute-start = (bf16[16,40,128]{2,1,0:T(8,128)(2,1)}, bf16[16,40,128]{2,1,0:T(8,128)(2,1)S(1)}, u32[]{:S(2)}, u32[]{:S(2)}) collective-permute-start(bf16[16,40,128]{2,1,0:T(8,128)(2,1)} %get-tuple-element.15), channel_id=1, source_target_pairs={{0,1},{1,3},{2,5},{3,7},{4,9},{5,11},{6,13},{7,15},{8,0},{9,2},{10... | collective-permute-start | bytes 491528 | tf_op jit(solution)/shard_map/ppermute | solution.py:238
  3.5 8.2 %all-to-all-start = ((bf16[16,40,128]{2,1,0:T(8,128)(2,1)}), bf16[16,40,128]{2,1,0:T(8,128)(2,1)S(1)}, u32[]{:S(2)}, u32[]{:S(2)}) async-start(bf16[16,40,128]{2,1,0:T(8,128)(2,1)} %get-tuple-element.15), calls=%async_computation | async-start | bytes 327680 | tf_op jit(solution)/shard_map/all_to_all | solution.py:252
  11.6 0.1 collective-permute-done.blocks_ref
  11.7 0.1 split_columns.1
  11.8 0.2 collective-permute-start.1
  12.0 1.2 %collective-permute-done.1.refs_1_ = bf16[64,512]{1,0:T(8,128)(2,1)S(1)} collective-permute-done((bf16[64,512]{1,0:T(8,128)(2,1)S(1)}, bf16[64,512]{1,0:T(8,128)(2,1)S(1)}, u32[]{:S(2)}, u32[]{:S(2)}) %collective-permute-start.1) | collective-permute-done | bytes 65568 | tf_op jit(solution)/shard_map/ppermute | solution.py:242
  13.2 0.0 copy-start
  13.2 3.2 %all-to-all-done.got_ref = bf16[16,40,128]{2,1,0:T(8,128)(2,1)S(1)} async-done(((bf16[16,40,128]{2,1,0:T(8,128)(2,1)}), bf16[16,40,128]{2,1,0:T(8,128)(2,1)S(1)}, u32[]{:S(2)}, u32[]{:S(2)}) %all-to-all-start) | async-done | bytes 163872 | tf_op jit(solution)/shard_map/all_to_all | solution.py:252
  16.3 0.3 %adapter_shares.1 = (f32[32,32]{1,0:T(8,128)S(1)}, f32[32,32]{1,0:T(8,128)S(1)}) custom-call(bf16[16,40,128]{2,1,0:T(8,128)(2,1)S(1)} %all-to-all-done.got_ref, bf16[2,64,512]{2,1,0:T(8,128)(2,1)S(1)} %order_pieces.1.pieces_ref), custom_call_target="tpu_custom_call" | custom-call | tf_op jit(solution)/shard_map/adapter_shares/pallas_call | solution.py:254
  16.6 1.3 %collective-permute-start.2 = (f32[32,32]{1,0:T(8,128)S(1)}, f32[32,32]{1,0:T(8,128)S(1)}, u32[]{:S(2)}, u32[]{:S(2)}) collective-permute-start(f32[32,32]{1,0:T(8,128)S(1)} %get-tuple-element.22), channel_id=1, source_target_pairs={{0,17},{1,16},{2,19},{3,18},{4,21},{5,20},{6,23},{7,22},{8,25},{9,... | collective-permute-start | bytes 12296 | tf_op jit(solution)/shard_map/ppermute | solution.py:268
  17.9 0.0 copy-done
  17.9 0.9 %owner_outputs.1 = (bf16[32,1024]{1,0:T(8,128)(2,1)}, bf16[32,1024]{1,0:T(8,128)(2,1)}, f32[32,32]{1,0:T(8,128)}) custom-call(bf16[16,40,128]{2,1,0:T(8,128)(2,1)S(1)} %all-to-all-done.got_ref, bf16[32,1024]{1,0:T(8,128)(2,1)S(1)} %copy-done), custom_call_target="tpu_custom_call" | custom-call | tf_op jit(solution)/shard_map/owner_outputs/pallas_call | solution.py:270
  18.8 1.1 %collective-permute-done.2 = f32[32,32]{1,0:T(8,128)S(1)} collective-permute-done((f32[32,32]{1,0:T(8,128)S(1)}, f32[32,32]{1,0:T(8,128)S(1)}, u32[]{:S(2)}, u32[]{:S(2)}) %collective-permute-start.2) | collective-permute-done | bytes 4128 | tf_op jit(solution)/shard_map/ppermute | solution.py:268
  19.8 0.6 %add.3 = f32[32,32]{1,0:T(8,128)} add(f32[32,32]{1,0:T(8,128)S(1)} %get-tuple-element.21, f32[32,32]{1,0:T(8,128)S(1)} %collective-permute-done.2) | non-fusion elementwise | flops 1024 | bytes 12288 | tf_op jit(solution)/shard_map/add | solution.py:268
  (1 shorter events, 0.0 us)
Async XLA Ops:
  3.0 8.7 %collective-permute-start = (bf16[16,40,128]{2,1,0:T(8,128)(2,1)}, bf16[16,40,128]{2,1,0:T(8,128)(2,1)S(1)}, u32[]{:S(2)}, u32[]{:S(2)}) collective-permute-start(bf16[16,40,128]{2,1,0:T(8,128)(2,1)} %get-tuple-element.15), channel_id=1, source_target_pairs={{0,1},{1,3},{2,5},{3,7},{4,9},{5,11},{6,13},{7,15},{8,0},{9,2},{10... | collective-permute-start | bytes 491528 | tf_op jit(solution)/shard_map/ppermute | solution.py:238
  3.5 12.9 %all-to-all-start = ((bf16[16,40,128]{2,1,0:T(8,128)(2,1)}), bf16[16,40,128]{2,1,0:T(8,128)(2,1)S(1)}, u32[]{:S(2)}, u32[]{:S(2)}) async-start(bf16[16,40,128]{2,1,0:T(8,128)(2,1)} %get-tuple-element.15), calls=%async_computation | async-start | bytes 327680 | tf_op jit(solution)/shard_map/all_to_all | solution.py:252
  11.8 1.3 %collective-permute-start.1 = (bf16[64,512]{1,0:T(8,128)(2,1)S(1)}, bf16[64,512]{1,0:T(8,128)(2,1)S(1)}, u32[]{:S(2)}, u32[]{:S(2)}) collective-permute-start(bf16[64,512]{1,0:T(8,128)(2,1)S(1)} %get-tuple-element.20), channel_id=1, source_target_pairs={{0,1},{1,0},{2,3},{3,2},{4,5},{5,4},{6,7},{7,6},{8,9},{9,8},{10,11... | collective-permute-start | bytes 196616 | tf_op jit(solution)/shard_map/ppermute | solution.py:242
  13.2 4.8 %copy-start = (bf16[32,1024]{1,0:T(8,128)(2,1)S(1)}, bf16[32,1024]{1,0:T(8,128)(2,1)}, u32[]{:S(2)}) copy-start(bf16[32,1024]{1,0:T(8,128)(2,1)} %up_ref.1) | copy-start | bytes 196612
  16.6 3.2 %collective-permute-start.2 = (f32[32,32]{1,0:T(8,128)S(1)}, f32[32,32]{1,0:T(8,128)S(1)}, u32[]{:S(2)}, u32[]{:S(2)}) collective-permute-start(f32[32,32]{1,0:T(8,128)S(1)} %get-tuple-element.22), channel_id=1, source_target_pairs={{0,17},{1,16},{2,19},{3,18},{4,21},{5,20},{6,23},{7,22},{8,25},{9,... | collective-permute-start | bytes 12296 | tf_op jit(solution)/shard_map/ppermute | solution.py:268
